TPU v7x, 32 devices: a whole 2x2x4 slice. The times are simulated.
32 devices in a mesh: src: 8 (over z, x), tgt: 4 (over y, core).
Axes of the slice: x: 2, y: 2, z: 4, core: 2. Of those that a mesh axis runs over, the one named last changes fastest.
Arguments:
- initial: bfloat16 [4096, 256], P(('src', 'tgt')), may hold values from -6 to 6
- stubborn: int32 [4096], P(('src', 'tgt')), may hold values from 0 to 255
- coupling: bfloat16 [256, 256], replicated, may hold values from -0.375 to 0.375
- tile_values: bfloat16 [8, 4, 144, 128, 128], P('src', 'tgt'), may hold values from -0.078125 to 0.078125
- tile_target: int32 [8, 4, 144], P('src', 'tgt'), may hold values from 0 to 3
- tile_source: int32 [8, 4, 144], P('src', 'tgt'), may hold values from 0 to 7, as said below
- tile_count: int32 [8, 4], P('src', 'tgt'), may hold values from 1 to 144, as said below
Outputs:
- opinions: bfloat16 [4096, 256], P(('src', 'tgt'))
Inputs may be any that keep to these rules, and one draw needn't show every extreme that they name: Among the live slots k < tile_count of one block pair, tile_source does not fall as k rises; a source tile may hold several slots. `tile_count`: some block pair has all 144 slots live in every draw.
All inputs are finite; a program needn't handle non-finite values.
Results may differ from a plain program's by a relative error of at most 0.02.
Values may be sent and summed in bfloat16 or wider, within the bound.
No kernel may reach another device: no remote copies, remote signals or barrier semaphores. Data moves between devices by JAX's collectives and lax.ppermute only.
A program may use at most 64 MiB of HBM per device.

v0:
```python
import jax
import jax.numpy as jnp
from jax import lax
from jax.sharding import PartitionSpec as P

STEPS = 3


def add_group(running, first_id, end_slot, tile_block, targets, sources, local_tiles, offset):
    slot_count = tile_block.shape[0]
    slot_ids = first_id + jnp.arange(8, dtype=jnp.int32)
    active = slot_ids < end_slot
    clipped = jnp.minimum(slot_ids, slot_count - 1)
    group_tiles = jnp.take(tile_block, clipped, axis=0)
    source_local = jnp.clip(jnp.take(sources, clipped) - offset, 0, local_tiles.shape[0] - 1)
    chosen = jnp.take(local_tiles, source_local, axis=0)
    contrib = jnp.einsum("kab,kbc->kac", group_tiles, chosen, preferred_element_type=jnp.float32)
    contrib = jnp.where(active[:, None, None], contrib, 0.0)
    return running.at[jnp.take(targets, clipped)].add(contrib)


def run_slots(running, end_slot, tile_block, targets, sources, local_tiles, offset):
    groups = (end_slot + 7) // 8

    def one_group(group_index, inner):
        return add_group(
            inner, 8 * group_index, end_slot, tile_block, targets, sources, local_tiles, offset
        )

    return lax.fori_loop(0, groups, one_group, running)


def shards(initial, stubborn, coupling, tile_values, tile_target, tile_source, tile_count):
    own_rows, topics = initial.shape
    tile_edge = tile_values.shape[-1]
    tile_block = tile_values[0, 0]
    targets = tile_target[0, 0]
    sources = tile_source[0, 0]
    tile_total = tile_count[0, 0]
    tgt_devices = lax.axis_size("tgt")
    src_devices = lax.axis_size("src")
    per_block = own_rows // tile_edge
    openness = ((256.0 - stubborn.astype(jnp.float32)) / 256.0)[:, None]
    base_term = (1.0 - openness) * initial.astype(jnp.float32)
    opinion = initial
    for iteration in range(STEPS):
        zeroed = jnp.zeros((tgt_devices * per_block, tile_edge, topics), jnp.float32)
        gathered = lax.all_gather(opinion, "src", axis=0, tiled=True)
        tiles_all = gathered.reshape(src_devices * per_block, tile_edge, topics)
        partial_value = run_slots(zeroed, tile_total, tile_block, targets, sources, tiles_all, 0)
        summed = lax.psum_scatter(
            partial_value.reshape(tgt_devices * own_rows, topics).astype(jnp.bfloat16),
            "tgt",
            scatter_dimension=0,
            tiled=True,
        )
        coupled = jnp.dot(summed, coupling, preferred_element_type=jnp.float32)
        opinion = (openness * coupled + base_term).astype(jnp.bfloat16)
    return opinion


def solution(mesh):
    in_specs = (
        P(("src", "tgt"), None),
        P(("src", "tgt")),
        P(),
        P("src", "tgt", None, None, None),
        P("src", "tgt", None),
        P("src", "tgt", None),
        P("src", "tgt"),
    )
    out_specs = P(("src", "tgt"), None)
    return jax.shard_map(shards, mesh=mesh, in_specs=in_specs, out_specs=out_specs, check_vma=False)
```

profile of v0, /device:TPU:0, one launch (start us, length us, event | category | flops | bytes accessed | tf_op | source)
XLA Modules:
  0.0 633.0 jit_solution(5495321734355845577)
XLA Ops:
  7.2 33.2 %all_gather.9 = bf16[1024,256]{1,0:T(8,128)(2,1)S(1)} all-gather(bf16[128,256]{1,0:T(8,128)(2,1)} %param.19), channel_id=1, replica_groups=mesh['src'=8,'tgt'=4] {'src'}, dimensions={0}, use_global_device_ids=true | all-gather | bytes 589824 | tf_op jit(solution)/shard_map/all_gather | solution.py:48
  40.5 43.2 %while.30 = (s32[]{:T(128)}, f32[4,128,256]{2,1,0:T(8,128)S(1)}, s32[]{:T(128)}, s32[144]{0:T(256)}, s32[]{:T(128)}, /*index=5*/bf16[144,128,128]{2,1,0:T(8,128)...) while((s32[]{:T(128)}, f32[4,128,256]{2,1,0:T(8,128)S(1)}, s32[]{:T(128)}, ...), condition=%wide.region_2.0_spmd, body=%wide.region_0.5_spmd.sunk | while | flops 68028696 | bytes 6562485 | solution.py:30
  41.3 1.3 gather_fusion.1
  42.6 1.3 gather_fusion
  44.0 2.9 gather_fusion.3
  49.9 1.3 gather_fusion.1
  51.2 1.3 gather_fusion
  52.6 2.9 gather_fusion.3
  59.9 1.3 gather_fusion
  61.3 2.9 gather_fusion.3
  68.5 1.3 gather_fusion
  69.9 2.9 gather_fusion.3
  77.2 1.3 gather_fusion
  78.5 2.9 gather_fusion.3
  84.6 129.7 %reduce-scatter.4.cloned.1.call-done = bf16[128,256]{1,0:T(8,128)(2,1)} async-done(((bf16[512,256]{1,0:T(8,128)(2,1)}), bf16[128,256]{1,0:T(8,128)(2,1)}) %reduce-scatter.4.cloned.1.call-update) | async-done | bytes 65552 | tf_op jit(solution)/shard_map/reduce_scatter | solution.py:51
  215.3 31.4 %all_gather.10 = bf16[1024,256]{1,0:T(8,128)(2,1)S(1)} all-gather(bf16[128,256]{1,0:T(8,128)(2,1)S(1)} %fusion.29), channel_id=1, replica_groups=mesh['src'=8,'tgt'=4] {'src'}, dimensions={0}, use_global_device_ids=true | all-gather | bytes 589824 | tf_op jit(solution)/shard_map/all_gather | solution.py:48
  246.8 43.2 %while.31 = (s32[]{:T(128)}, f32[4,128,256]{2,1,0:T(8,128)S(1)}, s32[]{:T(128)}, s32[144]{0:T(256)}, s32[]{:T(128)}, /*index=5*/bf16[144,128,128]{2,1,0:T(8,128)...) while((s32[]{:T(128)}, f32[4,128,256]{2,1,0:T(8,128)S(1)}, s32[]{:T(128)}, ...), condition=%wide.region_6.10_spmd, body=%wide.region_4.9_spmd.sunk | while | flops 68028696 | bytes 6562485 | solution.py:30
  247.5 1.3 gather_fusion.5
  248.8 1.3 gather_fusion.4
  250.2 2.9 gather_fusion.7
  257.4 1.3 gather_fusion.4
  258.8 2.9 gather_fusion.7
  266.1 1.3 gather_fusion.4
  267.5 2.9 gather_fusion.7
  274.7 1.3 gather_fusion.4
  276.1 2.9 gather_fusion.7
  282.0 1.3 gather_fusion.5
  283.4 1.3 gather_fusion.4
  284.7 2.9 gather_fusion.7
  290.8 128.8 %reduce-scatter.6.cloned.1.call-done = bf16[128,256]{1,0:T(8,128)(2,1)} async-done(((bf16[512,256]{1,0:T(8,128)(2,1)}), bf16[128,256]{1,0:T(8,128)(2,1)}) %reduce-scatter.6.cloned.1.call-update) | async-done | bytes 65552 | tf_op jit(solution)/shard_map/reduce_scatter | solution.py:51
  420.6 31.4 %all_gather.11 = bf16[1024,256]{1,0:T(8,128)(2,1)S(1)} all-gather(bf16[128,256]{1,0:T(8,128)(2,1)S(1)} %fusion.28), channel_id=1, replica_groups=mesh['src'=8,'tgt'=4] {'src'}, dimensions={0}, use_global_device_ids=true | all-gather | bytes 589824 | tf_op jit(solution)/shard_map/all_gather | solution.py:48
  452.0 43.2 %while.32 = (s32[]{:T(128)}, f32[4,128,256]{2,1,0:T(8,128)S(1)}, s32[]{:T(128)}, s32[144]{0:T(256)}, s32[]{:T(128)}, /*index=5*/bf16[144,128,128]{2,1,0:T(8,128)...) while((s32[]{:T(128)}, f32[4,128,256]{2,1,0:T(8,128)S(1)}, s32[]{:T(128)}, ...), condition=%wide.region_10.14_spmd, body=%wide.region_8.13_spmd.sunk | while | flops 68028696 | bytes 6562485 | solution.py:30
  452.7 1.3 gather_fusion.9
  454.0 1.3 gather_fusion.8
  455.4 2.9 gather_fusion.11
  461.3 1.3 gather_fusion.9
  462.7 1.3 gather_fusion.8
  464.1 2.9 gather_fusion.11
  470.0 1.3 gather_fusion.9
  471.3 1.3 gather_fusion.8
  472.7 2.9 gather_fusion.11
  479.9 1.3 gather_fusion.8
  481.3 2.9 gather_fusion.11
  487.3 1.3 gather_fusion.9
  488.6 1.3 gather_fusion.8
  490.0 2.9 gather_fusion.11
  496.0 128.8 %reduce-scatter.8.cloned.1.call-done = bf16[128,256]{1,0:T(8,128)(2,1)} async-done(((bf16[512,256]{1,0:T(8,128)(2,1)}), bf16[128,256]{1,0:T(8,128)(2,1)}) %reduce-scatter.8.cloned.1.call-update) | async-done | bytes 65552 | tf_op jit(solution)/shard_map/reduce_scatter | solution.py:51
  624.8 1.6 fusion.27
  (163 shorter events, 58.2 us)
Async XLA Ops:
  6.5 207.8 %copy-start = (bf16[256,256]{1,0:T(8,128)(2,1)S(1)}, bf16[256,256]{1,0:T(8,128)(2,1)}, u32[]{:S(2)}) copy-start(bf16[256,256]{1,0:T(8,128)(2,1)} %param.21) | copy-start | bytes 393220
  6.5 207.8 %reduce-scatter.4.cloned.1.call-start = ((), (), s32[]{:S(2)}) async-start(), calls=%async_computation.3 | async-start | bytes 327680 | tf_op jit(solution)/shard_map/reduce_scatter | solution.py:51
  40.5 44.1 %copy-start.2 = (s32[128]{0:T(128)S(1)}, s32[128]{0:T(128)}, u32[]{:S(2)}) copy-start(s32[128]{0:T(128)} %param.20) | copy-start | bytes 1540
  40.5 173.8 %copy-start.1 = (bf16[128,256]{1,0:T(8,128)(2,1)S(1)}, bf16[128,256]{1,0:T(8,128)(2,1)}, u32[]{:S(2)}) copy-start(bf16[128,256]{1,0:T(8,128)(2,1)} %param.19) | copy-start | bytes 196612
  84.5 335.0 %reduce-scatter.6.cloned.1.call-start = ((), (), s32[]{:S(2)}) async-start(), calls=%async_computation.4 | async-start | bytes 327680 | tf_op jit(solution)/shard_map/reduce_scatter | solution.py:51
  290.7 334.1 %reduce-scatter.8.cloned.1.call-start = ((), (), s32[]{:S(2)}) async-start(), calls=%async_computation.5 | async-start | bytes 327680 | tf_op jit(solution)/shard_map/reduce_scatter | solution.py:51
Sparse Core Ops, SparseCore 0:
  84.6 129.6 reduce-scatter.3
  290.8 128.6 reduce-scatter.5
  496.1 128.6 reduce-scatter.7
where the time goes:
time: 643 us; the launch traced here: 633 us
  waiting for transfers between devices  387 us (60%)
  blocking collectives  96 us (15%)
  local copies, waits for them, and re-layouts  92.7 us (14%)
  other arithmetic  32.4 us (5%)
  between operations  13.9 us (2%)
  matrix products  9.21 us (1%)
    reduce_scatter x3, waiting for transfers between devices, shards(): lax.psum_scatter(partial_value.reshape(tgt_devices * own_rows, topics).as...  387 us
    all_gather x3, blocking collectives, shards(): gathered = lax.all_gather(opinion, 'src', axis=0, tiled=True)  96 us
    gather x15, local copies, waits for them, and re-layouts, add_group(): group_tiles = jnp.take(tile_block, clipped, axis=0)  44 us
    gather x15, local copies, waits for them, and re-layouts, add_group(): return running.at[jnp.take(targets, clipped)].add(contrib)  19.9 us
    gather x15, local copies, waits for them, and re-layouts, add_group(): jnp.take(sources, clipped) - offset  19.9 us
    scatter-add x15, other arithmetic, add_group(): return running.at[jnp.take(targets, clipped)].add(contrib)  19.8 us
  transfers between devices with their start and end apart: 3, of which 3 were waited for; matrix products, arithmetic and copies ran while one was open for 0% of the time, Pallas kernels for 0%

commit v1 on v0

v1 whole, which is shorter than its diff:
```python
import functools

import jax
import jax.numpy as jnp
from jax import lax
from jax.experimental import pallas as pl
from jax.experimental.pallas import tpu as pltpu
from jax.sharding import PartitionSpec as P

STEPS = 3
ROW_TILES = 4
CHUNK = 16
BOTH = ("src", "tgt")


def densify_kernel(rows_ref, cols_ref, count_ref, tiles_ref, out_ref, total_ref):
    group, chunk = pl.program_id(0), pl.program_id(1)
    row_tiles, col_tiles, edge, _ = total_ref.shape

    @pl.when(chunk == 0)
    def _():
        total_ref[...] = jnp.zeros_like(total_ref)

    def absorb(k, carry):
        slot = chunk * CHUNK + k
        row = rows_ref[slot] - group * row_tiles

        @pl.when((row >= 0) & (row < row_tiles))
        def _():
            col = cols_ref[slot]
            total_ref[row, col] += tiles_ref[k].astype(jnp.float32)

        return carry

    live = jnp.clip(count_ref[0] - chunk * CHUNK, 0, CHUNK)
    lax.fori_loop(0, live, absorb, 0)

    @pl.when(chunk == pl.num_programs(1) - 1)
    def _():
        for i in range(row_tiles):
            for j in range(col_tiles):
                out_ref[i * edge:(i + 1) * edge, j * edge:(j + 1) * edge] = total_ref[i, j].astype(out_ref.dtype)


def densify(rows, cols, count, tiles, n_rows, n_cols):
    slots, edge, _ = tiles.shape
    row_tiles = min(ROW_TILES, n_rows)

    def pick(g, c, rows_ref, cols_ref, count_ref):
        return jnp.minimum(c, lax.div(count_ref[0] - 1, CHUNK)), 0, 0

    return pl.pallas_call(
        densify_kernel,
        out_shape=jax.ShapeDtypeStruct((n_rows * edge, n_cols * edge), jnp.bfloat16),
        grid_spec=pltpu.PrefetchScalarGridSpec(
            num_scalar_prefetch=3,
            grid=(n_rows // row_tiles, pl.cdiv(slots, CHUNK)),
            in_specs=[pl.BlockSpec((CHUNK, edge, edge), pick)],
            out_specs=pl.BlockSpec((row_tiles * edge, n_cols * edge), lambda g, c, *_: (g, 0)),
            scratch_shapes=[pltpu.VMEM((row_tiles, n_cols, edge, edge), jnp.float32)],
        ),
        compiler_params=pltpu.CompilerParams(vmem_limit_bytes=40 * 2**20),
        cost_estimate=pl.CostEstimate(flops=slots * edge * edge, bytes_accessed=2 * slots * edge * edge, transcendentals=0),
        name="densify",
    )(rows, cols, count, tiles)


def product_kernel(columns, weights_ref, *refs):
    *parts, out_ref = refs
    total = None
    for at, ref in zip(columns, parts):
        width = ref.shape[0]
        term = jnp.dot(weights_ref[:, at * 128:at * 128 + width], ref[...], preferred_element_type=jnp.float32)
        total = term if total is None else total + term
    out_ref[...] = total.astype(out_ref.dtype)


def product(weights, parts, columns):
    n_rows, n_cols = weights.shape
    topics = parts[0].shape[1]
    rows = min(n_rows, ROW_TILES * 128)
    return pl.pallas_call(
        functools.partial(product_kernel, columns),
        out_shape=jax.ShapeDtypeStruct((n_rows, topics), jnp.bfloat16),
        grid=(n_rows // rows,),
        in_specs=[pl.BlockSpec((rows, n_cols), lambda g: (g, 0))]
        + [pl.BlockSpec(p.shape, lambda g: (0, 0)) for p in parts],
        out_specs=pl.BlockSpec((rows, topics), lambda g: (g, 0)),
        compiler_params=pltpu.CompilerParams(vmem_limit_bytes=40 * 2**20),
        cost_estimate=pl.CostEstimate(flops=2 * n_rows * n_cols * topics, bytes_accessed=2 * n_rows * n_cols, transcendentals=0),
        name="product",
    )(weights, *parts)


def bits_of(n):
    assert n & (n - 1) == 0
    return [1 << i for i in range(n.bit_length() - 1)]


def shards(initial, stubborn, coupling, tile_values, tile_target, tile_source, tile_count):
    own_rows, topics = initial.shape
    n_src, n_tgt = lax.axis_size("src"), lax.axis_size("tgt")
    edge = tile_values.shape[-1]
    assert own_rows == edge
    s, t = lax.axis_index("src"), lax.axis_index("tgt")
    tgt_bits, src_bits = bits_of(n_tgt), bits_of(n_src)
    top, low = src_bits[-1], src_bits[:-1]

    def swap(value, src_mask, tgt_mask):
        mask = src_mask * n_tgt + tgt_mask
        return lax.ppermute(value, BOTH, [(d, d ^ mask) for d in range(n_src * n_tgt)])

    def spread(blocks):
        held = dict(blocks)
        pairs = [low[i:i + 2] for i in range(0, len(low), 2)]
        for pair in pairs:
            masks = [m for m in (pair if len(pair) == 1 else (pair[0], pair[1], pair[0] | pair[1]))]
            fresh = {}
            for block, value in held.items():
                for m in masks:
                    fresh[block | m] = swap(value, m, 0)
            held.update(fresh)
        return held

    relative = tile_target[0, 0] ^ t
    rows = sum(jnp.where(relative & b != 0, n_tgt // (2 * b), 0) for b in tgt_bits)
    cols = tile_source[0, 0] ^ s
    weights = densify(rows, cols, tile_count[0], tile_values[0, 0], n_tgt, n_src)

    openness = ((256.0 - stubborn.astype(jnp.float32)) / 256.0)[:, None]
    own = jnp.concatenate([initial, jnp.broadcast_to(openness.astype(jnp.bfloat16), (own_rows, 128))], axis=1)
    far = swap(own, top, 0)

    def update(influence, packed):
        start = packed[:, :topics].astype(jnp.float32)
        part = packed[:, topics:topics + 1].astype(jnp.float32)
        coupled = jnp.dot(influence, coupling, preferred_element_type=jnp.float32)
        return (part * coupled + (1.0 - part) * start).astype(jnp.bfloat16)

    def add(a, b):
        return (a.astype(jnp.float32) + b.astype(jnp.float32)).astype(jnp.bfloat16)

    held = spread({0: initial, top: far[:, :topics]})
    for step in range(STEPS):
        masks = sorted(held)
        terms = product(weights, [held[m] for m in masks], masks)
        for bit in tgt_bits[:-1]:
            half = terms.shape[0] // 2
            terms = add(terms[:half], swap(terms[half:], 0, bit))
        mine, other = terms[:own_rows], terms[own_rows:]
        last = tgt_bits[-1]
        near = update(add(mine, swap(other, 0, last)), own)
        if step == STEPS - 1:
            return near
        away = update(add(swap(mine, top, 0), swap(other, top, last)), far)
        held = spread({0: near, top: away})


def solution(mesh):
    in_specs = (
        P(("src", "tgt"), None),
        P(("src", "tgt")),
        P(),
        P("src", "tgt", None, None, None),
        P("src", "tgt", None),
        P("src", "tgt", None),
        P("src", "tgt"),
    )
    out_specs = P(("src", "tgt"), None)
    return jax.shard_map(shards, mesh=mesh, in_specs=in_specs, out_specs=out_specs, check_vma=False)
```

time: 643 us -> 76.2 us (0.12); the launches traced: 633 us -> 75.9 us
  waiting for transfers between devices: 387 us -> 27.6 us
  blocking collectives: 96 us -> 0 us
  local copies, waits for them, and re-layouts: 92.7 us -> 2.49 us
  starting transfers between devices: 0.09 us -> 35.8 us
  other arithmetic: 32.4 us -> 3.09 us
  between operations: 13.9 us -> 0.89 us
  matrix products: 9.21 us -> 1.47 us
    reduce_scatter x3 -> x0, waiting for transfers between devices: 387 us -> none  [shards(): lax.psum_scatter(partial_value.reshape(tgt_devices * own_rows, topics).as...]
    all_gather x3 -> x0, blocking collectives: 96 us -> none  [shards(): gathered = lax.all_gather(opinion, 'src', axis=0, tiled=True)]
    gather x60 -> x0, local copies, waits for them, and re-layouts: 92.5 us -> none  [the longest x15 44 us: add_group(): group_tiles = jnp.take(tile_block, clipped, axis=0)]
    ppermute x0 -> x29, starting transfers between devices: none -> 35.8 us  [swap(): lax.ppermute(value, BOTH, [(d, d ^ mask) for d in range(n_src * n_tgt)])]
    ppermute x0 -> x29, waiting for transfers between devices: none -> 27.6 us  [swap(): lax.ppermute(value, BOTH, [(d, d ^ mask) for d in range(n_src * n_tgt)])]
    scatter-add x15 -> x0, other arithmetic: 19.8 us -> none  [add_group(): return running.at[jnp.take(targets, clipped)].add(contrib)]
    lt x15 -> x0, other arithmetic: 9.83 us -> none  [add_group(): active = slot_ids < end_slot]
    dot_general x18 -> x5, matrix products: 9.21 us -> 1.47 us  [update(): coupled = jnp.dot(influence, coupling, preferred_element_type=jnp.float32)]
  transfers between devices with their start and end apart: 3 -> 29, of which waited for: 3 -> 15; matrix products, arithmetic and copies ran while one was open for 0% -> 5% of each run, Pallas kernels for 0% -> 3%
where the time goes in v1:
time: 76.2 us; the launch traced here: 75.9 us
  starting transfers between devices  35.8 us (47%)
  waiting for transfers between devices  27.6 us (36%)
  Pallas kernels  4.54 us (6%)
  other arithmetic  3.09 us (4%)
  local copies, waits for them, and re-layouts  2.49 us (3%)
  matrix products  1.47 us (2%)
  between operations  0.89 us (1%)
    ppermute x29, starting transfers between devices, swap(): lax.ppermute(value, BOTH, [(d, d ^ mask) for d in range(n_src * n_tgt)])  35.8 us
    ppermute x29, waiting for transfers between devices, swap(): lax.ppermute(value, BOTH, [(d, d ^ mask) for d in range(n_src * n_tgt)])  27.6 us
    pallas_call x1, Pallas kernels, densify(): pl.pallas_call(densify_kernel, out_shape=jax.ShapeDtypeStruct((n_rows * e...  2.45 us
    unnamed x6, local copies, waits for them, and re-layouts  2.34 us
    pallas_call x3, Pallas kernels, product(): pl.pallas_call(functools.partial(product_kernel, columns), out_shape=jax....  2.08 us
  transfers between devices with their start and end apart: 29, of which 15 were waited for; matrix products, arithmetic and copies ran while one was open for 5% of the time, Pallas kernels for 3%

profile of v1, /device:TPU:0, one launch (start us, length us, event | category | flops | bytes accessed | tf_op | source)
XLA Modules:
  0.0 75.9 jit_solution(9106700466148041393)
XLA Ops:
  0.0 4.0 %collective-permute-start.2 = (bf16[128,256]{1,0:T(8,128)(2,1)}, bf16[128,256]{1,0:T(8,128)(2,1)S(1)}, u32[]{:S(2)}, u32[]{:S(2)}) collective-permute-start(bf16[128,256]{1,0:T(8,128)(2,1)} %refs_0_.1), channel_id=1, source_target_pairs={{0,12},{1,13},{2,14},{3,15},{4,8},{5,9},{6,10},{7,11},{8,4},{9,5},... | collective-permute-start | bytes 196616 | tf_op jit(solution)/shard_map/ppermute | solution.py:111
  4.0 0.4 collective-permute-start.1
  4.6 0.7 fusion.13
  5.3 0.9 %pad_maximum_fusion = bf16[128,384]{1,0:T(8,128)(2,1)S(1)} fusion(bf16[128,128]{1,0:T(8,128)(2,1)S(1)} %broadcast_in_dim.15, bf16[128,256]{1,0:T(8,128)(2,1)} %refs_0_.1), kind=kLoop, calls=%fused_computation.25 | loop fusion | flops 196608 | bytes 196608 | tf_op jit(solution)/shard_map/concatenate | solution.py:131
  6.2 3.0 %collective-permute-start.3 = (bf16[128,384]{1,0:T(8,128)(2,1)S(1)}, bf16[128,384]{1,0:T(8,128)(2,1)S(1)}, u32[]{:S(2)}, u32[]{:S(2)}) collective-permute-start(bf16[128,384]{1,0:T(8,128)(2,1)S(1)} %pad_maximum_fusion), channel_id=1, source_target_pairs={{0,16},{1,17},{2,18},{3,19},{4,20},{5,21},{6,22},{7,23},{8,24},{9,... | collective-permute-start | bytes 294920 | tf_op jit(solution)/shard_map/ppermute | solution.py:111
  9.2 0.7 fusion.12
  9.9 3.7 %collective-permute-done.3 = bf16[128,384]{1,0:T(8,128)(2,1)S(1)} collective-permute-done((bf16[128,384]{1,0:T(8,128)(2,1)S(1)}, bf16[128,384]{1,0:T(8,128)(2,1)S(1)}, u32[]{:S(2)}, u32[]{:S(2)}) %collective-permute-start.3) | collective-permute-done | bytes 98336 | tf_op jit(solution)/shard_map/ppermute | solution.py:111
  13.6 1.4 %collective-permute-start.6 = (bf16[128,256]{1,0:T(8,128)(2,1)S(1)}, bf16[128,256]{1,0:T(8,128)(2,1)S(1)}, u32[]{:S(2)}, u32[]{:S(2)}) collective-permute-start(bf16[128,256]{1,0:T(8,128)(2,1)S(1)} %slice.62.refs_4_), channel_id=1, source_target_pairs={{0,12},{1,13},{2,14},{3,15},{4,8},{5,9},{6,10},{7,11},{8,4},{9,5},... | collective-permute-start | bytes 196616 | tf_op jit(solution)/shard_map/ppermute | solution.py:111
  14.9 1.5 %collective-permute-start.5 = (bf16[128,256]{1,0:T(8,128)(2,1)S(1)}, bf16[128,256]{1,0:T(8,128)(2,1)S(1)}, u32[]{:S(2)}, u32[]{:S(2)}) collective-permute-start(bf16[128,256]{1,0:T(8,128)(2,1)S(1)} %slice.62.refs_4_), channel_id=1, source_target_pairs={{0,8},{1,9},{2,10},{3,11},{4,12},{5,13},{6,14},{7,15},{8,0},{9,1},... | collective-permute-start | bytes 196616 | tf_op jit(solution)/shard_map/ppermute | solution.py:111
  16.4 0.7 collective-permute-start.4
  17.0 0.7 broadcast_xor_fusion
  18.4 2.3 %copy-done.1 = bf16[1,1,144,128,128]{4,3,2,1,0:T(8,128)(2,1)S(1)} copy-done((bf16[1,1,144,128,128]{4,3,2,1,0:T(8,128)(2,1)S(1)}, bf16[1,1,144,128,128]{4,3,2,1,0:T(8,128)(2,1)}, u32[]{:S(2)}) %copy-start.1) | copy-done | bytes 4718616
  20.7 2.5 %densify.1.weights_ref = bf16[512,1024]{1,0:T(8,128)(2,1)S(1)} custom-call(s32[144]{0:T(256)S(1)} %bitcast.11, s32[144]{0:T(256)S(1)} %bitcast.12, s32[1]{0:T(128)} %bitcast.9.count_ref, bf16[144,128,128]{2,1,0:T(8,128)(2,1)S(1)} %bitcast.10), custom_call_target="tpu_custom_call" | custom-call | flops 2359296 | bytes 4718592 | tf_op jit(solution)/shard_map/densify/pallas_call | solution.py:52
  23.2 0.7 product.3
  24.0 1.3 %collective-permute-done.7 = bf16[256,256]{1,0:T(8,128)(2,1)S(1)} collective-permute-done((bf16[256,256]{1,0:T(8,128)(2,1)S(1)}, bf16[256,256]{1,0:T(8,128)(2,1)S(1)}, u32[]{:S(2)}, u32[]{:S(2)}) %collective-permute-start.7) | collective-permute-done | bytes 131104 | tf_op jit(solution)/shard_map/ppermute | solution.py:111
  25.4 2.0 %collective-permute-start.12 = (bf16[128,256]{1,0:T(8,128)(2,1)S(1)}, bf16[128,256]{1,0:T(8,128)(2,1)S(1)}, u32[]{:S(2)}, u32[]{:S(2)}) collective-permute-start(bf16[128,256]{1,0:T(8,128)(2,1)S(1)} %get-tuple-element.9), channel_id=1, source_target_pairs={{0,16},{1,17},{2,18},{3,19},{4,20},{5,21},{6,22},{7,23},{8,24},{9,... | collective-permute-start | bytes 196616 | tf_op jit(solution)/shard_map/ppermute | solution.py:111
  27.4 1.9 %collective-permute-start.13 = (bf16[128,256]{1,0:T(8,128)(2,1)S(1)}, bf16[128,256]{1,0:T(8,128)(2,1)S(1)}, u32[]{:S(2)}, u32[]{:S(2)}) collective-permute-start(bf16[128,256]{1,0:T(8,128)(2,1)S(1)} %get-tuple-element.10), channel_id=1, source_target_pairs={{0,18},{1,19},{2,16},{3,17},{4,22},{5,23},{6,20},{7,21},{8,26},{9,... | collective-permute-start | bytes 196616 | tf_op jit(solution)/shard_map/ppermute | solution.py:111
  29.4 0.7 collective-permute-start.8
  30.1 2.4 %collective-permute-done.12 = bf16[128,256]{1,0:T(8,128)(2,1)S(1)} collective-permute-done((bf16[128,256]{1,0:T(8,128)(2,1)S(1)}, bf16[128,256]{1,0:T(8,128)(2,1)S(1)}, u32[]{:S(2)}, u32[]{:S(2)}) %collective-permute-start.12) | collective-permute-done | bytes 65568 | tf_op jit(solution)/shard_map/ppermute | solution.py:111
  32.5 3.1 %collective-permute-done.13 = bf16[128,256]{1,0:T(8,128)(2,1)S(1)} collective-permute-done((bf16[128,256]{1,0:T(8,128)(2,1)S(1)}, bf16[128,256]{1,0:T(8,128)(2,1)S(1)}, u32[]{:S(2)}, u32[]{:S(2)}) %collective-permute-start.13) | collective-permute-done | bytes 65568 | tf_op jit(solution)/shard_map/ppermute | solution.py:111
  35.8 0.8 %collective-permute-start.16 = (bf16[128,256]{1,0:T(8,128)(2,1)S(1)}, bf16[128,256]{1,0:T(8,128)(2,1)S(1)}, u32[]{:S(2)}, u32[]{:S(2)}) collective-permute-start(bf16[128,256]{1,0:T(8,128)(2,1)S(1)} %fusion.8.refs_4_), channel_id=1, source_target_pairs={{0,12},{1,13},{2,14},{3,15},{4,8},{5,9},{6,10},{7,11},{8,4},{9,5},... | collective-permute-start | bytes 196616 | tf_op jit(solution)/shard_map/ppermute | solution.py:111
  36.6 2.4 %collective-permute-start.15 = (bf16[128,256]{1,0:T(8,128)(2,1)S(1)}, bf16[128,256]{1,0:T(8,128)(2,1)S(1)}, u32[]{:S(2)}, u32[]{:S(2)}) collective-permute-start(bf16[128,256]{1,0:T(8,128)(2,1)S(1)} %fusion.8.refs_4_), channel_id=1, source_target_pairs={{0,8},{1,9},{2,10},{3,11},{4,12},{5,13},{6,14},{7,15},{8,0},{9,1},... | collective-permute-start | bytes 196616 | tf_op jit(solution)/shard_map/ppermute | solution.py:111
  39.0 0.3 collective-permute-start.14
  39.5 1.2 %collective-permute-start.11 = (bf16[128,256]{1,0:T(8,128)(2,1)S(1)}, bf16[128,256]{1,0:T(8,128)(2,1)S(1)}, u32[]{:S(2)}, u32[]{:S(2)}) collective-permute-start(bf16[128,256]{1,0:T(8,128)(2,1)S(1)} %fusion.9.refs_0_), channel_id=1, source_target_pairs={{0,12},{1,13},{2,14},{3,15},{4,8},{5,9},{6,10},{7,11},{8,4},{9,5},... | collective-permute-start | bytes 196616 | tf_op jit(solution)/shard_map/ppermute | solution.py:111
  40.7 2.0 %collective-permute-start.10 = (bf16[128,256]{1,0:T(8,128)(2,1)S(1)}, bf16[128,256]{1,0:T(8,128)(2,1)S(1)}, u32[]{:S(2)}, u32[]{:S(2)}) collective-permute-start(bf16[128,256]{1,0:T(8,128)(2,1)S(1)} %fusion.9.refs_0_), channel_id=1, source_target_pairs={{0,8},{1,9},{2,10},{3,11},{4,12},{5,13},{6,14},{7,15},{8,0},{9,1},... | collective-permute-start | bytes 196616 | tf_op jit(solution)/shard_map/ppermute | solution.py:111
  42.7 0.4 collective-permute-start.9
  43.1 0.5 collective-permute-done.14.refs_5_
  43.6 1.2 %collective-permute-done.11.refs_3_ = bf16[128,256]{1,0:T(8,128)(2,1)S(1)} collective-permute-done((bf16[128,256]{1,0:T(8,128)(2,1)S(1)}, bf16[128,256]{1,0:T(8,128)(2,1)S(1)}, u32[]{:S(2)}, u32[]{:S(2)}) %collective-permute-start.11) | collective-permute-done | bytes 65568 | tf_op jit(solution)/shard_map/ppermute | solution.py:111
  44.8 0.8 %collective-permute-done.10.refs_2_ = bf16[128,256]{1,0:T(8,128)(2,1)S(1)} collective-permute-done((bf16[128,256]{1,0:T(8,128)(2,1)S(1)}, bf16[128,256]{1,0:T(8,128)(2,1)S(1)}, u32[]{:S(2)}, u32[]{:S(2)}) %collective-permute-start.10) | collective-permute-done | bytes 65568 | tf_op jit(solution)/shard_map/ppermute | solution.py:111
  45.7 1.3 %collective-permute-done.9.refs_1_ = bf16[128,256]{1,0:T(8,128)(2,1)S(1)} collective-permute-done((bf16[128,256]{1,0:T(8,128)(2,1)S(1)}, bf16[128,256]{1,0:T(8,128)(2,1)S(1)}, u32[]{:S(2)}, u32[]{:S(2)}) %collective-permute-start.9) | collective-permute-done | bytes 65568 | tf_op jit(solution)/shard_map/ppermute | solution.py:111
  47.0 0.7 product.4
  47.8 1.3 %collective-permute-done.17 = bf16[256,256]{1,0:T(8,128)(2,1)S(1)} collective-permute-done((bf16[256,256]{1,0:T(8,128)(2,1)S(1)}, bf16[256,256]{1,0:T(8,128)(2,1)S(1)}, u32[]{:S(2)}, u32[]{:S(2)}) %collective-permute-start.17) | collective-permute-done | bytes 131104 | tf_op jit(solution)/shard_map/ppermute | solution.py:111
  49.2 0.8 collective-permute-start.22
  49.9 1.9 %collective-permute-start.23 = (bf16[128,256]{1,0:T(8,128)(2,1)S(1)}, bf16[128,256]{1,0:T(8,128)(2,1)S(1)}, u32[]{:S(2)}, u32[]{:S(2)}) collective-permute-start(bf16[128,256]{1,0:T(8,128)(2,1)S(1)} %get-tuple-element.8), channel_id=1, source_target_pairs={{0,18},{1,19},{2,16},{3,17},{4,22},{5,23},{6,20},{7,21},{8,26},{9,... | collective-permute-start | bytes 196616 | tf_op jit(solution)/shard_map/ppermute | solution.py:111
  51.9 1.8 %collective-permute-start.18 = (bf16[128,256]{1,0:T(8,128)(2,1)S(1)}, bf16[128,256]{1,0:T(8,128)(2,1)S(1)}, u32[]{:S(2)}, u32[]{:S(2)}) collective-permute-start(bf16[128,256]{1,0:T(8,128)(2,1)S(1)} %get-tuple-element.8), channel_id=1, source_target_pairs={{0,2},{1,3},{2,0},{3,1},{4,6},{5,7},{6,4},{7,5},{8,10},{9,11},{10,... | collective-permute-start | bytes 196616 | tf_op jit(solution)/shard_map/ppermute | solution.py:111
  53.6 1.7 %collective-permute-done.22 = bf16[128,256]{1,0:T(8,128)(2,1)S(1)} collective-permute-done((bf16[128,256]{1,0:T(8,128)(2,1)S(1)}, bf16[128,256]{1,0:T(8,128)(2,1)S(1)}, u32[]{:S(2)}, u32[]{:S(2)}) %collective-permute-start.22) | collective-permute-done | bytes 65568 | tf_op jit(solution)/shard_map/ppermute | solution.py:111
  55.3 2.9 %collective-permute-done.23 = bf16[128,256]{1,0:T(8,128)(2,1)S(1)} collective-permute-done((bf16[128,256]{1,0:T(8,128)(2,1)S(1)}, bf16[128,256]{1,0:T(8,128)(2,1)S(1)}, u32[]{:S(2)}, u32[]{:S(2)}) %collective-permute-start.23) | collective-permute-done | bytes 65568 | tf_op jit(solution)/shard_map/ppermute | solution.py:111
  58.5 2.1 %collective-permute-start.25 = (bf16[128,256]{1,0:T(8,128)(2,1)S(1)}, bf16[128,256]{1,0:T(8,128)(2,1)S(1)}, u32[]{:S(2)}, u32[]{:S(2)}) collective-permute-start(bf16[128,256]{1,0:T(8,128)(2,1)S(1)} %fusion.6.refs_4_), channel_id=1, source_target_pairs={{0,8},{1,9},{2,10},{3,11},{4,12},{5,13},{6,14},{7,15},{8,0},{9,1},... | collective-permute-start | bytes 196616 | tf_op jit(solution)/shard_map/ppermute | solution.py:111
  60.6 1.4 %collective-permute-start.24 = (bf16[128,256]{1,0:T(8,128)(2,1)S(1)}, bf16[128,256]{1,0:T(8,128)(2,1)S(1)}, u32[]{:S(2)}, u32[]{:S(2)}) collective-permute-start(bf16[128,256]{1,0:T(8,128)(2,1)S(1)} %fusion.6.refs_4_), channel_id=1, source_target_pairs={{0,4},{1,5},{2,6},{3,7},{4,0},{5,1},{6,2},{7,3},{8,12},{9,13},{10,... | collective-permute-start | bytes 196616 | tf_op jit(solution)/shard_map/ppermute | solution.py:111
  62.3 2.0 %collective-permute-start.20 = (bf16[128,256]{1,0:T(8,128)(2,1)S(1)}, bf16[128,256]{1,0:T(8,128)(2,1)S(1)}, u32[]{:S(2)}, u32[]{:S(2)}) collective-permute-start(bf16[128,256]{1,0:T(8,128)(2,1)S(1)} %fusion.7.refs_0_), channel_id=1, source_target_pairs={{0,8},{1,9},{2,10},{3,11},{4,12},{5,13},{6,14},{7,15},{8,0},{9,1},... | collective-permute-start | bytes 196616 | tf_op jit(solution)/shard_map/ppermute | solution.py:111
  64.3 1.4 %collective-permute-start.19 = (bf16[128,256]{1,0:T(8,128)(2,1)S(1)}, bf16[128,256]{1,0:T(8,128)(2,1)S(1)}, u32[]{:S(2)}, u32[]{:S(2)}) collective-permute-start(bf16[128,256]{1,0:T(8,128)(2,1)S(1)} %fusion.7.refs_0_), channel_id=1, source_target_pairs={{0,4},{1,5},{2,6},{3,7},{4,0},{5,1},{6,2},{7,3},{8,12},{9,13},{10,... | collective-permute-start | bytes 196616 | tf_op jit(solution)/shard_map/ppermute | solution.py:111
  65.7 1.6 %collective-permute-done.21.refs_3_ = bf16[128,256]{1,0:T(8,128)(2,1)S(1)} collective-permute-done((bf16[128,256]{1,0:T(8,128)(2,1)S(1)}, bf16[128,256]{1,0:T(8,128)(2,1)S(1)}, u32[]{:S(2)}, u32[]{:S(2)}) %collective-permute-start.21) | collective-permute-done | bytes 65568 | tf_op jit(solution)/shard_map/ppermute | solution.py:111
  67.4 1.2 %collective-permute-done.19.refs_1_ = bf16[128,256]{1,0:T(8,128)(2,1)S(1)} collective-permute-done((bf16[128,256]{1,0:T(8,128)(2,1)S(1)}, bf16[128,256]{1,0:T(8,128)(2,1)S(1)}, u32[]{:S(2)}, u32[]{:S(2)}) %collective-permute-start.19) | collective-permute-done | bytes 65568 | tf_op jit(solution)/shard_map/ppermute | solution.py:111
  68.6 0.7 product.5
  69.4 1.3 %collective-permute-done.27 = bf16[256,256]{1,0:T(8,128)(2,1)S(1)} collective-permute-done((bf16[256,256]{1,0:T(8,128)(2,1)S(1)}, bf16[256,256]{1,0:T(8,128)(2,1)S(1)}, u32[]{:S(2)}, u32[]{:S(2)}) %collective-permute-start.27) | collective-permute-done | bytes 131104 | tf_op jit(solution)/shard_map/ppermute | solution.py:111
  70.8 1.3 %collective-permute-start.28 = (bf16[128,256]{1,0:T(8,128)(2,1)S(1)}, bf16[128,256]{1,0:T(8,128)(2,1)S(1)}, u32[]{:S(2)}, u32[]{:S(2)}) collective-permute-start(bf16[128,256]{1,0:T(8,128)(2,1)S(1)} %slice.75), channel_id=1, source_target_pairs={{0,2},{1,3},{2,0},{3,1},{4,6},{5,7},{6,4},{7,5},{8,10},{9,11},{10,... | collective-permute-start | bytes 196616 | tf_op jit(solution)/shard_map/ppermute | solution.py:111
  72.1 3.0 %collective-permute-done.28 = bf16[128,256]{1,0:T(8,128)(2,1)S(1)} collective-permute-done((bf16[128,256]{1,0:T(8,128)(2,1)S(1)}, bf16[128,256]{1,0:T(8,128)(2,1)S(1)}, u32[]{:S(2)}, u32[]{:S(2)}) %collective-permute-start.28) | collective-permute-done | bytes 65568 | tf_op jit(solution)/shard_map/ppermute | solution.py:111
  75.1 0.8 %fusion.5 = bf16[128,256]{1,0:T(8,128)(2,1)} fusion(bf16[256,256]{1,0:T(8,128)(2,1)S(1)} %copy-done, bf16[128,256]{1,0:T(8,128)(2,1)S(1)} %copy-done.2, bf16[128,256]{1,0:T(8,128)(2,1)S(1)} %collective-permute-done.28, bf16[256,256]{1,0:T(8,128)(2,1)S(1)} %add_convert_fusion, f32[128]{0:T(128)S(1)} %get-tuple-element.12, f32[128]{0:T(128)S(1)} %get-tuple-element.11), kind=kOutput, calls=%fused_computation.10 | convolution fusion | flops 17072128 | bytes 394240 | tf_op jit(solution)/shard_map/dot_general | solution.py:137
  (41 shorter events, 1.8 us)
Async XLA Ops:
  0.0 35.6 %copy-start = (bf16[256,256]{1,0:T(8,128)(2,1)S(1)}, bf16[256,256]{1,0:T(8,128)(2,1)}, u32[]{:S(2)}) copy-start(bf16[256,256]{1,0:T(8,128)(2,1)} %param.9) | copy-start | bytes 393220
  0.0 23.2 %copy-start.2 = (bf16[128,256]{1,0:T(8,128)(2,1)S(1)}, bf16[128,256]{1,0:T(8,128)(2,1)}, u32[]{:S(2)}) copy-start(bf16[128,256]{1,0:T(8,128)(2,1)} %refs_0_.1) | copy-start | bytes 196612
  0.0 16.4 %collective-permute-start.2 = (bf16[128,256]{1,0:T(8,128)(2,1)}, bf16[128,256]{1,0:T(8,128)(2,1)S(1)}, u32[]{:S(2)}, u32[]{:S(2)}) collective-permute-start(bf16[128,256]{1,0:T(8,128)(2,1)} %refs_0_.1), channel_id=1, source_target_pairs={{0,12},{1,13},{2,14},{3,15},{4,8},{5,9},{6,10},{7,11},{8,4},{9,5},... | collective-permute-start | bytes 196616 | tf_op jit(solution)/shard_map/ppermute | solution.py:111
  4.0 19.2 %collective-permute-start.1 = (bf16[128,256]{1,0:T(8,128)(2,1)}, bf16[128,256]{1,0:T(8,128)(2,1)S(1)}, u32[]{:S(2)}, u32[]{:S(2)}) collective-permute-start(bf16[128,256]{1,0:T(8,128)(2,1)} %refs_0_.1), channel_id=1, source_target_pairs={{0,8},{1,9},{2,10},{3,11},{4,12},{5,13},{6,14},{7,15},{8,0},{9,1},... | collective-permute-start | bytes 196616 | tf_op jit(solution)/shard_map/ppermute | solution.py:111
  4.4 18.8 %collective-permute-start = (bf16[128,256]{1,0:T(8,128)(2,1)}, bf16[128,256]{1,0:T(8,128)(2,1)S(1)}, u32[]{:S(2)}, u32[]{:S(2)}) collective-permute-start(bf16[128,256]{1,0:T(8,128)(2,1)} %refs_0_.1), channel_id=1, source_target_pairs={{0,4},{1,5},{2,6},{3,7},{4,0},{5,1},{6,2},{7,3},{8,12},{9,13},{10,... | collective-permute-start | bytes 196616 | tf_op jit(solution)/shard_map/ppermute | solution.py:111
  6.2 7.3 %collective-permute-start.3 = (bf16[128,384]{1,0:T(8,128)(2,1)S(1)}, bf16[128,384]{1,0:T(8,128)(2,1)S(1)}, u32[]{:S(2)}, u32[]{:S(2)}) collective-permute-start(bf16[128,384]{1,0:T(8,128)(2,1)S(1)} %pad_maximum_fusion), channel_id=1, source_target_pairs={{0,16},{1,17},{2,18},{3,19},{4,20},{5,21},{6,22},{7,23},{8,24},{9,... | collective-permute-start | bytes 294920 | tf_op jit(solution)/shard_map/ppermute | solution.py:111
  13.6 9.6 %collective-permute-start.6 = (bf16[128,256]{1,0:T(8,128)(2,1)S(1)}, bf16[128,256]{1,0:T(8,128)(2,1)S(1)}, u32[]{:S(2)}, u32[]{:S(2)}) collective-permute-start(bf16[128,256]{1,0:T(8,128)(2,1)S(1)} %slice.62.refs_4_), channel_id=1, source_target_pairs={{0,12},{1,13},{2,14},{3,15},{4,8},{5,9},{6,10},{7,11},{8,4},{9,5},... | collective-permute-start | bytes 196616 | tf_op jit(solution)/shard_map/ppermute | solution.py:111
  14.9 8.3 %collective-permute-start.5 = (bf16[128,256]{1,0:T(8,128)(2,1)S(1)}, bf16[128,256]{1,0:T(8,128)(2,1)S(1)}, u32[]{:S(2)}, u32[]{:S(2)}) collective-permute-start(bf16[128,256]{1,0:T(8,128)(2,1)S(1)} %slice.62.refs_4_), channel_id=1, source_target_pairs={{0,8},{1,9},{2,10},{3,11},{4,12},{5,13},{6,14},{7,15},{8,0},{9,1},... | collective-permute-start | bytes 196616 | tf_op jit(solution)/shard_map/ppermute | solution.py:111
  16.4 6.8 %collective-permute-start.4 = (bf16[128,256]{1,0:T(8,128)(2,1)S(1)}, bf16[128,256]{1,0:T(8,128)(2,1)S(1)}, u32[]{:S(2)}, u32[]{:S(2)}) collective-permute-start(bf16[128,256]{1,0:T(8,128)(2,1)S(1)} %slice.62.refs_4_), channel_id=1, source_target_pairs={{0,4},{1,5},{2,6},{3,7},{4,0},{5,1},{6,2},{7,3},{8,12},{9,13},{10,... | collective-permute-start | bytes 196616 | tf_op jit(solution)/shard_map/ppermute | solution.py:111
  18.4 2.3 %copy-start.1 = (bf16[1,1,144,128,128]{4,3,2,1,0:T(8,128)(2,1)S(1)}, bf16[1,1,144,128,128]{4,3,2,1,0:T(8,128)(2,1)}, u32[]{:S(2)}) copy-start(bf16[1,1,144,128,128]{4,3,2,1,0:T(8,128)(2,1)} %param.10) | copy-start | bytes 14155780
  24.0 1.4 %collective-permute-start.7 = (bf16[256,256]{1,0:T(8,128)(2,1)S(1)}, bf16[256,256]{1,0:T(8,128)(2,1)S(1)}, u32[]{:S(2)}, u32[]{:S(2)}) collective-permute-start(bf16[256,256]{1,0:T(8,128)(2,1)S(1)} %slice.64), channel_id=1, source_target_pairs={{0,1},{1,0},{2,3},{3,2},{4,5},{5,4},{6,7},{7,6},{8,9},{9,8},{10,11... | collective-permute-start | bytes 393224 | tf_op jit(solution)/shard_map/ppermute | solution.py:111
  25.4 7.0 %collective-permute-start.12 = (bf16[128,256]{1,0:T(8,128)(2,1)S(1)}, bf16[128,256]{1,0:T(8,128)(2,1)S(1)}, u32[]{:S(2)}, u32[]{:S(2)}) collective-permute-start(bf16[128,256]{1,0:T(8,128)(2,1)S(1)} %get-tuple-element.9), channel_id=1, source_target_pairs={{0,16},{1,17},{2,18},{3,19},{4,20},{5,21},{6,22},{7,23},{8,24},{9,... | collective-permute-start | bytes 196616 | tf_op jit(solution)/shard_map/ppermute | solution.py:111
  27.4 8.2 %collective-permute-start.13 = (bf16[128,256]{1,0:T(8,128)(2,1)S(1)}, bf16[128,256]{1,0:T(8,128)(2,1)S(1)}, u32[]{:S(2)}, u32[]{:S(2)}) collective-permute-start(bf16[128,256]{1,0:T(8,128)(2,1)S(1)} %get-tuple-element.10), channel_id=1, source_target_pairs={{0,18},{1,19},{2,16},{3,17},{4,22},{5,23},{6,20},{7,21},{8,26},{9,... | collective-permute-start | bytes 196616 | tf_op jit(solution)/shard_map/ppermute | solution.py:111
  29.4 9.9 %collective-permute-start.8 = (bf16[128,256]{1,0:T(8,128)(2,1)S(1)}, bf16[128,256]{1,0:T(8,128)(2,1)S(1)}, u32[]{:S(2)}, u32[]{:S(2)}) collective-permute-start(bf16[128,256]{1,0:T(8,128)(2,1)S(1)} %get-tuple-element.10), channel_id=1, source_target_pairs={{0,2},{1,3},{2,0},{3,1},{4,6},{5,7},{6,4},{7,5},{8,10},{9,11},{10,... | collective-permute-start | bytes 196616 | tf_op jit(solution)/shard_map/ppermute | solution.py:111
  35.8 7.0 %collective-permute-start.16 = (bf16[128,256]{1,0:T(8,128)(2,1)S(1)}, bf16[128,256]{1,0:T(8,128)(2,1)S(1)}, u32[]{:S(2)}, u32[]{:S(2)}) collective-permute-start(bf16[128,256]{1,0:T(8,128)(2,1)S(1)} %fusion.8.refs_4_), channel_id=1, source_target_pairs={{0,12},{1,13},{2,14},{3,15},{4,8},{5,9},{6,10},{7,11},{8,4},{9,5},... | collective-permute-start | bytes 196616 | tf_op jit(solution)/shard_map/ppermute | solution.py:111
  36.6 6.5 %collective-permute-start.15 = (bf16[128,256]{1,0:T(8,128)(2,1)S(1)}, bf16[128,256]{1,0:T(8,128)(2,1)S(1)}, u32[]{:S(2)}, u32[]{:S(2)}) collective-permute-start(bf16[128,256]{1,0:T(8,128)(2,1)S(1)} %fusion.8.refs_4_), channel_id=1, source_target_pairs={{0,8},{1,9},{2,10},{3,11},{4,12},{5,13},{6,14},{7,15},{8,0},{9,1},... | collective-permute-start | bytes 196616 | tf_op jit(solution)/shard_map/ppermute | solution.py:111
  39.0 4.6 %collective-permute-start.14 = (bf16[128,256]{1,0:T(8,128)(2,1)S(1)}, bf16[128,256]{1,0:T(8,128)(2,1)S(1)}, u32[]{:S(2)}, u32[]{:S(2)}) collective-permute-start(bf16[128,256]{1,0:T(8,128)(2,1)S(1)} %fusion.8.refs_4_), channel_id=1, source_target_pairs={{0,4},{1,5},{2,6},{3,7},{4,0},{5,1},{6,2},{7,3},{8,12},{9,13},{10,... | collective-permute-start | bytes 196616 | tf_op jit(solution)/shard_map/ppermute | solution.py:111
  39.5 5.3 %collective-permute-start.11 = (bf16[128,256]{1,0:T(8,128)(2,1)S(1)}, bf16[128,256]{1,0:T(8,128)(2,1)S(1)}, u32[]{:S(2)}, u32[]{:S(2)}) collective-permute-start(bf16[128,256]{1,0:T(8,128)(2,1)S(1)} %fusion.9.refs_0_), channel_id=1, source_target_pairs={{0,12},{1,13},{2,14},{3,15},{4,8},{5,9},{6,10},{7,11},{8,4},{9,5},... | collective-permute-start | bytes 196616 | tf_op jit(solution)/shard_map/ppermute | solution.py:111
  40.7 5.0 %collective-permute-start.10 = (bf16[128,256]{1,0:T(8,128)(2,1)S(1)}, bf16[128,256]{1,0:T(8,128)(2,1)S(1)}, u32[]{:S(2)}, u32[]{:S(2)}) collective-permute-start(bf16[128,256]{1,0:T(8,128)(2,1)S(1)} %fusion.9.refs_0_), channel_id=1, source_target_pairs={{0,8},{1,9},{2,10},{3,11},{4,12},{5,13},{6,14},{7,15},{8,0},{9,1},... | collective-permute-start | bytes 196616 | tf_op jit(solution)/shard_map/ppermute | solution.py:111
  42.7 4.3 %collective-permute-start.9 = (bf16[128,256]{1,0:T(8,128)(2,1)S(1)}, bf16[128,256]{1,0:T(8,128)(2,1)S(1)}, u32[]{:S(2)}, u32[]{:S(2)}) collective-permute-start(bf16[128,256]{1,0:T(8,128)(2,1)S(1)} %fusion.9.refs_0_), channel_id=1, source_target_pairs={{0,4},{1,5},{2,6},{3,7},{4,0},{5,1},{6,2},{7,3},{8,12},{9,13},{10,... | collective-permute-start | bytes 196616 | tf_op jit(solution)/shard_map/ppermute | solution.py:111
  47.7 1.4 %collective-permute-start.17 = (bf16[256,256]{1,0:T(8,128)(2,1)S(1)}, bf16[256,256]{1,0:T(8,128)(2,1)S(1)}, u32[]{:S(2)}, u32[]{:S(2)}) collective-permute-start(bf16[256,256]{1,0:T(8,128)(2,1)S(1)} %slice.69), channel_id=1, source_target_pairs={{0,1},{1,0},{2,3},{3,2},{4,5},{5,4},{6,7},{7,6},{8,9},{9,8},{10,11... | collective-permute-start | bytes 393224 | tf_op jit(solution)/shard_map/ppermute | solution.py:111
  49.2 6.1 %collective-permute-start.22 = (bf16[128,256]{1,0:T(8,128)(2,1)S(1)}, bf16[128,256]{1,0:T(8,128)(2,1)S(1)}, u32[]{:S(2)}, u32[]{:S(2)}) collective-permute-start(bf16[128,256]{1,0:T(8,128)(2,1)S(1)} %get-tuple-element.7), channel_id=1, source_target_pairs={{0,16},{1,17},{2,18},{3,19},{4,20},{5,21},{6,22},{7,23},{8,24},{9,... | collective-permute-start | bytes 196616 | tf_op jit(solution)/shard_map/ppermute | solution.py:111
  49.9 8.3 %collective-permute-start.23 = (bf16[128,256]{1,0:T(8,128)(2,1)S(1)}, bf16[128,256]{1,0:T(8,128)(2,1)S(1)}, u32[]{:S(2)}, u32[]{:S(2)}) collective-permute-start(bf16[128,256]{1,0:T(8,128)(2,1)S(1)} %get-tuple-element.8), channel_id=1, source_target_pairs={{0,18},{1,19},{2,16},{3,17},{4,22},{5,23},{6,20},{7,21},{8,26},{9,... | collective-permute-start | bytes 196616 | tf_op jit(solution)/shard_map/ppermute | solution.py:111
  51.9 10.1 %collective-permute-start.18 = (bf16[128,256]{1,0:T(8,128)(2,1)S(1)}, bf16[128,256]{1,0:T(8,128)(2,1)S(1)}, u32[]{:S(2)}, u32[]{:S(2)}) collective-permute-start(bf16[128,256]{1,0:T(8,128)(2,1)S(1)} %get-tuple-element.8), channel_id=1, source_target_pairs={{0,2},{1,3},{2,0},{3,1},{4,6},{5,7},{6,4},{7,5},{8,10},{9,11},{10,... | collective-permute-start | bytes 196616 | tf_op jit(solution)/shard_map/ppermute | solution.py:111
  58.4 5.9 %collective-permute-start.26 = (bf16[128,256]{1,0:T(8,128)(2,1)S(1)}, bf16[128,256]{1,0:T(8,128)(2,1)S(1)}, u32[]{:S(2)}, u32[]{:S(2)}) collective-permute-start(bf16[128,256]{1,0:T(8,128)(2,1)S(1)} %fusion.6.refs_4_), channel_id=1, source_target_pairs={{0,12},{1,13},{2,14},{3,15},{4,8},{5,9},{6,10},{7,11},{8,4},{9,5},... | collective-permute-start | bytes 196616 | tf_op jit(solution)/shard_map/ppermute | solution.py:111
  58.5 7.2 %collective-permute-start.25 = (bf16[128,256]{1,0:T(8,128)(2,1)S(1)}, bf16[128,256]{1,0:T(8,128)(2,1)S(1)}, u32[]{:S(2)}, u32[]{:S(2)}) collective-permute-start(bf16[128,256]{1,0:T(8,128)(2,1)S(1)} %fusion.6.refs_4_), channel_id=1, source_target_pairs={{0,8},{1,9},{2,10},{3,11},{4,12},{5,13},{6,14},{7,15},{8,0},{9,1},... | collective-permute-start | bytes 196616 | tf_op jit(solution)/shard_map/ppermute | solution.py:111
  60.6 5.1 %collective-permute-start.24 = (bf16[128,256]{1,0:T(8,128)(2,1)S(1)}, bf16[128,256]{1,0:T(8,128)(2,1)S(1)}, u32[]{:S(2)}, u32[]{:S(2)}) collective-permute-start(bf16[128,256]{1,0:T(8,128)(2,1)S(1)} %fusion.6.refs_4_), channel_id=1, source_target_pairs={{0,4},{1,5},{2,6},{3,7},{4,0},{5,1},{6,2},{7,3},{8,12},{9,13},{10,... | collective-permute-start | bytes 196616 | tf_op jit(solution)/shard_map/ppermute | solution.py:111
  62.1 5.2 %collective-permute-start.21 = (bf16[128,256]{1,0:T(8,128)(2,1)S(1)}, bf16[128,256]{1,0:T(8,128)(2,1)S(1)}, u32[]{:S(2)}, u32[]{:S(2)}) collective-permute-start(bf16[128,256]{1,0:T(8,128)(2,1)S(1)} %fusion.7.refs_0_), channel_id=1, source_target_pairs={{0,12},{1,13},{2,14},{3,15},{4,8},{5,9},{6,10},{7,11},{8,4},{9,5},... | collective-permute-start | bytes 196616 | tf_op jit(solution)/shard_map/ppermute | solution.py:111
  62.3 5.1 %collective-permute-start.20 = (bf16[128,256]{1,0:T(8,128)(2,1)S(1)}, bf16[128,256]{1,0:T(8,128)(2,1)S(1)}, u32[]{:S(2)}, u32[]{:S(2)}) collective-permute-start(bf16[128,256]{1,0:T(8,128)(2,1)S(1)} %fusion.7.refs_0_), channel_id=1, source_target_pairs={{0,8},{1,9},{2,10},{3,11},{4,12},{5,13},{6,14},{7,15},{8,0},{9,1},... | collective-permute-start | bytes 196616 | tf_op jit(solution)/shard_map/ppermute | solution.py:111
  64.3 4.3 %collective-permute-start.19 = (bf16[128,256]{1,0:T(8,128)(2,1)S(1)}, bf16[128,256]{1,0:T(8,128)(2,1)S(1)}, u32[]{:S(2)}, u32[]{:S(2)}) collective-permute-start(bf16[128,256]{1,0:T(8,128)(2,1)S(1)} %fusion.7.refs_0_), channel_id=1, source_target_pairs={{0,4},{1,5},{2,6},{3,7},{4,0},{5,1},{6,2},{7,3},{8,12},{9,13},{10,... | collective-permute-start | bytes 196616 | tf_op jit(solution)/shard_map/ppermute | solution.py:111
  69.3 1.4 %collective-permute-start.27 = (bf16[256,256]{1,0:T(8,128)(2,1)S(1)}, bf16[256,256]{1,0:T(8,128)(2,1)S(1)}, u32[]{:S(2)}, u32[]{:S(2)}) collective-permute-start(bf16[256,256]{1,0:T(8,128)(2,1)S(1)} %slice.73), channel_id=1, source_target_pairs={{0,1},{1,0},{2,3},{3,2},{4,5},{5,4},{6,7},{7,6},{8,9},{9,8},{10,11... | collective-permute-start | bytes 393224 | tf_op jit(solution)/shard_map/ppermute | solution.py:111
  70.8 4.3 %collective-permute-start.28 = (bf16[128,256]{1,0:T(8,128)(2,1)S(1)}, bf16[128,256]{1,0:T(8,128)(2,1)S(1)}, u32[]{:S(2)}, u32[]{:S(2)}) collective-permute-start(bf16[128,256]{1,0:T(8,128)(2,1)S(1)} %slice.75), channel_id=1, source_target_pairs={{0,2},{1,3},{2,0},{3,1},{4,6},{5,7},{6,4},{7,5},{8,10},{9,11},{10,... | collective-permute-start | bytes 196616 | tf_op jit(solution)/shard_map/ppermute | solution.py:111

commit v2 on v1

v2 whole, which is shorter than its diff:
```python
import functools

import jax
import jax.numpy as jnp
from jax import lax
from jax.experimental import pallas as pl
from jax.experimental.pallas import tpu as pltpu
from jax.sharding import PartitionSpec as P

STEPS = 3
ROW_TILES = 4
CHUNK = 16
BOTH = ("src", "tgt")


def densify_kernel(target_ref, source_ref, count_ref, tiles_ref, out_ref, held_ref, total_ref, sems):
    group = pl.program_id(0)
    row_tiles, col_tiles, edge, _ = total_ref.shape
    slots = held_ref.shape[0]
    n_rows = pl.num_programs(0) * row_tiles
    s, t = lax.axis_index("src"), lax.axis_index("tgt")
    count = count_ref[0, 0]

    def copy(c):
        part = pl.ds(c * CHUNK, CHUNK)
        return pltpu.make_async_copy(tiles_ref.at[0, 0, part], held_ref.at[part], sems.at[c])

    for c in range(slots // CHUNK):
        pl.when((group == 0) & (c * CHUNK < count))(lambda c=c: copy(c).start())
    total_ref[...] = jnp.zeros_like(total_ref)

    def absorb(slot, carry):
        relative = target_ref[0, 0, slot] ^ t
        row = sum(jnp.where((relative & b) != 0, n_tgt // (2 * b), 0) for b in bits_of(n_tgt)) - group * row_tiles

        @pl.when((row >= 0) & (row < row_tiles))
        def _():
            col = source_ref[0, 0, slot] ^ s
            total_ref[row, col] += held_ref[slot].astype(jnp.float32)

        return carry

    n_tgt = lax.axis_size("tgt")
    for c in range(slots // CHUNK):
        pl.when((group == 0) & (c * CHUNK < count))(lambda c=c: copy(c).wait())
        lax.fori_loop(c * CHUNK, jnp.minimum(count, (c + 1) * CHUNK), absorb, 0)
    for i in range(row_tiles):
        for j in range(col_tiles):
            out_ref[i * edge:(i + 1) * edge, j * edge:(j + 1) * edge] = total_ref[i, j].astype(out_ref.dtype)


def densify(target, source, count, tiles, n_rows, n_cols):
    slots, edge = tiles.shape[2:4]
    assert slots % CHUNK == 0
    row_tiles = min(ROW_TILES, n_rows)
    scalars = pl.BlockSpec(memory_space=pltpu.SMEM)
    return pl.pallas_call(
        densify_kernel,
        out_shape=jax.ShapeDtypeStruct((n_rows * edge, n_cols * edge), jnp.bfloat16),
        grid=(n_rows // row_tiles,),
        in_specs=[scalars, scalars, scalars, pl.BlockSpec(memory_space=pltpu.HBM)],
        out_specs=pl.BlockSpec((row_tiles * edge, n_cols * edge), lambda g: (g, 0)),
        scratch_shapes=[
            pltpu.VMEM((slots, edge, edge), jnp.bfloat16),
            pltpu.VMEM((row_tiles, n_cols, edge, edge), jnp.float32),
            pltpu.SemaphoreType.DMA((slots // CHUNK,)),
        ],
        compiler_params=pltpu.CompilerParams(vmem_limit_bytes=52 * 2**20),
        cost_estimate=pl.CostEstimate(flops=slots * edge * edge, bytes_accessed=2 * slots * edge * edge, transcendentals=0),
        name="densify",
    )(target, source, count, tiles)


def product_kernel(columns, weights_ref, *refs):
    *parts, out_ref = refs
    total = None
    for group, ref in zip(columns, parts):
        for i, at in enumerate(group):
            block = ref[i * 128:(i + 1) * 128]
            term = jnp.dot(weights_ref[:, at * 128:(at + 1) * 128], block, preferred_element_type=jnp.float32)
            total = term if total is None else total + term
    out_ref[...] = total.astype(out_ref.dtype)


def product(weights, parts, columns):
    n_rows, n_cols = weights.shape
    topics = parts[0].shape[1]
    rows = min(n_rows, ROW_TILES * 128)
    return pl.pallas_call(
        functools.partial(product_kernel, columns),
        out_shape=jax.ShapeDtypeStruct((n_rows, topics), jnp.bfloat16),
        grid=(n_rows // rows,),
        in_specs=[pl.BlockSpec((rows, n_cols), lambda g: (g, 0))]
        + [pl.BlockSpec(p.shape, lambda g: (0, 0)) for p in parts],
        out_specs=pl.BlockSpec((rows, topics), lambda g: (g, 0)),
        compiler_params=pltpu.CompilerParams(vmem_limit_bytes=32 * 2**20),
        cost_estimate=pl.CostEstimate(flops=2 * n_rows * n_cols * topics, bytes_accessed=2 * n_rows * n_cols, transcendentals=0),
        name="product",
    )(weights, *parts)


def bits_of(n):
    assert n & (n - 1) == 0
    return [1 << i for i in range(n.bit_length() - 1)]


def shards(initial, stubborn, coupling, tile_values, tile_target, tile_source, tile_count):
    own_rows, topics = initial.shape
    n_src, n_tgt = lax.axis_size("src"), lax.axis_size("tgt")
    assert own_rows == tile_values.shape[-1]
    tgt_bits, src_bits = bits_of(n_tgt), bits_of(n_src)
    top, low = src_bits[-1], src_bits[:-1]

    def swap(value, src_mask, tgt_mask):
        mask = src_mask * n_tgt + tgt_mask
        return lax.ppermute(value, BOTH, [(d, d ^ mask) for d in range(n_src * n_tgt)])

    def spread(blocks):
        held = dict(blocks)
        for pair in [low[i:i + 2] for i in range(0, len(low), 2)]:
            masks = pair if len(pair) == 1 else (pair[0], pair[1], pair[0] | pair[1])
            held.update({tuple(k | m for k in ks): swap(value, m, 0) for ks, value in held.items() for m in masks})
        return held

    def gather(near):
        far = swap(near, top, 0)
        return spread({(0,): near}) | spread({(top,): far})

    weights = densify(tile_target, tile_source, tile_count, tile_values, n_tgt, n_src)
    openness = ((256.0 - stubborn.astype(jnp.float32)) / 256.0)[:, None]
    base = (1.0 - openness) * initial.astype(jnp.float32)

    def add(a, b):
        return (a.astype(jnp.float32) + b.astype(jnp.float32)).astype(jnp.bfloat16)

    opinion = initial
    for step in range(STEPS):
        held = gather(opinion)
        terms = product(weights, list(held.values()), list(held))
        for bit in tgt_bits:
            half = terms.shape[0] // 2
            terms = add(terms[:half], swap(terms[half:], 0, bit))
        coupled = jnp.dot(terms, coupling, preferred_element_type=jnp.float32)
        opinion = (openness * coupled + base).astype(jnp.bfloat16)
    return opinion


def solution(mesh):
    in_specs = (
        P(("src", "tgt"), None),
        P(("src", "tgt")),
        P(),
        P("src", "tgt", None, None, None),
        P("src", "tgt", None),
        P("src", "tgt", None),
        P("src", "tgt"),
    )
    out_specs = P(("src", "tgt"), None)
    return jax.shard_map(shards, mesh=mesh, in_specs=in_specs, out_specs=out_specs, check_vma=False)
```

time: 76.2 us -> 62.8 us (0.82)
  waiting for transfers between devices: 27.6 us -> 19.8 us
  other arithmetic: 3.09 us -> 0.11 us
  starting transfers between devices: 35.8 us -> 34.1 us
  local copies, waits for them, and re-layouts: 2.49 us -> 1.41 us
    ppermute x29 -> x27, waiting for transfers between devices: 27.6 us -> 19.8 us  [swap(): lax.ppermute(value, BOTH, [(d, d ^ mask) for d in range(n_src * n_tgt)])]
    ppermute x29 -> x27, starting transfers between devices: 35.8 us -> 34.1 us  [swap(): lax.ppermute(value, BOTH, [(d, d ^ mask) for d in range(n_src * n_tgt)])]
    unnamed x6 -> x10, local copies, waits for them, and re-layouts: 2.34 us -> 1.36 us
    concatenate x1 -> x0, other arithmetic: 0.85 us -> none  [shards(): jnp.concatenate([initial, jnp.broadcast_to(openness.astype(jnp.bfloat16),...]
    convert_element_type x2 -> x0, other arithmetic: 0.77 us -> none  [update(): part = packed[:, topics:topics + 1].astype(jnp.float32)]
  transfers between devices with their start and end apart: 29 -> 27, of which waited for: 15 -> 16; matrix products, arithmetic and copies ran while one was open for 5% -> 0% of each run, Pallas kernels for 3% -> 4%
where the time goes in v2:
time: 62.8 us; the launch traced here: 62.1 us
  starting transfers between devices  34.1 us (54%)
  waiting for transfers between devices  19.8 us (32%)
  Pallas kernels  4.61 us (7%)
  local copies, waits for them, and re-layouts  1.41 us (2%)
  matrix products  1.15 us (2%)
  between operations  0.85 us (1%)
    ppermute x27, starting transfers between devices, swap(): lax.ppermute(value, BOTH, [(d, d ^ mask) for d in range(n_src * n_tgt)])  34.1 us
    ppermute x27, waiting for transfers between devices, swap(): lax.ppermute(value, BOTH, [(d, d ^ mask) for d in range(n_src * n_tgt)])  19.8 us
    pallas_call x1, Pallas kernels, densify(): pl.pallas_call(densify_kernel, out_shape=jax.ShapeDtypeStruct((n_rows * e...  2.54 us
    pallas_call x3, Pallas kernels, product(): pl.pallas_call(functools.partial(product_kernel, columns), out_shape=jax....  2.08 us
    unnamed x10, local copies, waits for them, and re-layouts  1.36 us
  transfers between devices with their start and end apart: 27, of which 16 were waited for; matrix products, arithmetic and copies ran while one was open for 0% of the time, Pallas kernels for 4%

profile of v2, /device:TPU:0, one launch (start us, length us, event | category | flops | bytes accessed | tf_op | source)
XLA Modules:
  0.0 62.1 jit_solution(3502964298989870611)
XLA Ops:
  0.0 4.0 %collective-permute-start.3 = (bf16[128,256]{1,0:T(8,128)(2,1)}, bf16[128,256]{1,0:T(8,128)(2,1)S(1)}, u32[]{:S(2)}, u32[]{:S(2)}) collective-permute-start(bf16[128,256]{1,0:T(8,128)(2,1)} %refs_0_.1), channel_id=1, source_target_pairs={{0,16},{1,17},{2,18},{3,19},{4,20},{5,21},{6,22},{7,23},{8,24},{9,... | collective-permute-start | bytes 196616 | tf_op jit(solution)/shard_map/ppermute | solution.py:116
  4.0 2.5 %collective-permute-start.2 = (bf16[128,256]{1,0:T(8,128)(2,1)}, bf16[128,256]{1,0:T(8,128)(2,1)S(1)}, u32[]{:S(2)}, u32[]{:S(2)}) collective-permute-start(bf16[128,256]{1,0:T(8,128)(2,1)} %refs_0_.1), channel_id=1, source_target_pairs={{0,12},{1,13},{2,14},{3,15},{4,8},{5,9},{6,10},{7,11},{8,4},{9,5},... | collective-permute-start | bytes 196616 | tf_op jit(solution)/shard_map/ppermute | solution.py:116
  6.5 0.4 collective-permute-start.1
  7.0 0.5 collective-permute-start
  7.5 2.5 %collective-permute-start.6 = (bf16[128,256]{1,0:T(8,128)(2,1)S(1)}, bf16[128,256]{1,0:T(8,128)(2,1)S(1)}, u32[]{:S(2)}, u32[]{:S(2)}) collective-permute-start(bf16[128,256]{1,0:T(8,128)(2,1)S(1)} %collective-permute-done.3.refs_4_), channel_id=1, source_target_pairs={{0,12},{1,13},{2,14},{3,15},{4,8},{5,9},{6,10},{7,11},{8,4},{9,5},... | collective-permute-start | bytes 196616 | tf_op jit(solution)/shard_map/ppermute | solution.py:116
  10.0 0.6 collective-permute-start.5
  10.6 1.1 %collective-permute-start.4 = (bf16[128,256]{1,0:T(8,128)(2,1)S(1)}, bf16[128,256]{1,0:T(8,128)(2,1)S(1)}, u32[]{:S(2)}, u32[]{:S(2)}) collective-permute-start(bf16[128,256]{1,0:T(8,128)(2,1)S(1)} %collective-permute-done.3.refs_4_), channel_id=1, source_target_pairs={{0,4},{1,5},{2,6},{3,7},{4,0},{5,1},{6,2},{7,3},{8,12},{9,13},{10,... | collective-permute-start | bytes 196616 | tf_op jit(solution)/shard_map/ppermute | solution.py:116
  12.4 0.7 %copy-done.2 = s32[1,1,144]{2,1,0:T(1,128)S(1)} copy-done((s32[1,1,144]{2,1,0:T(1,128)S(1)}, s32[1,1,144]{2,1,0:T(1,128)}, u32[]{:S(2)}) %copy-start.2) | copy-done | bytes 600
  13.0 0.7 %copy-done.3 = s32[1,1,144]{2,1,0:T(1,128)S(1)} copy-done((s32[1,1,144]{2,1,0:T(1,128)S(1)}, s32[1,1,144]{2,1,0:T(1,128)}, u32[]{:S(2)}) %copy-start.3) | copy-done | bytes 600
  13.7 2.5 %densify.1.weights_ref = bf16[512,1024]{1,0:T(8,128)(2,1)S(1)} custom-call(s32[1,1,144]{2,1,0:T(1,128)S(1)} %copy-done.2, s32[1,1,144]{2,1,0:T(1,128)S(1)} %copy-done.3, s32[1,1]{1,0:T(1,128)S(6)} %copy.8.count_ref, bf16[1,1,144,128,128]{4,3,2,1,0:T(8,128)(2,1)} %tiles_ref.1), custom_call_target="tpu_custom_call" | custom-call | flops 2359296 | bytes 4718592 | tf_op jit(solution)/shard_map/densify/pallas_call | solution.py:57
  16.3 0.7 %product.3 = bf16[512,256]{1,0:T(8,128)(2,1)S(1)} custom-call(bf16[512,1024]{1,0:T(8,128)(2,1)S(1)} %densify.1.weights_ref, bf16[128,256]{1,0:T(8,128)(2,1)S(1)} %copy-done.1, bf16[128,256]{1,0:T(8,128)(2,1)S(1)} %collective-permute-done.refs_1_, bf16[128,256]{1,0:T(8,128)(2,1)S(1)} %collective-permute-done.1.refs_2_, ...), custom_call_target="tpu_custom_call" | custom-call | flops 268435456 | bytes 1048576 | tf_op jit(solution)/shard_map/product/pallas_call | solution.py:89
  17.1 1.3 %collective-permute-done.7 = bf16[256,256]{1,0:T(8,128)(2,1)S(1)} collective-permute-done((bf16[256,256]{1,0:T(8,128)(2,1)S(1)}, bf16[256,256]{1,0:T(8,128)(2,1)S(1)}, u32[]{:S(2)}, u32[]{:S(2)}) %collective-permute-start.7) | collective-permute-done | bytes 131104 | tf_op jit(solution)/shard_map/ppermute | solution.py:116
  18.5 1.6 %collective-permute-start.8 = (bf16[128,256]{1,0:T(8,128)(2,1)S(1)}, bf16[128,256]{1,0:T(8,128)(2,1)S(1)}, u32[]{:S(2)}, u32[]{:S(2)}) collective-permute-start(bf16[128,256]{1,0:T(8,128)(2,1)S(1)} %slice.51), channel_id=1, source_target_pairs={{0,2},{1,3},{2,0},{3,1},{4,6},{5,7},{6,4},{7,5},{8,10},{9,11},{10,... | collective-permute-start | bytes 196616 | tf_op jit(solution)/shard_map/ppermute | solution.py:116
  20.1 2.8 %collective-permute-done.8 = bf16[128,256]{1,0:T(8,128)(2,1)S(1)} collective-permute-done((bf16[128,256]{1,0:T(8,128)(2,1)S(1)}, bf16[128,256]{1,0:T(8,128)(2,1)S(1)}, u32[]{:S(2)}, u32[]{:S(2)}) %collective-permute-start.8) | collective-permute-done | bytes 65568 | tf_op jit(solution)/shard_map/ppermute | solution.py:116
  22.8 0.2 fusion.5.refs_0_
  23.0 1.9 %collective-permute-start.12 = (bf16[128,256]{1,0:T(8,128)(2,1)S(1)}, bf16[128,256]{1,0:T(8,128)(2,1)S(1)}, u32[]{:S(2)}, u32[]{:S(2)}) collective-permute-start(bf16[128,256]{1,0:T(8,128)(2,1)S(1)} %fusion.5.refs_0_), channel_id=1, source_target_pairs={{0,16},{1,17},{2,18},{3,19},{4,20},{5,21},{6,22},{7,23},{8,24},{9,... | collective-permute-start | bytes 196616 | tf_op jit(solution)/shard_map/ppermute | solution.py:116
  24.9 2.9 %collective-permute-start.11 = (bf16[128,256]{1,0:T(8,128)(2,1)S(1)}, bf16[128,256]{1,0:T(8,128)(2,1)S(1)}, u32[]{:S(2)}, u32[]{:S(2)}) collective-permute-start(bf16[128,256]{1,0:T(8,128)(2,1)S(1)} %fusion.5.refs_0_), channel_id=1, source_target_pairs={{0,12},{1,13},{2,14},{3,15},{4,8},{5,9},{6,10},{7,11},{8,4},{9,5},... | collective-permute-start | bytes 196616 | tf_op jit(solution)/shard_map/ppermute | solution.py:116
  27.8 0.3 collective-permute-start.10
  28.1 0.3 collective-permute-start.9
  28.4 0.5 collective-permute-done.12.refs_4_
  28.9 2.4 %collective-permute-start.15 = (bf16[128,256]{1,0:T(8,128)(2,1)S(1)}, bf16[128,256]{1,0:T(8,128)(2,1)S(1)}, u32[]{:S(2)}, u32[]{:S(2)}) collective-permute-start(bf16[128,256]{1,0:T(8,128)(2,1)S(1)} %collective-permute-done.12.refs_4_), channel_id=1, source_target_pairs={{0,12},{1,13},{2,14},{3,15},{4,8},{5,9},{6,10},{7,11},{8,4},{9,5},... | collective-permute-start | bytes 196616 | tf_op jit(solution)/shard_map/ppermute | solution.py:116
  31.3 0.3 collective-permute-start.14
  31.5 0.8 %collective-permute-start.13 = (bf16[128,256]{1,0:T(8,128)(2,1)S(1)}, bf16[128,256]{1,0:T(8,128)(2,1)S(1)}, u32[]{:S(2)}, u32[]{:S(2)}) collective-permute-start(bf16[128,256]{1,0:T(8,128)(2,1)S(1)} %collective-permute-done.12.refs_4_), channel_id=1, source_target_pairs={{0,4},{1,5},{2,6},{3,7},{4,0},{5,1},{6,2},{7,3},{8,12},{9,13},{10,... | collective-permute-start | bytes 196616 | tf_op jit(solution)/shard_map/ppermute | solution.py:116
  32.4 0.3 collective-permute-done.10.refs_2_
  32.6 0.3 collective-permute-done.9.refs_1_
  32.9 1.1 %collective-permute-done.15.refs_7_ = bf16[128,256]{1,0:T(8,128)(2,1)S(1)} collective-permute-done((bf16[128,256]{1,0:T(8,128)(2,1)S(1)}, bf16[128,256]{1,0:T(8,128)(2,1)S(1)}, u32[]{:S(2)}, u32[]{:S(2)}) %collective-permute-start.15) | collective-permute-done | bytes 65568 | tf_op jit(solution)/shard_map/ppermute | solution.py:116
  34.0 1.5 %collective-permute-done.14.refs_6_ = bf16[128,256]{1,0:T(8,128)(2,1)S(1)} collective-permute-done((bf16[128,256]{1,0:T(8,128)(2,1)S(1)}, bf16[128,256]{1,0:T(8,128)(2,1)S(1)}, u32[]{:S(2)}, u32[]{:S(2)}) %collective-permute-start.14) | collective-permute-done | bytes 65568 | tf_op jit(solution)/shard_map/ppermute | solution.py:116
  35.6 0.3 collective-permute-done.13.refs_5_
  35.8 0.7 %product.4 = bf16[512,256]{1,0:T(8,128)(2,1)S(1)} custom-call(bf16[512,1024]{1,0:T(8,128)(2,1)S(1)} %densify.1.weights_ref, bf16[128,256]{1,0:T(8,128)(2,1)S(1)} %fusion.5.refs_0_, bf16[128,256]{1,0:T(8,128)(2,1)S(1)} %collective-permute-done.9.refs_1_, bf16[128,256]{1,0:T(8,128)(2,1)S(1)} %collective-permute-done.10.refs_2_, ...), custom_call_target="tpu_custom_call" | custom-call | flops 268435456 | bytes 1048576 | tf_op jit(solution)/shard_map/product/pallas_call | solution.py:89
  36.6 1.3 %collective-permute-done.16 = bf16[256,256]{1,0:T(8,128)(2,1)S(1)} collective-permute-done((bf16[256,256]{1,0:T(8,128)(2,1)S(1)}, bf16[256,256]{1,0:T(8,128)(2,1)S(1)}, u32[]{:S(2)}, u32[]{:S(2)}) %collective-permute-start.16) | collective-permute-done | bytes 131104 | tf_op jit(solution)/shard_map/ppermute | solution.py:116
  38.0 1.3 %collective-permute-start.17 = (bf16[128,256]{1,0:T(8,128)(2,1)S(1)}, bf16[128,256]{1,0:T(8,128)(2,1)S(1)}, u32[]{:S(2)}, u32[]{:S(2)}) collective-permute-start(bf16[128,256]{1,0:T(8,128)(2,1)S(1)} %slice.55), channel_id=1, source_target_pairs={{0,2},{1,3},{2,0},{3,1},{4,6},{5,7},{6,4},{7,5},{8,10},{9,11},{10,... | collective-permute-start | bytes 196616 | tf_op jit(solution)/shard_map/ppermute | solution.py:116
  39.3 3.0 %collective-permute-done.17 = bf16[128,256]{1,0:T(8,128)(2,1)S(1)} collective-permute-done((bf16[128,256]{1,0:T(8,128)(2,1)S(1)}, bf16[128,256]{1,0:T(8,128)(2,1)S(1)}, u32[]{:S(2)}, u32[]{:S(2)}) %collective-permute-start.17) | collective-permute-done | bytes 65568 | tf_op jit(solution)/shard_map/ppermute | solution.py:116
  42.3 0.2 fusion.4.refs_0_
  42.5 2.4 %collective-permute-start.21 = (bf16[128,256]{1,0:T(8,128)(2,1)S(1)}, bf16[128,256]{1,0:T(8,128)(2,1)S(1)}, u32[]{:S(2)}, u32[]{:S(2)}) collective-permute-start(bf16[128,256]{1,0:T(8,128)(2,1)S(1)} %fusion.4.refs_0_), channel_id=1, source_target_pairs={{0,16},{1,17},{2,18},{3,19},{4,20},{5,21},{6,22},{7,23},{8,24},{9,... | collective-permute-start | bytes 196616 | tf_op jit(solution)/shard_map/ppermute | solution.py:116
  44.9 1.4 %collective-permute-start.20 = (bf16[128,256]{1,0:T(8,128)(2,1)S(1)}, bf16[128,256]{1,0:T(8,128)(2,1)S(1)}, u32[]{:S(2)}, u32[]{:S(2)}) collective-permute-start(bf16[128,256]{1,0:T(8,128)(2,1)S(1)} %fusion.4.refs_0_), channel_id=1, source_target_pairs={{0,12},{1,13},{2,14},{3,15},{4,8},{5,9},{6,10},{7,11},{8,4},{9,5},... | collective-permute-start | bytes 196616 | tf_op jit(solution)/shard_map/ppermute | solution.py:116
  46.3 0.4 collective-permute-start.19
  46.6 1.7 %collective-permute-start.18 = (bf16[128,256]{1,0:T(8,128)(2,1)S(1)}, bf16[128,256]{1,0:T(8,128)(2,1)S(1)}, u32[]{:S(2)}, u32[]{:S(2)}) collective-permute-start(bf16[128,256]{1,0:T(8,128)(2,1)S(1)} %fusion.4.refs_0_), channel_id=1, source_target_pairs={{0,4},{1,5},{2,6},{3,7},{4,0},{5,1},{6,2},{7,3},{8,12},{9,13},{10,... | collective-permute-start | bytes 196616 | tf_op jit(solution)/shard_map/ppermute | solution.py:116
  48.4 1.6 %collective-permute-start.24 = (bf16[128,256]{1,0:T(8,128)(2,1)S(1)}, bf16[128,256]{1,0:T(8,128)(2,1)S(1)}, u32[]{:S(2)}, u32[]{:S(2)}) collective-permute-start(bf16[128,256]{1,0:T(8,128)(2,1)S(1)} %collective-permute-done.21.refs_4_), channel_id=1, source_target_pairs={{0,12},{1,13},{2,14},{3,15},{4,8},{5,9},{6,10},{7,11},{8,4},{9,5},... | collective-permute-start | bytes 196616 | tf_op jit(solution)/shard_map/ppermute | solution.py:116
  50.1 0.3 collective-permute-done.20.refs_3_
  50.5 1.4 %collective-permute-start.22 = (bf16[128,256]{1,0:T(8,128)(2,1)S(1)}, bf16[128,256]{1,0:T(8,128)(2,1)S(1)}, u32[]{:S(2)}, u32[]{:S(2)}) collective-permute-start(bf16[128,256]{1,0:T(8,128)(2,1)S(1)} %collective-permute-done.21.refs_4_), channel_id=1, source_target_pairs={{0,4},{1,5},{2,6},{3,7},{4,0},{5,1},{6,2},{7,3},{8,12},{9,13},{10,... | collective-permute-start | bytes 196616 | tf_op jit(solution)/shard_map/ppermute | solution.py:116
  51.9 1.7 %collective-permute-done.24.refs_7_ = bf16[128,256]{1,0:T(8,128)(2,1)S(1)} collective-permute-done((bf16[128,256]{1,0:T(8,128)(2,1)S(1)}, bf16[128,256]{1,0:T(8,128)(2,1)S(1)}, u32[]{:S(2)}, u32[]{:S(2)}) %collective-permute-start.24) | collective-permute-done | bytes 65568 | tf_op jit(solution)/shard_map/ppermute | solution.py:116
  53.6 0.7 %collective-permute-done.23.refs_6_ = bf16[128,256]{1,0:T(8,128)(2,1)S(1)} collective-permute-done((bf16[128,256]{1,0:T(8,128)(2,1)S(1)}, bf16[128,256]{1,0:T(8,128)(2,1)S(1)}, u32[]{:S(2)}, u32[]{:S(2)}) %collective-permute-start.23) | collective-permute-done | bytes 65568 | tf_op jit(solution)/shard_map/ppermute | solution.py:116
  54.3 0.5 collective-permute-done.22.refs_5_
  54.7 0.7 %product.5 = bf16[512,256]{1,0:T(8,128)(2,1)S(1)} custom-call(bf16[512,1024]{1,0:T(8,128)(2,1)S(1)} %densify.1.weights_ref, bf16[128,256]{1,0:T(8,128)(2,1)S(1)} %fusion.4.refs_0_, bf16[128,256]{1,0:T(8,128)(2,1)S(1)} %collective-permute-done.18.refs_1_, bf16[128,256]{1,0:T(8,128)(2,1)S(1)} %collective-permute-done.19.refs_2_, ...), custom_call_target="tpu_custom_call" | custom-call | flops 268435456 | bytes 1048576 | tf_op jit(solution)/shard_map/product/pallas_call | solution.py:89
  55.5 1.3 %collective-permute-done.25 = bf16[256,256]{1,0:T(8,128)(2,1)S(1)} collective-permute-done((bf16[256,256]{1,0:T(8,128)(2,1)S(1)}, bf16[256,256]{1,0:T(8,128)(2,1)S(1)}, u32[]{:S(2)}, u32[]{:S(2)}) %collective-permute-start.25) | collective-permute-done | bytes 131104 | tf_op jit(solution)/shard_map/ppermute | solution.py:116
  56.9 1.4 %collective-permute-start.26 = (bf16[128,256]{1,0:T(8,128)(2,1)S(1)}, bf16[128,256]{1,0:T(8,128)(2,1)S(1)}, u32[]{:S(2)}, u32[]{:S(2)}) collective-permute-start(bf16[128,256]{1,0:T(8,128)(2,1)S(1)} %slice.59), channel_id=1, source_target_pairs={{0,2},{1,3},{2,0},{3,1},{4,6},{5,7},{6,4},{7,5},{8,10},{9,11},{10,... | collective-permute-start | bytes 196616 | tf_op jit(solution)/shard_map/ppermute | solution.py:116
  58.4 2.9 %collective-permute-done.26 = bf16[128,256]{1,0:T(8,128)(2,1)S(1)} collective-permute-done((bf16[128,256]{1,0:T(8,128)(2,1)S(1)}, bf16[128,256]{1,0:T(8,128)(2,1)S(1)}, u32[]{:S(2)}, u32[]{:S(2)}) %collective-permute-start.26) | collective-permute-done | bytes 65568 | tf_op jit(solution)/shard_map/ppermute | solution.py:116
  61.2 0.8 %fusion.3 = bf16[128,256]{1,0:T(8,128)(2,1)} fusion(bf16[256,256]{1,0:T(8,128)(2,1)S(1)} %copy-done, bf16[128,256]{1,0:T(8,128)(2,1)S(1)} %copy-done.1, bf16[128,256]{1,0:T(8,128)(2,1)S(1)} %collective-permute-done.26, bf16[256,256]{1,0:T(8,128)(2,1)S(1)} %add_convert_fusion, f32[128]{0:T(128)S(1)} %get-tuple-element.6, f32[128]{0:T(128)S(1)} %get-tuple-element.5), kind=kOutput, calls=%fused_computation.6 | convolution fusion | flops 17072128 | bytes 394240 | tf_op jit(solution)/shard_map/dot_general | solution.py:143
  (33 shorter events, 0.6 us)
Async XLA Ops:
  0.0 22.8 %copy-start = (bf16[256,256]{1,0:T(8,128)(2,1)S(1)}, bf16[256,256]{1,0:T(8,128)(2,1)}, u32[]{:S(2)}) copy-start(bf16[256,256]{1,0:T(8,128)(2,1)} %param.9) | copy-start | bytes 393220
  0.0 16.3 %copy-start.1 = (bf16[128,256]{1,0:T(8,128)(2,1)S(1)}, bf16[128,256]{1,0:T(8,128)(2,1)}, u32[]{:S(2)}) copy-start(bf16[128,256]{1,0:T(8,128)(2,1)} %refs_0_.1) | copy-start | bytes 196612
  0.0 7.5 %collective-permute-start.3 = (bf16[128,256]{1,0:T(8,128)(2,1)}, bf16[128,256]{1,0:T(8,128)(2,1)S(1)}, u32[]{:S(2)}, u32[]{:S(2)}) collective-permute-start(bf16[128,256]{1,0:T(8,128)(2,1)} %refs_0_.1), channel_id=1, source_target_pairs={{0,16},{1,17},{2,18},{3,19},{4,20},{5,21},{6,22},{7,23},{8,24},{9,... | collective-permute-start | bytes 196616 | tf_op jit(solution)/shard_map/ppermute | solution.py:116
  4.0 6.6 %collective-permute-start.2 = (bf16[128,256]{1,0:T(8,128)(2,1)}, bf16[128,256]{1,0:T(8,128)(2,1)S(1)}, u32[]{:S(2)}, u32[]{:S(2)}) collective-permute-start(bf16[128,256]{1,0:T(8,128)(2,1)} %refs_0_.1), channel_id=1, source_target_pairs={{0,12},{1,13},{2,14},{3,15},{4,8},{5,9},{6,10},{7,11},{8,4},{9,5},... | collective-permute-start | bytes 196616 | tf_op jit(solution)/shard_map/ppermute | solution.py:116
  6.5 9.7 %collective-permute-start.1 = (bf16[128,256]{1,0:T(8,128)(2,1)}, bf16[128,256]{1,0:T(8,128)(2,1)S(1)}, u32[]{:S(2)}, u32[]{:S(2)}) collective-permute-start(bf16[128,256]{1,0:T(8,128)(2,1)} %refs_0_.1), channel_id=1, source_target_pairs={{0,8},{1,9},{2,10},{3,11},{4,12},{5,13},{6,14},{7,15},{8,0},{9,1},... | collective-permute-start | bytes 196616 | tf_op jit(solution)/shard_map/ppermute | solution.py:116
  7.0 9.3 %collective-permute-start = (bf16[128,256]{1,0:T(8,128)(2,1)}, bf16[128,256]{1,0:T(8,128)(2,1)S(1)}, u32[]{:S(2)}, u32[]{:S(2)}) collective-permute-start(bf16[128,256]{1,0:T(8,128)(2,1)} %refs_0_.1), channel_id=1, source_target_pairs={{0,4},{1,5},{2,6},{3,7},{4,0},{5,1},{6,2},{7,3},{8,12},{9,13},{10,... | collective-permute-start | bytes 196616 | tf_op jit(solution)/shard_map/ppermute | solution.py:116
  7.5 8.8 %collective-permute-start.6 = (bf16[128,256]{1,0:T(8,128)(2,1)S(1)}, bf16[128,256]{1,0:T(8,128)(2,1)S(1)}, u32[]{:S(2)}, u32[]{:S(2)}) collective-permute-start(bf16[128,256]{1,0:T(8,128)(2,1)S(1)} %collective-permute-done.3.refs_4_), channel_id=1, source_target_pairs={{0,12},{1,13},{2,14},{3,15},{4,8},{5,9},{6,10},{7,11},{8,4},{9,5},... | collective-permute-start | bytes 196616 | tf_op jit(solution)/shard_map/ppermute | solution.py:116
  10.0 6.3 %collective-permute-start.5 = (bf16[128,256]{1,0:T(8,128)(2,1)S(1)}, bf16[128,256]{1,0:T(8,128)(2,1)S(1)}, u32[]{:S(2)}, u32[]{:S(2)}) collective-permute-start(bf16[128,256]{1,0:T(8,128)(2,1)S(1)} %collective-permute-done.3.refs_4_), channel_id=1, source_target_pairs={{0,8},{1,9},{2,10},{3,11},{4,12},{5,13},{6,14},{7,15},{8,0},{9,1},... | collective-permute-start | bytes 196616 | tf_op jit(solution)/shard_map/ppermute | solution.py:116
  10.6 5.7 %collective-permute-start.4 = (bf16[128,256]{1,0:T(8,128)(2,1)S(1)}, bf16[128,256]{1,0:T(8,128)(2,1)S(1)}, u32[]{:S(2)}, u32[]{:S(2)}) collective-permute-start(bf16[128,256]{1,0:T(8,128)(2,1)S(1)} %collective-permute-done.3.refs_4_), channel_id=1, source_target_pairs={{0,4},{1,5},{2,6},{3,7},{4,0},{5,1},{6,2},{7,3},{8,12},{9,13},{10,... | collective-permute-start | bytes 196616 | tf_op jit(solution)/shard_map/ppermute | solution.py:116
  12.4 0.7 %copy-start.2 = (s32[1,1,144]{2,1,0:T(1,128)S(1)}, s32[1,1,144]{2,1,0:T(1,128)}, u32[]{:S(2)}) copy-start(s32[1,1,144]{2,1,0:T(1,128)} %target_ref.1) | copy-start | bytes 1732
  13.0 0.7 %copy-start.3 = (s32[1,1,144]{2,1,0:T(1,128)S(1)}, s32[1,1,144]{2,1,0:T(1,128)}, u32[]{:S(2)}) copy-start(s32[1,1,144]{2,1,0:T(1,128)} %source_ref.1) | copy-start | bytes 1732
  13.7 6.3 %copy-start.4 = (s32[128]{0:T(128)S(1)}, s32[128]{0:T(128)}, u32[]{:S(2)}) copy-start(s32[128]{0:T(128)} %param.8) | copy-start | bytes 1540
  17.0 1.4 %collective-permute-start.7 = (bf16[256,256]{1,0:T(8,128)(2,1)S(1)}, bf16[256,256]{1,0:T(8,128)(2,1)S(1)}, u32[]{:S(2)}, u32[]{:S(2)}) collective-permute-start(bf16[256,256]{1,0:T(8,128)(2,1)S(1)} %slice.49), channel_id=1, source_target_pairs={{0,1},{1,0},{2,3},{3,2},{4,5},{5,4},{6,7},{7,6},{8,9},{9,8},{10,11... | collective-permute-start | bytes 393224 | tf_op jit(solution)/shard_map/ppermute | solution.py:116
  18.5 4.3 %collective-permute-start.8 = (bf16[128,256]{1,0:T(8,128)(2,1)S(1)}, bf16[128,256]{1,0:T(8,128)(2,1)S(1)}, u32[]{:S(2)}, u32[]{:S(2)}) collective-permute-start(bf16[128,256]{1,0:T(8,128)(2,1)S(1)} %slice.51), channel_id=1, source_target_pairs={{0,2},{1,3},{2,0},{3,1},{4,6},{5,7},{6,4},{7,5},{8,10},{9,11},{10,... | collective-permute-start | bytes 196616 | tf_op jit(solution)/shard_map/ppermute | solution.py:116
  23.0 5.8 %collective-permute-start.12 = (bf16[128,256]{1,0:T(8,128)(2,1)S(1)}, bf16[128,256]{1,0:T(8,128)(2,1)S(1)}, u32[]{:S(2)}, u32[]{:S(2)}) collective-permute-start(bf16[128,256]{1,0:T(8,128)(2,1)S(1)} %fusion.5.refs_0_), channel_id=1, source_target_pairs={{0,16},{1,17},{2,18},{3,19},{4,20},{5,21},{6,22},{7,23},{8,24},{9,... | collective-permute-start | bytes 196616 | tf_op jit(solution)/shard_map/ppermute | solution.py:116
  24.9 6.6 %collective-permute-start.11 = (bf16[128,256]{1,0:T(8,128)(2,1)S(1)}, bf16[128,256]{1,0:T(8,128)(2,1)S(1)}, u32[]{:S(2)}, u32[]{:S(2)}) collective-permute-start(bf16[128,256]{1,0:T(8,128)(2,1)S(1)} %fusion.5.refs_0_), channel_id=1, source_target_pairs={{0,12},{1,13},{2,14},{3,15},{4,8},{5,9},{6,10},{7,11},{8,4},{9,5},... | collective-permute-start | bytes 196616 | tf_op jit(solution)/shard_map/ppermute | solution.py:116
  27.8 4.8 %collective-permute-start.10 = (bf16[128,256]{1,0:T(8,128)(2,1)S(1)}, bf16[128,256]{1,0:T(8,128)(2,1)S(1)}, u32[]{:S(2)}, u32[]{:S(2)}) collective-permute-start(bf16[128,256]{1,0:T(8,128)(2,1)S(1)} %fusion.5.refs_0_), channel_id=1, source_target_pairs={{0,8},{1,9},{2,10},{3,11},{4,12},{5,13},{6,14},{7,15},{8,0},{9,1},... | collective-permute-start | bytes 196616 | tf_op jit(solution)/shard_map/ppermute | solution.py:116
  28.1 4.9 %collective-permute-start.9 = (bf16[128,256]{1,0:T(8,128)(2,1)S(1)}, bf16[128,256]{1,0:T(8,128)(2,1)S(1)}, u32[]{:S(2)}, u32[]{:S(2)}) collective-permute-start(bf16[128,256]{1,0:T(8,128)(2,1)S(1)} %fusion.5.refs_0_), channel_id=1, source_target_pairs={{0,4},{1,5},{2,6},{3,7},{4,0},{5,1},{6,2},{7,3},{8,12},{9,13},{10,... | collective-permute-start | bytes 196616 | tf_op jit(solution)/shard_map/ppermute | solution.py:116
  28.9 5.2 %collective-permute-start.15 = (bf16[128,256]{1,0:T(8,128)(2,1)S(1)}, bf16[128,256]{1,0:T(8,128)(2,1)S(1)}, u32[]{:S(2)}, u32[]{:S(2)}) collective-permute-start(bf16[128,256]{1,0:T(8,128)(2,1)S(1)} %collective-permute-done.12.refs_4_), channel_id=1, source_target_pairs={{0,12},{1,13},{2,14},{3,15},{4,8},{5,9},{6,10},{7,11},{8,4},{9,5},... | collective-permute-start | bytes 196616 | tf_op jit(solution)/shard_map/ppermute | solution.py:116
  31.3 4.3 %collective-permute-start.14 = (bf16[128,256]{1,0:T(8,128)(2,1)S(1)}, bf16[128,256]{1,0:T(8,128)(2,1)S(1)}, u32[]{:S(2)}, u32[]{:S(2)}) collective-permute-start(bf16[128,256]{1,0:T(8,128)(2,1)S(1)} %collective-permute-done.12.refs_4_), channel_id=1, source_target_pairs={{0,8},{1,9},{2,10},{3,11},{4,12},{5,13},{6,14},{7,15},{8,0},{9,1},... | collective-permute-start | bytes 196616 | tf_op jit(solution)/shard_map/ppermute | solution.py:116
  31.5 4.3 %collective-permute-start.13 = (bf16[128,256]{1,0:T(8,128)(2,1)S(1)}, bf16[128,256]{1,0:T(8,128)(2,1)S(1)}, u32[]{:S(2)}, u32[]{:S(2)}) collective-permute-start(bf16[128,256]{1,0:T(8,128)(2,1)S(1)} %collective-permute-done.12.refs_4_), channel_id=1, source_target_pairs={{0,4},{1,5},{2,6},{3,7},{4,0},{5,1},{6,2},{7,3},{8,12},{9,13},{10,... | collective-permute-start | bytes 196616 | tf_op jit(solution)/shard_map/ppermute | solution.py:116
  36.5 1.4 %collective-permute-start.16 = (bf16[256,256]{1,0:T(8,128)(2,1)S(1)}, bf16[256,256]{1,0:T(8,128)(2,1)S(1)}, u32[]{:S(2)}, u32[]{:S(2)}) collective-permute-start(bf16[256,256]{1,0:T(8,128)(2,1)S(1)} %slice.53), channel_id=1, source_target_pairs={{0,1},{1,0},{2,3},{3,2},{4,5},{5,4},{6,7},{7,6},{8,9},{9,8},{10,11... | collective-permute-start | bytes 393224 | tf_op jit(solution)/shard_map/ppermute | solution.py:116
  38.0 4.3 %collective-permute-start.17 = (bf16[128,256]{1,0:T(8,128)(2,1)S(1)}, bf16[128,256]{1,0:T(8,128)(2,1)S(1)}, u32[]{:S(2)}, u32[]{:S(2)}) collective-permute-start(bf16[128,256]{1,0:T(8,128)(2,1)S(1)} %slice.55), channel_id=1, source_target_pairs={{0,2},{1,3},{2,0},{3,1},{4,6},{5,7},{6,4},{7,5},{8,10},{9,11},{10,... | collective-permute-start | bytes 196616 | tf_op jit(solution)/shard_map/ppermute | solution.py:116
  42.5 5.9 %collective-permute-start.21 = (bf16[128,256]{1,0:T(8,128)(2,1)S(1)}, bf16[128,256]{1,0:T(8,128)(2,1)S(1)}, u32[]{:S(2)}, u32[]{:S(2)}) collective-permute-start(bf16[128,256]{1,0:T(8,128)(2,1)S(1)} %fusion.4.refs_0_), channel_id=1, source_target_pairs={{0,16},{1,17},{2,18},{3,19},{4,20},{5,21},{6,22},{7,23},{8,24},{9,... | collective-permute-start | bytes 196616 | tf_op jit(solution)/shard_map/ppermute | solution.py:116
  44.9 5.6 %collective-permute-start.20 = (bf16[128,256]{1,0:T(8,128)(2,1)S(1)}, bf16[128,256]{1,0:T(8,128)(2,1)S(1)}, u32[]{:S(2)}, u32[]{:S(2)}) collective-permute-start(bf16[128,256]{1,0:T(8,128)(2,1)S(1)} %fusion.4.refs_0_), channel_id=1, source_target_pairs={{0,12},{1,13},{2,14},{3,15},{4,8},{5,9},{6,10},{7,11},{8,4},{9,5},... | collective-permute-start | bytes 196616 | tf_op jit(solution)/shard_map/ppermute | solution.py:116
  46.3 5.6 %collective-permute-start.19 = (bf16[128,256]{1,0:T(8,128)(2,1)S(1)}, bf16[128,256]{1,0:T(8,128)(2,1)S(1)}, u32[]{:S(2)}, u32[]{:S(2)}) collective-permute-start(bf16[128,256]{1,0:T(8,128)(2,1)S(1)} %fusion.4.refs_0_), channel_id=1, source_target_pairs={{0,8},{1,9},{2,10},{3,11},{4,12},{5,13},{6,14},{7,15},{8,0},{9,1},... | collective-permute-start | bytes 196616 | tf_op jit(solution)/shard_map/ppermute | solution.py:116
  46.6 5.2 %collective-permute-start.18 = (bf16[128,256]{1,0:T(8,128)(2,1)S(1)}, bf16[128,256]{1,0:T(8,128)(2,1)S(1)}, u32[]{:S(2)}, u32[]{:S(2)}) collective-permute-start(bf16[128,256]{1,0:T(8,128)(2,1)S(1)} %fusion.4.refs_0_), channel_id=1, source_target_pairs={{0,4},{1,5},{2,6},{3,7},{4,0},{5,1},{6,2},{7,3},{8,12},{9,13},{10,... | collective-permute-start | bytes 196616 | tf_op jit(solution)/shard_map/ppermute | solution.py:116
  48.4 5.2 %collective-permute-start.24 = (bf16[128,256]{1,0:T(8,128)(2,1)S(1)}, bf16[128,256]{1,0:T(8,128)(2,1)S(1)}, u32[]{:S(2)}, u32[]{:S(2)}) collective-permute-start(bf16[128,256]{1,0:T(8,128)(2,1)S(1)} %collective-permute-done.21.refs_4_), channel_id=1, source_target_pairs={{0,12},{1,13},{2,14},{3,15},{4,8},{5,9},{6,10},{7,11},{8,4},{9,5},... | collective-permute-start | bytes 196616 | tf_op jit(solution)/shard_map/ppermute | solution.py:116
  50.0 4.3 %collective-permute-start.23 = (bf16[128,256]{1,0:T(8,128)(2,1)S(1)}, bf16[128,256]{1,0:T(8,128)(2,1)S(1)}, u32[]{:S(2)}, u32[]{:S(2)}) collective-permute-start(bf16[128,256]{1,0:T(8,128)(2,1)S(1)} %collective-permute-done.21.refs_4_), channel_id=1, source_target_pairs={{0,8},{1,9},{2,10},{3,11},{4,12},{5,13},{6,14},{7,15},{8,0},{9,1},... | collective-permute-start | bytes 196616 | tf_op jit(solution)/shard_map/ppermute | solution.py:116
  50.5 4.3 %collective-permute-start.22 = (bf16[128,256]{1,0:T(8,128)(2,1)S(1)}, bf16[128,256]{1,0:T(8,128)(2,1)S(1)}, u32[]{:S(2)}, u32[]{:S(2)}) collective-permute-start(bf16[128,256]{1,0:T(8,128)(2,1)S(1)} %collective-permute-done.21.refs_4_), channel_id=1, source_target_pairs={{0,4},{1,5},{2,6},{3,7},{4,0},{5,1},{6,2},{7,3},{8,12},{9,13},{10,... | collective-permute-start | bytes 196616 | tf_op jit(solution)/shard_map/ppermute | solution.py:116
  55.5 1.4 %collective-permute-start.25 = (bf16[256,256]{1,0:T(8,128)(2,1)S(1)}, bf16[256,256]{1,0:T(8,128)(2,1)S(1)}, u32[]{:S(2)}, u32[]{:S(2)}) collective-permute-start(bf16[256,256]{1,0:T(8,128)(2,1)S(1)} %slice.57), channel_id=1, source_target_pairs={{0,1},{1,0},{2,3},{3,2},{4,5},{5,4},{6,7},{7,6},{8,9},{9,8},{10,11... | collective-permute-start | bytes 393224 | tf_op jit(solution)/shard_map/ppermute | solution.py:116
  56.9 4.3 %collective-permute-start.26 = (bf16[128,256]{1,0:T(8,128)(2,1)S(1)}, bf16[128,256]{1,0:T(8,128)(2,1)S(1)}, u32[]{:S(2)}, u32[]{:S(2)}) collective-permute-start(bf16[128,256]{1,0:T(8,128)(2,1)S(1)} %slice.59), channel_id=1, source_target_pairs={{0,2},{1,3},{2,0},{3,1},{4,6},{5,7},{6,4},{7,5},{8,10},{9,11},{10,... | collective-permute-start | bytes 196616 | tf_op jit(solution)/shard_map/ppermute | solution.py:116

commit v3 on v2

v3 whole, which is shorter than its diff:
```python
import functools

import jax
import jax.numpy as jnp
from jax import lax
from jax.experimental import pallas as pl
from jax.experimental.pallas import tpu as pltpu
from jax.sharding import PartitionSpec as P

STEPS = 3
ROW_TILES = 4
CHUNK = 16
UNROLL = 4
LOCAL = 32
BOTH = ("src", "tgt")


def densify_kernel(places_ref, tiles_ref, out_ref, held_ref, total_ref, sems):
    group = pl.program_id(0)
    slots, edge = held_ref.shape[:2]
    places = total_ref.shape[0] - 1
    columns = out_ref.shape[1] // edge
    count = places_ref[slots]

    def copy(c):
        part = pl.ds(c * CHUNK, CHUNK)
        return pltpu.make_async_copy(tiles_ref.at[0, 0, part], held_ref.at[part], sems.at[c])

    for c in range(slots // CHUNK):
        pl.when((group == 0) & (c * CHUNK < count))(lambda c=c: copy(c).start())
    total_ref[...] = jnp.zeros_like(total_ref)

    def absorb(c):
        pl.when(group == 0)(lambda: copy(c).wait())

        def some(k, carry):
            for i in range(UNROLL):
                slot = c * CHUNK + k * UNROLL + i
                place = places_ref[slot] - group * places
                place = jnp.where((place >= 0) & (place < places), place, places)
                total_ref[place] += held_ref[slot].astype(jnp.float32)
            return carry

        lax.fori_loop(0, CHUNK // UNROLL, some, 0)

    for c in range(slots // CHUNK):
        pl.when(c * CHUNK < count)(lambda c=c: absorb(c))
    for place in range(places):
        i, j = divmod(place, columns)
        out_ref[i * edge:(i + 1) * edge, j * edge:(j + 1) * edge] = total_ref[place].astype(out_ref.dtype)


def densify(places, tiles, n_rows, n_cols):
    slots, edge = tiles.shape[2:4]
    assert slots % CHUNK == 0
    row_tiles = min(ROW_TILES, n_rows)
    return pl.pallas_call(
        densify_kernel,
        out_shape=jax.ShapeDtypeStruct((n_rows * edge, n_cols * edge), jnp.bfloat16),
        grid=(n_rows // row_tiles,),
        in_specs=[pl.BlockSpec(memory_space=pltpu.SMEM), pl.BlockSpec(memory_space=pltpu.HBM)],
        out_specs=pl.BlockSpec((row_tiles * edge, n_cols * edge), lambda g: (g, 0)),
        scratch_shapes=[
            pltpu.VMEM((slots, edge, edge), jnp.bfloat16),
            pltpu.VMEM((row_tiles * n_cols + 1, edge, edge), jnp.float32),
            pltpu.SemaphoreType.DMA((slots // CHUNK,)),
        ],
        compiler_params=pltpu.CompilerParams(vmem_limit_bytes=52 * 2**20),
        cost_estimate=pl.CostEstimate(flops=slots * edge * edge, bytes_accessed=2 * slots * edge * edge, transcendentals=0),
        name="densify",
    )(places, tiles)


def early_kernel(weights_ref, *refs):
    *parts, total_ref = refs
    block = jnp.concatenate([ref[...] for ref in reversed(parts)], axis=0)
    for start, size in row_groups(total_ref.shape[0]):
        lhs = weights_ref[start:start + size, :block.shape[0]]
        total_ref[start:start + size] = jnp.dot(lhs, block, preferred_element_type=jnp.float32)


def late_kernel(quarters, begun, weights_ref, *refs):
    parts, outs = refs[begun:-len(quarters)], refs[-len(quarters):]
    block = jnp.concatenate([ref[...] for ref in reversed(parts)], axis=0)
    for quarter, out_ref in zip(quarters, outs):
        rows = out_ref.shape[0]
        for start, size in row_groups(rows):
            at = slice(quarter * rows + start, quarter * rows + start + size)
            lhs = weights_ref[at, weights_ref.shape[1] - block.shape[0]:]
            term = jnp.dot(lhs, block, preferred_element_type=jnp.float32)
            out_ref[start:start + size] = (refs[0][at] + term if begun else term).astype(out_ref.dtype)


def row_groups(rows):
    size = min(rows, ROW_TILES * 128)
    return [(start, size) for start in range(0, rows, size)]


def local(kernel, name, out_shapes, flops, *args):
    whole = pl.BlockSpec(memory_space=pltpu.VMEM)
    return pl.pallas_call(
        kernel,
        out_shape=out_shapes,
        in_specs=[whole] * len(args),
        out_specs=jax.tree.map(lambda _: whole, out_shapes),
        compiler_params=pltpu.CompilerParams(vmem_limit_bytes=LOCAL * 2**20),
        cost_estimate=pl.CostEstimate(flops=flops, bytes_accessed=0, transcendentals=0),
        name=name,
    )(*args)


def bits_of(n):
    assert n & (n - 1) == 0
    return [1 << i for i in range(n.bit_length() - 1)]


def shards(initial, stubborn, coupling, tile_values, tile_target, tile_source, tile_count):
    own_rows, topics = initial.shape
    n_src, n_tgt = lax.axis_size("src"), lax.axis_size("tgt")
    assert own_rows == tile_values.shape[-1]
    tgt_bits, src_bits = bits_of(n_tgt), bits_of(n_src)
    top, low = src_bits[-1], src_bits[:-1]

    def swap(value, src_mask, tgt_mask):
        mask = src_mask * n_tgt + tgt_mask
        return lax.ppermute(value, BOTH, [(d, d ^ mask) for d in range(n_src * n_tgt)])

    def spread(blocks):
        held = dict(blocks)
        for pair in [low[i:i + 2] for i in range(0, len(low), 2)]:
            masks = pair if len(pair) == 1 else (pair[0], pair[1], pair[0] | pair[1])
            held.update({k | m: swap(value, m, 0) for k, value in held.items() for m in masks})
        return held

    def gather(near):
        far = swap(near, top, 0)
        close, beyond = spread({0: near}), spread({top: far})
        beyond.pop(top)
        return [far] + [close[m] for m in sorted(close, reverse=True)], [beyond[m] for m in sorted(beyond, reverse=True)]

    row, column = tile_target[0, 0] ^ lax.axis_index("tgt"), tile_source[0, 0] ^ lax.axis_index("src")
    row = sum(jnp.where(row & b != 0, n_tgt // (2 * b), 0) for b in tgt_bits)
    live = jnp.arange(row.shape[0]) < tile_count[0, 0]
    places = jnp.where(live, row * n_src + column, n_tgt * n_src)
    weights = densify(jnp.concatenate([places, tile_count[0]]), tile_values, n_tgt, n_src)
    openness = ((256.0 - stubborn.astype(jnp.float32)) / 256.0)[:, None]
    base = (1.0 - openness) * initial.astype(jnp.float32)

    def add(a, b):
        return (a.astype(jnp.float32) + b.astype(jnp.float32)).astype(jnp.bfloat16)

    work = 2 * n_tgt * own_rows * own_rows * topics
    opinion = initial
    for step in range(STEPS):
        first, others = gather(opinion)
        begun = [] if step == 0 else [
            local(early_kernel, "early", jax.ShapeDtypeStruct((n_tgt * own_rows, topics), jnp.float32), work * len(first), weights, *first)
        ]
        late = begun + others if begun else others + first
        quarter = jax.ShapeDtypeStruct((n_tgt * own_rows // 4, topics), jnp.bfloat16)

        def finish(name, *quarters):
            kernel = functools.partial(late_kernel, quarters, len(begun))
            return local(kernel, name, [quarter] * len(quarters), work * len(late) * len(quarters) // 4, weights, *late)

        (sent,) = finish("late_first", 3)
        received = swap(sent, 0, tgt_bits[0])
        kept, mine, sent = finish("late_rest", 1, 0, 2)
        other = swap(add(kept, received), 0, tgt_bits[1])
        terms = add(add(mine, swap(sent, 0, tgt_bits[0])), other)
        for bit in tgt_bits[2:]:
            half = terms.shape[0] // 2
            terms = add(terms[:half], swap(terms[half:], 0, bit))
        coupled = jnp.dot(terms, coupling, preferred_element_type=jnp.float32)
        opinion = (openness * coupled + base).astype(jnp.bfloat16)
    return opinion


def solution(mesh):
    in_specs = (
        P(("src", "tgt"), None),
        P(("src", "tgt")),
        P(),
        P("src", "tgt", None, None, None),
        P("src", "tgt", None),
        P("src", "tgt", None),
        P("src", "tgt"),
    )
    out_specs = P(("src", "tgt"), None)
    return jax.shard_map(shards, mesh=mesh, in_specs=in_specs, out_specs=out_specs, check_vma=False)
```

time: 62.8 us -> 59.7 us (0.951); the launches traced: 62.1 us -> 59.8 us
  local copies, waits for them, and re-layouts: 1.41 us -> 0.01 us
  waiting for transfers between devices: 19.8 us -> 18.7 us
  other arithmetic: 0.11 us -> 0.85 us
    unnamed x10 -> x6, local copies, waits for them, and re-layouts: 1.36 us -> 0.01 us
    ppermute x27 -> x30, waiting for transfers between devices: 19.8 us -> 18.7 us  [swap(): lax.ppermute(value, BOTH, [(d, d ^ mask) for d in range(n_src * n_tgt)])]
    add x0 -> x1, other arithmetic: none -> 0.71 us  [shards(): places = jnp.where(live, row * n_src + column, n_tgt * n_src)]
    ppermute x27 -> x30, starting transfers between devices: 34.1 us -> 33.5 us  [swap(): lax.ppermute(value, BOTH, [(d, d ^ mask) for d in range(n_src * n_tgt)])]
    pallas_call x3 -> x8, Pallas kernels: 2.08 us -> 2.28 us  [local(): pl.pallas_call(kernel, out_shape=out_shapes, in_specs=[whole] * len(args)...]
  transfers between devices with their start and end apart: 27 -> 30, of which waited for: 16 -> 14; matrix products, arithmetic and copies ran while one was open for 0% -> 1% of each run, Pallas kernels for 4% -> 7%
where the time goes in v3:
time: 59.7 us; the launch traced here: 59.8 us
  starting transfers between devices  33.5 us (56%)
  waiting for transfers between devices  18.7 us (31%)
  Pallas kernels  4.78 us (8%)
  matrix products  1.15 us (2%)
  other arithmetic  0.85 us (1%)
  between operations  0.81 us (1%)
    ppermute x30, starting transfers between devices, swap(): lax.ppermute(value, BOTH, [(d, d ^ mask) for d in range(n_src * n_tgt)])  33.5 us
    ppermute x30, waiting for transfers between devices, swap(): lax.ppermute(value, BOTH, [(d, d ^ mask) for d in range(n_src * n_tgt)])  18.7 us
    pallas_call x1, Pallas kernels, densify(): pl.pallas_call(densify_kernel, out_shape=jax.ShapeDtypeStruct((n_rows * e...  2.51 us
    pallas_call x8, Pallas kernels, local(): pl.pallas_call(kernel, out_shape=out_shapes, in_specs=[whole] * len(args)...  2.28 us
  transfers between devices with their start and end apart: 30, of which 14 were waited for; matrix products, arithmetic and copies ran while one was open for 1% of the time, Pallas kernels for 7%

profile of v3, /device:TPU:0, one launch (start us, length us, event | category | flops | bytes accessed | tf_op | source)
XLA Modules:
  0.0 59.8 jit_solution(1301767748451715907)
XLA Ops:
  0.0 4.1 %collective-permute-start = (bf16[128,256]{1,0:T(8,128)(2,1)}, bf16[128,256]{1,0:T(8,128)(2,1)S(1)}, u32[]{:S(2)}, u32[]{:S(2)}) collective-permute-start(bf16[128,256]{1,0:T(8,128)(2,1)} %refs_7_.3), channel_id=1, source_target_pairs={{0,16},{1,17},{2,18},{3,19},{4,20},{5,21},{6,22},{7,23},{8,24},{9,... | collective-permute-start | bytes 196616 | tf_op jit(solution)/shard_map/ppermute | solution.py:126
  4.1 2.5 %collective-permute-start.4 = (bf16[128,256]{1,0:T(8,128)(2,1)}, bf16[128,256]{1,0:T(8,128)(2,1)S(1)}, u32[]{:S(2)}, u32[]{:S(2)}) collective-permute-start(bf16[128,256]{1,0:T(8,128)(2,1)} %refs_7_.3), channel_id=1, source_target_pairs={{0,12},{1,13},{2,14},{3,15},{4,8},{5,9},{6,10},{7,11},{8,4},{9,5},... | collective-permute-start | bytes 196616 | tf_op jit(solution)/shard_map/ppermute | solution.py:126
  6.6 0.4 collective-permute-start.5
  7.1 0.5 collective-permute-start.6
  8.3 0.7 %multiply_add_fusion = s32[1,1,144]{2,1,0:T(1,128)S(1)} fusion(s32[1,1,144]{2,1,0:T(1,128)} %param.12, s32[1,1,144]{2,1,0:T(1,128)} %param.11, s32[]{:T(128)S(6)} %axis_index.25, s32[]{:T(128)S(6)} %axis_index.22), kind=kLoop, calls=%fused_computation.24 | loop fusion | flops 1584 | bytes 1736 | tf_op jit(solution)/shard_map/add | solution.py:144
  9.0 2.6 %collective-permute-start.1 = (bf16[128,256]{1,0:T(8,128)(2,1)S(1)}, bf16[128,256]{1,0:T(8,128)(2,1)S(1)}, u32[]{:S(2)}, u32[]{:S(2)}) collective-permute-start(bf16[128,256]{1,0:T(8,128)(2,1)S(1)} %collective-permute-done.refs_3_), channel_id=1, source_target_pairs={{0,12},{1,13},{2,14},{3,15},{4,8},{5,9},{6,10},{7,11},{8,4},{9,5},... | collective-permute-start | bytes 196616 | tf_op jit(solution)/shard_map/ppermute | solution.py:126
  11.5 0.4 collective-permute-start.2
  12.0 0.5 collective-permute-start.3
  12.6 2.5 %densify.1.weights_ref = bf16[512,1024]{1,0:T(8,128)(2,1)S(1)} custom-call(s32[145]{0:T(256)S(1)} %pad_add_fusion.places_ref, bf16[1,1,144,128,128]{4,3,2,1,0:T(8,128)(2,1)} %tiles_ref.1), custom_call_target="tpu_custom_call" | custom-call | flops 2359296 | bytes 4718592 | tf_op jit(solution)/shard_map/densify/pallas_call | solution.py:57
  15.2 0.7 %collective-permute-done.2.refs_1_ = bf16[128,256]{1,0:T(8,128)(2,1)S(1)} collective-permute-done((bf16[128,256]{1,0:T(8,128)(2,1)S(1)}, bf16[128,256]{1,0:T(8,128)(2,1)S(1)}, u32[]{:S(2)}, u32[]{:S(2)}) %collective-permute-start.2) | collective-permute-done | bytes 65568 | tf_op jit(solution)/shard_map/ppermute | solution.py:126
  15.8 0.5 collective-permute-done.3.refs_2_
  16.3 0.2 late_first.3
  16.6 0.4 late_rest.3
  17.0 0.6 collective-permute-start.7
  17.5 0.3 collective-permute-done.8
  17.8 1.6 %collective-permute-start.9 = (bf16[128,256]{1,0:T(8,128)(2,1)S(1)}, bf16[128,256]{1,0:T(8,128)(2,1)S(1)}, u32[]{:S(2)}, u32[]{:S(2)}) collective-permute-start(bf16[128,256]{1,0:T(8,128)(2,1)S(1)} %add_convert_fusion.7), channel_id=1, source_target_pairs={{0,2},{1,3},{2,0},{3,1},{4,6},{5,7},{6,4},{7,5},{8,10},{9,11},{10,... | collective-permute-start | bytes 196616 | tf_op jit(solution)/shard_map/ppermute | solution.py:126
  19.4 2.7 %collective-permute-done.9 = bf16[128,256]{1,0:T(8,128)(2,1)S(1)} collective-permute-done((bf16[128,256]{1,0:T(8,128)(2,1)S(1)}, bf16[128,256]{1,0:T(8,128)(2,1)S(1)}, u32[]{:S(2)}, u32[]{:S(2)}) %collective-permute-start.9) | collective-permute-done | bytes 65568 | tf_op jit(solution)/shard_map/ppermute | solution.py:126
  22.4 1.1 %collective-permute-start.10 = (bf16[128,256]{1,0:T(8,128)(2,1)S(1)}, bf16[128,256]{1,0:T(8,128)(2,1)S(1)}, u32[]{:S(2)}, u32[]{:S(2)}) collective-permute-start(bf16[128,256]{1,0:T(8,128)(2,1)S(1)} %fusion.5.refs_4_), channel_id=1, source_target_pairs={{0,16},{1,17},{2,18},{3,19},{4,20},{5,21},{6,22},{7,23},{8,24},{9,... | collective-permute-start | bytes 196616 | tf_op jit(solution)/shard_map/ppermute | solution.py:126
  23.4 1.9 %collective-permute-start.11 = (bf16[128,256]{1,0:T(8,128)(2,1)S(1)}, bf16[128,256]{1,0:T(8,128)(2,1)S(1)}, u32[]{:S(2)}, u32[]{:S(2)}) collective-permute-start(bf16[128,256]{1,0:T(8,128)(2,1)S(1)} %fusion.5.refs_4_), channel_id=1, source_target_pairs={{0,12},{1,13},{2,14},{3,15},{4,8},{5,9},{6,10},{7,11},{8,4},{9,5},... | collective-permute-start | bytes 196616 | tf_op jit(solution)/shard_map/ppermute | solution.py:126
  25.4 1.5 %collective-permute-start.13 = (bf16[128,256]{1,0:T(8,128)(2,1)S(1)}, bf16[128,256]{1,0:T(8,128)(2,1)S(1)}, u32[]{:S(2)}, u32[]{:S(2)}) collective-permute-start(bf16[128,256]{1,0:T(8,128)(2,1)S(1)} %fusion.5.refs_4_), channel_id=1, source_target_pairs={{0,4},{1,5},{2,6},{3,7},{4,0},{5,1},{6,2},{7,3},{8,12},{9,13},{10,... | collective-permute-start | bytes 196616 | tf_op jit(solution)/shard_map/ppermute | solution.py:126
  26.9 0.8 %collective-permute-done.10.refs_0_ = bf16[128,256]{1,0:T(8,128)(2,1)S(1)} collective-permute-done((bf16[128,256]{1,0:T(8,128)(2,1)S(1)}, bf16[128,256]{1,0:T(8,128)(2,1)S(1)}, u32[]{:S(2)}, u32[]{:S(2)}) %collective-permute-start.10) | collective-permute-done | bytes 65568 | tf_op jit(solution)/shard_map/ppermute | solution.py:126
  27.7 2.6 %collective-permute-start.14 = (bf16[128,256]{1,0:T(8,128)(2,1)S(1)}, bf16[128,256]{1,0:T(8,128)(2,1)S(1)}, u32[]{:S(2)}, u32[]{:S(2)}) collective-permute-start(bf16[128,256]{1,0:T(8,128)(2,1)S(1)} %collective-permute-done.10.refs_0_), channel_id=1, source_target_pairs={{0,12},{1,13},{2,14},{3,15},{4,8},{5,9},{6,10},{7,11},{8,4},{9,5},... | collective-permute-start | bytes 196616 | tf_op jit(solution)/shard_map/ppermute | solution.py:126
  30.3 0.9 %collective-permute-start.16 = (bf16[128,256]{1,0:T(8,128)(2,1)S(1)}, bf16[128,256]{1,0:T(8,128)(2,1)S(1)}, u32[]{:S(2)}, u32[]{:S(2)}) collective-permute-start(bf16[128,256]{1,0:T(8,128)(2,1)S(1)} %collective-permute-done.10.refs_0_), channel_id=1, source_target_pairs={{0,4},{1,5},{2,6},{3,7},{4,0},{5,1},{6,2},{7,3},{8,12},{9,13},{10,... | collective-permute-start | bytes 196616 | tf_op jit(solution)/shard_map/ppermute | solution.py:126
  31.2 0.4 early.2.refs_0_
  31.6 1.3 %collective-permute-done.14.refs_1_ = bf16[128,256]{1,0:T(8,128)(2,1)S(1)} collective-permute-done((bf16[128,256]{1,0:T(8,128)(2,1)S(1)}, bf16[128,256]{1,0:T(8,128)(2,1)S(1)}, u32[]{:S(2)}, u32[]{:S(2)}) %collective-permute-start.14) | collective-permute-done | bytes 65568 | tf_op jit(solution)/shard_map/ppermute | solution.py:126
  32.9 1.7 %collective-permute-done.15.refs_2_ = bf16[128,256]{1,0:T(8,128)(2,1)S(1)} collective-permute-done((bf16[128,256]{1,0:T(8,128)(2,1)S(1)}, bf16[128,256]{1,0:T(8,128)(2,1)S(1)}, u32[]{:S(2)}, u32[]{:S(2)}) %collective-permute-start.15) | collective-permute-done | bytes 65568 | tf_op jit(solution)/shard_map/ppermute | solution.py:126
  34.6 0.2 late_first.4
  34.8 0.3 late_rest.4
  35.1 0.6 collective-permute-start.17
  35.7 0.4 collective-permute-done.18
  36.1 0.9 %collective-permute-start.19 = (bf16[128,256]{1,0:T(8,128)(2,1)S(1)}, bf16[128,256]{1,0:T(8,128)(2,1)S(1)}, u32[]{:S(2)}, u32[]{:S(2)}) collective-permute-start(bf16[128,256]{1,0:T(8,128)(2,1)S(1)} %add_convert_fusion.4), channel_id=1, source_target_pairs={{0,2},{1,3},{2,0},{3,1},{4,6},{5,7},{6,4},{7,5},{8,10},{9,11},{10,... | collective-permute-start | bytes 196616 | tf_op jit(solution)/shard_map/ppermute | solution.py:126
  37.0 3.4 %collective-permute-done.19 = bf16[128,256]{1,0:T(8,128)(2,1)S(1)} collective-permute-done((bf16[128,256]{1,0:T(8,128)(2,1)S(1)}, bf16[128,256]{1,0:T(8,128)(2,1)S(1)}, u32[]{:S(2)}, u32[]{:S(2)}) %collective-permute-start.19) | collective-permute-done | bytes 65568 | tf_op jit(solution)/shard_map/ppermute | solution.py:126
  40.6 1.5 %collective-permute-start.20 = (bf16[128,256]{1,0:T(8,128)(2,1)S(1)}, bf16[128,256]{1,0:T(8,128)(2,1)S(1)}, u32[]{:S(2)}, u32[]{:S(2)}) collective-permute-start(bf16[128,256]{1,0:T(8,128)(2,1)S(1)} %fusion.4.refs_4_), channel_id=1, source_target_pairs={{0,16},{1,17},{2,18},{3,19},{4,20},{5,21},{6,22},{7,23},{8,24},{9,... | collective-permute-start | bytes 196616 | tf_op jit(solution)/shard_map/ppermute | solution.py:126
  42.1 2.2 %collective-permute-start.21 = (bf16[128,256]{1,0:T(8,128)(2,1)S(1)}, bf16[128,256]{1,0:T(8,128)(2,1)S(1)}, u32[]{:S(2)}, u32[]{:S(2)}) collective-permute-start(bf16[128,256]{1,0:T(8,128)(2,1)S(1)} %fusion.4.refs_4_), channel_id=1, source_target_pairs={{0,12},{1,13},{2,14},{3,15},{4,8},{5,9},{6,10},{7,11},{8,4},{9,5},... | collective-permute-start | bytes 196616 | tf_op jit(solution)/shard_map/ppermute | solution.py:126
  44.3 0.3 collective-permute-start.22
  44.6 1.0 %collective-permute-start.23 = (bf16[128,256]{1,0:T(8,128)(2,1)S(1)}, bf16[128,256]{1,0:T(8,128)(2,1)S(1)}, u32[]{:S(2)}, u32[]{:S(2)}) collective-permute-start(bf16[128,256]{1,0:T(8,128)(2,1)S(1)} %fusion.4.refs_4_), channel_id=1, source_target_pairs={{0,4},{1,5},{2,6},{3,7},{4,0},{5,1},{6,2},{7,3},{8,12},{9,13},{10,... | collective-permute-start | bytes 196616 | tf_op jit(solution)/shard_map/ppermute | solution.py:126
  45.6 0.6 collective-permute-done.20.refs_0_
  46.1 2.7 %collective-permute-start.24 = (bf16[128,256]{1,0:T(8,128)(2,1)S(1)}, bf16[128,256]{1,0:T(8,128)(2,1)S(1)}, u32[]{:S(2)}, u32[]{:S(2)}) collective-permute-start(bf16[128,256]{1,0:T(8,128)(2,1)S(1)} %collective-permute-done.20.refs_0_), channel_id=1, source_target_pairs={{0,12},{1,13},{2,14},{3,15},{4,8},{5,9},{6,10},{7,11},{8,4},{9,5},... | collective-permute-start | bytes 196616 | tf_op jit(solution)/shard_map/ppermute | solution.py:126
  48.9 1.2 %collective-permute-start.26 = (bf16[128,256]{1,0:T(8,128)(2,1)S(1)}, bf16[128,256]{1,0:T(8,128)(2,1)S(1)}, u32[]{:S(2)}, u32[]{:S(2)}) collective-permute-start(bf16[128,256]{1,0:T(8,128)(2,1)S(1)} %collective-permute-done.20.refs_0_), channel_id=1, source_target_pairs={{0,4},{1,5},{2,6},{3,7},{4,0},{5,1},{6,2},{7,3},{8,12},{9,13},{10,... | collective-permute-start | bytes 196616 | tf_op jit(solution)/shard_map/ppermute | solution.py:126
  50.0 0.4 early.3.refs_0_
  50.4 0.9 %collective-permute-done.24.refs_1_ = bf16[128,256]{1,0:T(8,128)(2,1)S(1)} collective-permute-done((bf16[128,256]{1,0:T(8,128)(2,1)S(1)}, bf16[128,256]{1,0:T(8,128)(2,1)S(1)}, u32[]{:S(2)}, u32[]{:S(2)}) %collective-permute-start.24) | collective-permute-done | bytes 65568 | tf_op jit(solution)/shard_map/ppermute | solution.py:126
  51.3 1.8 %collective-permute-done.25.refs_2_ = bf16[128,256]{1,0:T(8,128)(2,1)S(1)} collective-permute-done((bf16[128,256]{1,0:T(8,128)(2,1)S(1)}, bf16[128,256]{1,0:T(8,128)(2,1)S(1)}, u32[]{:S(2)}, u32[]{:S(2)}) %collective-permute-start.25) | collective-permute-done | bytes 65568 | tf_op jit(solution)/shard_map/ppermute | solution.py:126
  53.4 0.3 late_rest.5
  53.7 0.6 collective-permute-start.27
  54.2 0.4 collective-permute-done.28
  54.7 1.0 %collective-permute-start.29 = (bf16[128,256]{1,0:T(8,128)(2,1)S(1)}, bf16[128,256]{1,0:T(8,128)(2,1)S(1)}, u32[]{:S(2)}, u32[]{:S(2)}) collective-permute-start(bf16[128,256]{1,0:T(8,128)(2,1)S(1)} %add_convert_fusion.1), channel_id=1, source_target_pairs={{0,2},{1,3},{2,0},{3,1},{4,6},{5,7},{6,4},{7,5},{8,10},{9,11},{10,... | collective-permute-start | bytes 196616 | tf_op jit(solution)/shard_map/ppermute | solution.py:126
  55.7 3.3 %collective-permute-done.29 = bf16[128,256]{1,0:T(8,128)(2,1)S(1)} collective-permute-done((bf16[128,256]{1,0:T(8,128)(2,1)S(1)}, bf16[128,256]{1,0:T(8,128)(2,1)S(1)}, u32[]{:S(2)}, u32[]{:S(2)}) %collective-permute-start.29) | collective-permute-done | bytes 65568 | tf_op jit(solution)/shard_map/ppermute | solution.py:126
  59.0 0.8 %fusion.3 = bf16[128,256]{1,0:T(8,128)(2,1)} fusion(bf16[256,256]{1,0:T(8,128)(2,1)S(1)} %copy-done, bf16[128,256]{1,0:T(8,128)(2,1)S(1)} %copy-done.1, bf16[128,256]{1,0:T(8,128)(2,1)S(1)} %collective-permute-done.29, bf16[128,256]{1,0:T(8,128)(2,1)S(1)} %collective-permute-done.27, bf16[128,256]{1,0:T(8,128)(2,1)S(1)} %get-tuple-element.20, ...), kind=kOutput, calls=%fused_computation.6 | convolution fusion | flops 17203200 | bytes 459776 | tf_op jit(solution)/shard_map/dot_general | solution.py:174
  (37 shorter events, 1.0 us)
Async XLA Ops:
  0.0 22.2 %copy-start = (bf16[256,256]{1,0:T(8,128)(2,1)S(1)}, bf16[256,256]{1,0:T(8,128)(2,1)}, u32[]{:S(2)}) copy-start(bf16[256,256]{1,0:T(8,128)(2,1)} %param.9) | copy-start | bytes 393220
  0.0 16.3 %copy-start.1 = (bf16[128,256]{1,0:T(8,128)(2,1)S(1)}, bf16[128,256]{1,0:T(8,128)(2,1)}, u32[]{:S(2)}) copy-start(bf16[128,256]{1,0:T(8,128)(2,1)} %refs_7_.3) | copy-start | bytes 196612
  0.0 19.4 %copy-start.2 = (s32[128]{0:T(128)S(1)}, s32[128]{0:T(128)}, u32[]{:S(2)}) copy-start(s32[128]{0:T(128)} %param.8) | copy-start | bytes 1540
  0.0 9.0 %collective-permute-start = (bf16[128,256]{1,0:T(8,128)(2,1)}, bf16[128,256]{1,0:T(8,128)(2,1)S(1)}, u32[]{:S(2)}, u32[]{:S(2)}) collective-permute-start(bf16[128,256]{1,0:T(8,128)(2,1)} %refs_7_.3), channel_id=1, source_target_pairs={{0,16},{1,17},{2,18},{3,19},{4,20},{5,21},{6,22},{7,23},{8,24},{9,... | collective-permute-start | bytes 196616 | tf_op jit(solution)/shard_map/ppermute | solution.py:126
  4.1 7.9 %collective-permute-start.4 = (bf16[128,256]{1,0:T(8,128)(2,1)}, bf16[128,256]{1,0:T(8,128)(2,1)S(1)}, u32[]{:S(2)}, u32[]{:S(2)}) collective-permute-start(bf16[128,256]{1,0:T(8,128)(2,1)} %refs_7_.3), channel_id=1, source_target_pairs={{0,12},{1,13},{2,14},{3,15},{4,8},{5,9},{6,10},{7,11},{8,4},{9,5},... | collective-permute-start | bytes 196616 | tf_op jit(solution)/shard_map/ppermute | solution.py:126
  6.6 8.5 %collective-permute-start.5 = (bf16[128,256]{1,0:T(8,128)(2,1)}, bf16[128,256]{1,0:T(8,128)(2,1)S(1)}, u32[]{:S(2)}, u32[]{:S(2)}) collective-permute-start(bf16[128,256]{1,0:T(8,128)(2,1)} %refs_7_.3), channel_id=1, source_target_pairs={{0,8},{1,9},{2,10},{3,11},{4,12},{5,13},{6,14},{7,15},{8,0},{9,1},... | collective-permute-start | bytes 196616 | tf_op jit(solution)/shard_map/ppermute | solution.py:126
  7.1 8.1 %collective-permute-start.6 = (bf16[128,256]{1,0:T(8,128)(2,1)}, bf16[128,256]{1,0:T(8,128)(2,1)S(1)}, u32[]{:S(2)}, u32[]{:S(2)}) collective-permute-start(bf16[128,256]{1,0:T(8,128)(2,1)} %refs_7_.3), channel_id=1, source_target_pairs={{0,4},{1,5},{2,6},{3,7},{4,0},{5,1},{6,2},{7,3},{8,12},{9,13},{10,... | collective-permute-start | bytes 196616 | tf_op jit(solution)/shard_map/ppermute | solution.py:126
  9.0 6.2 %collective-permute-start.1 = (bf16[128,256]{1,0:T(8,128)(2,1)S(1)}, bf16[128,256]{1,0:T(8,128)(2,1)S(1)}, u32[]{:S(2)}, u32[]{:S(2)}) collective-permute-start(bf16[128,256]{1,0:T(8,128)(2,1)S(1)} %collective-permute-done.refs_3_), channel_id=1, source_target_pairs={{0,12},{1,13},{2,14},{3,15},{4,8},{5,9},{6,10},{7,11},{8,4},{9,5},... | collective-permute-start | bytes 196616 | tf_op jit(solution)/shard_map/ppermute | solution.py:126
  11.5 4.3 %collective-permute-start.2 = (bf16[128,256]{1,0:T(8,128)(2,1)S(1)}, bf16[128,256]{1,0:T(8,128)(2,1)S(1)}, u32[]{:S(2)}, u32[]{:S(2)}) collective-permute-start(bf16[128,256]{1,0:T(8,128)(2,1)S(1)} %collective-permute-done.refs_3_), channel_id=1, source_target_pairs={{0,8},{1,9},{2,10},{3,11},{4,12},{5,13},{6,14},{7,15},{8,0},{9,1},... | collective-permute-start | bytes 196616 | tf_op jit(solution)/shard_map/ppermute | solution.py:126
  12.0 4.3 %collective-permute-start.3 = (bf16[128,256]{1,0:T(8,128)(2,1)S(1)}, bf16[128,256]{1,0:T(8,128)(2,1)S(1)}, u32[]{:S(2)}, u32[]{:S(2)}) collective-permute-start(bf16[128,256]{1,0:T(8,128)(2,1)S(1)} %collective-permute-done.refs_3_), channel_id=1, source_target_pairs={{0,4},{1,5},{2,6},{3,7},{4,0},{5,1},{6,2},{7,3},{8,12},{9,13},{10,... | collective-permute-start | bytes 196616 | tf_op jit(solution)/shard_map/ppermute | solution.py:126
  16.5 1.3 %collective-permute-start.8 = (bf16[128,256]{1,0:T(8,128)(2,1)S(1)}, bf16[128,256]{1,0:T(8,128)(2,1)S(1)}, u32[]{:S(2)}, u32[]{:S(2)}) collective-permute-start(bf16[128,256]{1,0:T(8,128)(2,1)S(1)} %late_first.3), channel_id=1, source_target_pairs={{0,1},{1,0},{2,3},{3,2},{4,5},{5,4},{6,7},{7,6},{8,9},{9,8},{10,11... | collective-permute-start | bytes 196616 | tf_op jit(solution)/shard_map/ppermute | solution.py:126
  17.0 2.5 %collective-permute-start.7 = (bf16[128,256]{1,0:T(8,128)(2,1)S(1)}, bf16[128,256]{1,0:T(8,128)(2,1)S(1)}, u32[]{:S(2)}, u32[]{:S(2)}) collective-permute-start(bf16[128,256]{1,0:T(8,128)(2,1)S(1)} %get-tuple-element.15), channel_id=1, source_target_pairs={{0,1},{1,0},{2,3},{3,2},{4,5},{5,4},{6,7},{7,6},{8,9},{9,8},{10,11... | collective-permute-start | bytes 196616 | tf_op jit(solution)/shard_map/ppermute | solution.py:126
  17.8 4.3 %collective-permute-start.9 = (bf16[128,256]{1,0:T(8,128)(2,1)S(1)}, bf16[128,256]{1,0:T(8,128)(2,1)S(1)}, u32[]{:S(2)}, u32[]{:S(2)}) collective-permute-start(bf16[128,256]{1,0:T(8,128)(2,1)S(1)} %add_convert_fusion.7), channel_id=1, source_target_pairs={{0,2},{1,3},{2,0},{3,1},{4,6},{5,7},{6,4},{7,5},{8,10},{9,11},{10,... | collective-permute-start | bytes 196616 | tf_op jit(solution)/shard_map/ppermute | solution.py:126
  22.4 5.3 %collective-permute-start.10 = (bf16[128,256]{1,0:T(8,128)(2,1)S(1)}, bf16[128,256]{1,0:T(8,128)(2,1)S(1)}, u32[]{:S(2)}, u32[]{:S(2)}) collective-permute-start(bf16[128,256]{1,0:T(8,128)(2,1)S(1)} %fusion.5.refs_4_), channel_id=1, source_target_pairs={{0,16},{1,17},{2,18},{3,19},{4,20},{5,21},{6,22},{7,23},{8,24},{9,... | collective-permute-start | bytes 196616 | tf_op jit(solution)/shard_map/ppermute | solution.py:126
  23.4 6.9 %collective-permute-start.11 = (bf16[128,256]{1,0:T(8,128)(2,1)S(1)}, bf16[128,256]{1,0:T(8,128)(2,1)S(1)}, u32[]{:S(2)}, u32[]{:S(2)}) collective-permute-start(bf16[128,256]{1,0:T(8,128)(2,1)S(1)} %fusion.5.refs_4_), channel_id=1, source_target_pairs={{0,12},{1,13},{2,14},{3,15},{4,8},{5,9},{6,10},{7,11},{8,4},{9,5},... | collective-permute-start | bytes 196616 | tf_op jit(solution)/shard_map/ppermute | solution.py:126
  25.4 5.8 %collective-permute-start.12 = (bf16[128,256]{1,0:T(8,128)(2,1)S(1)}, bf16[128,256]{1,0:T(8,128)(2,1)S(1)}, u32[]{:S(2)}, u32[]{:S(2)}) collective-permute-start(bf16[128,256]{1,0:T(8,128)(2,1)S(1)} %fusion.5.refs_4_), channel_id=1, source_target_pairs={{0,8},{1,9},{2,10},{3,11},{4,12},{5,13},{6,14},{7,15},{8,0},{9,1},... | collective-permute-start | bytes 196616 | tf_op jit(solution)/shard_map/ppermute | solution.py:126
  25.4 5.8 %collective-permute-start.13 = (bf16[128,256]{1,0:T(8,128)(2,1)S(1)}, bf16[128,256]{1,0:T(8,128)(2,1)S(1)}, u32[]{:S(2)}, u32[]{:S(2)}) collective-permute-start(bf16[128,256]{1,0:T(8,128)(2,1)S(1)} %fusion.5.refs_4_), channel_id=1, source_target_pairs={{0,4},{1,5},{2,6},{3,7},{4,0},{5,1},{6,2},{7,3},{8,12},{9,13},{10,... | collective-permute-start | bytes 196616 | tf_op jit(solution)/shard_map/ppermute | solution.py:126
  27.7 5.2 %collective-permute-start.14 = (bf16[128,256]{1,0:T(8,128)(2,1)S(1)}, bf16[128,256]{1,0:T(8,128)(2,1)S(1)}, u32[]{:S(2)}, u32[]{:S(2)}) collective-permute-start(bf16[128,256]{1,0:T(8,128)(2,1)S(1)} %collective-permute-done.10.refs_0_), channel_id=1, source_target_pairs={{0,12},{1,13},{2,14},{3,15},{4,8},{5,9},{6,10},{7,11},{8,4},{9,5},... | collective-permute-start | bytes 196616 | tf_op jit(solution)/shard_map/ppermute | solution.py:126
  30.3 4.3 %collective-permute-start.15 = (bf16[128,256]{1,0:T(8,128)(2,1)S(1)}, bf16[128,256]{1,0:T(8,128)(2,1)S(1)}, u32[]{:S(2)}, u32[]{:S(2)}) collective-permute-start(bf16[128,256]{1,0:T(8,128)(2,1)S(1)} %collective-permute-done.10.refs_0_), channel_id=1, source_target_pairs={{0,8},{1,9},{2,10},{3,11},{4,12},{5,13},{6,14},{7,15},{8,0},{9,1},... | collective-permute-start | bytes 196616 | tf_op jit(solution)/shard_map/ppermute | solution.py:126
  30.3 4.3 %collective-permute-start.16 = (bf16[128,256]{1,0:T(8,128)(2,1)S(1)}, bf16[128,256]{1,0:T(8,128)(2,1)S(1)}, u32[]{:S(2)}, u32[]{:S(2)}) collective-permute-start(bf16[128,256]{1,0:T(8,128)(2,1)S(1)} %collective-permute-done.10.refs_0_), channel_id=1, source_target_pairs={{0,4},{1,5},{2,6},{3,7},{4,0},{5,1},{6,2},{7,3},{8,12},{9,13},{10,... | collective-permute-start | bytes 196616 | tf_op jit(solution)/shard_map/ppermute | solution.py:126
  34.8 1.3 %collective-permute-start.18 = (bf16[128,256]{1,0:T(8,128)(2,1)S(1)}, bf16[128,256]{1,0:T(8,128)(2,1)S(1)}, u32[]{:S(2)}, u32[]{:S(2)}) collective-permute-start(bf16[128,256]{1,0:T(8,128)(2,1)S(1)} %late_first.4), channel_id=1, source_target_pairs={{0,1},{1,0},{2,3},{3,2},{4,5},{5,4},{6,7},{7,6},{8,9},{9,8},{10,11... | collective-permute-start | bytes 196616 | tf_op jit(solution)/shard_map/ppermute | solution.py:126
  35.1 1.9 %collective-permute-start.17 = (bf16[128,256]{1,0:T(8,128)(2,1)S(1)}, bf16[128,256]{1,0:T(8,128)(2,1)S(1)}, u32[]{:S(2)}, u32[]{:S(2)}) collective-permute-start(bf16[128,256]{1,0:T(8,128)(2,1)S(1)} %get-tuple-element.18), channel_id=1, source_target_pairs={{0,1},{1,0},{2,3},{3,2},{4,5},{5,4},{6,7},{7,6},{8,9},{9,8},{10,11... | collective-permute-start | bytes 196616 | tf_op jit(solution)/shard_map/ppermute | solution.py:126
  36.1 4.3 %collective-permute-start.19 = (bf16[128,256]{1,0:T(8,128)(2,1)S(1)}, bf16[128,256]{1,0:T(8,128)(2,1)S(1)}, u32[]{:S(2)}, u32[]{:S(2)}) collective-permute-start(bf16[128,256]{1,0:T(8,128)(2,1)S(1)} %add_convert_fusion.4), channel_id=1, source_target_pairs={{0,2},{1,3},{2,0},{3,1},{4,6},{5,7},{6,4},{7,5},{8,10},{9,11},{10,... | collective-permute-start | bytes 196616 | tf_op jit(solution)/shard_map/ppermute | solution.py:126
  40.6 5.5 %collective-permute-start.20 = (bf16[128,256]{1,0:T(8,128)(2,1)S(1)}, bf16[128,256]{1,0:T(8,128)(2,1)S(1)}, u32[]{:S(2)}, u32[]{:S(2)}) collective-permute-start(bf16[128,256]{1,0:T(8,128)(2,1)S(1)} %fusion.4.refs_4_), channel_id=1, source_target_pairs={{0,16},{1,17},{2,18},{3,19},{4,20},{5,21},{6,22},{7,23},{8,24},{9,... | collective-permute-start | bytes 196616 | tf_op jit(solution)/shard_map/ppermute | solution.py:126
  42.1 6.8 %collective-permute-start.21 = (bf16[128,256]{1,0:T(8,128)(2,1)S(1)}, bf16[128,256]{1,0:T(8,128)(2,1)S(1)}, u32[]{:S(2)}, u32[]{:S(2)}) collective-permute-start(bf16[128,256]{1,0:T(8,128)(2,1)S(1)} %fusion.4.refs_4_), channel_id=1, source_target_pairs={{0,12},{1,13},{2,14},{3,15},{4,8},{5,9},{6,10},{7,11},{8,4},{9,5},... | collective-permute-start | bytes 196616 | tf_op jit(solution)/shard_map/ppermute | solution.py:126
  44.3 5.7 %collective-permute-start.22 = (bf16[128,256]{1,0:T(8,128)(2,1)S(1)}, bf16[128,256]{1,0:T(8,128)(2,1)S(1)}, u32[]{:S(2)}, u32[]{:S(2)}) collective-permute-start(bf16[128,256]{1,0:T(8,128)(2,1)S(1)} %fusion.4.refs_4_), channel_id=1, source_target_pairs={{0,8},{1,9},{2,10},{3,11},{4,12},{5,13},{6,14},{7,15},{8,0},{9,1},... | collective-permute-start | bytes 196616 | tf_op jit(solution)/shard_map/ppermute | solution.py:126
  44.6 5.4 %collective-permute-start.23 = (bf16[128,256]{1,0:T(8,128)(2,1)S(1)}, bf16[128,256]{1,0:T(8,128)(2,1)S(1)}, u32[]{:S(2)}, u32[]{:S(2)}) collective-permute-start(bf16[128,256]{1,0:T(8,128)(2,1)S(1)} %fusion.4.refs_4_), channel_id=1, source_target_pairs={{0,4},{1,5},{2,6},{3,7},{4,0},{5,1},{6,2},{7,3},{8,12},{9,13},{10,... | collective-permute-start | bytes 196616 | tf_op jit(solution)/shard_map/ppermute | solution.py:126
  46.1 5.2 %collective-permute-start.24 = (bf16[128,256]{1,0:T(8,128)(2,1)S(1)}, bf16[128,256]{1,0:T(8,128)(2,1)S(1)}, u32[]{:S(2)}, u32[]{:S(2)}) collective-permute-start(bf16[128,256]{1,0:T(8,128)(2,1)S(1)} %collective-permute-done.20.refs_0_), channel_id=1, source_target_pairs={{0,12},{1,13},{2,14},{3,15},{4,8},{5,9},{6,10},{7,11},{8,4},{9,5},... | collective-permute-start | bytes 196616 | tf_op jit(solution)/shard_map/ppermute | solution.py:126
  48.8 4.3 %collective-permute-start.25 = (bf16[128,256]{1,0:T(8,128)(2,1)S(1)}, bf16[128,256]{1,0:T(8,128)(2,1)S(1)}, u32[]{:S(2)}, u32[]{:S(2)}) collective-permute-start(bf16[128,256]{1,0:T(8,128)(2,1)S(1)} %collective-permute-done.20.refs_0_), channel_id=1, source_target_pairs={{0,8},{1,9},{2,10},{3,11},{4,12},{5,13},{6,14},{7,15},{8,0},{9,1},... | collective-permute-start | bytes 196616 | tf_op jit(solution)/shard_map/ppermute | solution.py:126
  48.9 4.3 %collective-permute-start.26 = (bf16[128,256]{1,0:T(8,128)(2,1)S(1)}, bf16[128,256]{1,0:T(8,128)(2,1)S(1)}, u32[]{:S(2)}, u32[]{:S(2)}) collective-permute-start(bf16[128,256]{1,0:T(8,128)(2,1)S(1)} %collective-permute-done.20.refs_0_), channel_id=1, source_target_pairs={{0,4},{1,5},{2,6},{3,7},{4,0},{5,1},{6,2},{7,3},{8,12},{9,13},{10,... | collective-permute-start | bytes 196616 | tf_op jit(solution)/shard_map/ppermute | solution.py:126
  53.3 1.3 %collective-permute-start.28 = (bf16[128,256]{1,0:T(8,128)(2,1)S(1)}, bf16[128,256]{1,0:T(8,128)(2,1)S(1)}, u32[]{:S(2)}, u32[]{:S(2)}) collective-permute-start(bf16[128,256]{1,0:T(8,128)(2,1)S(1)} %late_first.5), channel_id=1, source_target_pairs={{0,1},{1,0},{2,3},{3,2},{4,5},{5,4},{6,7},{7,6},{8,9},{9,8},{10,11... | collective-permute-start | bytes 196616 | tf_op jit(solution)/shard_map/ppermute | solution.py:126
  53.7 2.0 %collective-permute-start.27 = (bf16[128,256]{1,0:T(8,128)(2,1)S(1)}, bf16[128,256]{1,0:T(8,128)(2,1)S(1)}, u32[]{:S(2)}, u32[]{:S(2)}) collective-permute-start(bf16[128,256]{1,0:T(8,128)(2,1)S(1)} %get-tuple-element.21), channel_id=1, source_target_pairs={{0,1},{1,0},{2,3},{3,2},{4,5},{5,4},{6,7},{7,6},{8,9},{9,8},{10,11... | collective-permute-start | bytes 196616 | tf_op jit(solution)/shard_map/ppermute | solution.py:126
  54.7 4.3 %collective-permute-start.29 = (bf16[128,256]{1,0:T(8,128)(2,1)S(1)}, bf16[128,256]{1,0:T(8,128)(2,1)S(1)}, u32[]{:S(2)}, u32[]{:S(2)}) collective-permute-start(bf16[128,256]{1,0:T(8,128)(2,1)S(1)} %add_convert_fusion.1), channel_id=1, source_target_pairs={{0,2},{1,3},{2,0},{3,1},{4,6},{5,7},{6,4},{7,5},{8,10},{9,11},{10,... | collective-permute-start | bytes 196616 | tf_op jit(solution)/shard_map/ppermute | solution.py:126

commit v4 on v3

--- a/solution.py
+++ b/solution.py
@@ -73,7 +73,7 @@
 
 def early_kernel(weights_ref, *refs):
     *parts, total_ref = refs
-    block = jnp.concatenate([ref[...] for ref in reversed(parts)], axis=0)
+    block = jnp.concatenate([ref[...] for ref in parts], axis=0)
     for start, size in row_groups(total_ref.shape[0]):
         lhs = weights_ref[start:start + size, :block.shape[0]]
         total_ref[start:start + size] = jnp.dot(lhs, block, preferred_element_type=jnp.float32)
@@ -81,7 +81,7 @@
 
 def late_kernel(quarters, begun, weights_ref, *refs):
     parts, outs = refs[begun:-len(quarters)], refs[-len(quarters):]
-    block = jnp.concatenate([ref[...] for ref in reversed(parts)], axis=0)
+    block = jnp.concatenate([ref[...] for ref in parts], axis=0)
     for quarter, out_ref in zip(quarters, outs):
         rows = out_ref.shape[0]
         for start, size in row_groups(rows):
@@ -133,10 +133,18 @@
         return held
 
     def gather(near):
-        far = swap(near, top, 0)
-        close, beyond = spread({0: near}), spread({top: far})
-        beyond.pop(top)
-        return [far] + [close[m] for m in sorted(close, reverse=True)], [beyond[m] for m in sorted(beyond, reverse=True)]
+        across = tgt_bits[0]
+        there = swap(near, top, across)
+        far = swap(there, 0, across)
+        close, beyond = spread({0: near}), {top: far}
+        for i in range(0, len(low), 2):
+            pair = low[i:i + 2]
+            masks = pair if len(pair) == 1 else (pair[0], pair[1], pair[0] | pair[1])
+            if i == 0:
+                beyond |= {top | m: swap(there, m, across) for m in masks}
+            else:
+                beyond |= {k | m: swap(value, m, 0) for k, value in beyond.items() for m in masks}
+        return [close[m] for m in sorted(close)], [beyond[m] for m in sorted(beyond)]
 
     row, column = tile_target[0, 0] ^ lax.axis_index("tgt"), tile_source[0, 0] ^ lax.axis_index("src")
     row = sum(jnp.where(row & b != 0, n_tgt // (2 * b), 0) for b in tgt_bits)
@@ -156,7 +164,7 @@
         begun = [] if step == 0 else [
             local(early_kernel, "early", jax.ShapeDtypeStruct((n_tgt * own_rows, topics), jnp.float32), work * len(first), weights, *first)
         ]
-        late = begun + others if begun else others + first
+        late = begun + others if begun else first + others
         quarter = jax.ShapeDtypeStruct((n_tgt * own_rows // 4, topics), jnp.bfloat16)
 
         def finish(name, *quarters):

time: 59.7 us -> 58.1 us (0.973)
  waiting for transfers between devices: 18.7 us -> 16 us
  starting transfers between devices: 33.5 us -> 34.6 us
    ppermute x30 -> x33, waiting for transfers between devices: 18.7 us -> 16 us  [swap(): lax.ppermute(value, BOTH, [(d, d ^ mask) for d in range(n_src * n_tgt)])]
    ppermute x30 -> x33, starting transfers between devices: 33.5 us -> 34.6 us  [swap(): lax.ppermute(value, BOTH, [(d, d ^ mask) for d in range(n_src * n_tgt)])]
  transfers between devices with their start and end apart: 30 -> 33, of which waited for: 14 -> 14; matrix products, arithmetic and copies ran while one was open for 1% -> 1% of each run, Pallas kernels for 7% -> 7%
where the time goes in v4:
time: 58.1 us
  starting transfers between devices  34.6 us (60%)
  waiting for transfers between devices  16 us (28%)
  Pallas kernels  4.66 us (8%)
  matrix products  1.15 us (2%)
  other arithmetic  0.85 us (1%)
  between operations  0.79 us (1%)
    ppermute x33, starting transfers between devices, swap(): lax.ppermute(value, BOTH, [(d, d ^ mask) for d in range(n_src * n_tgt)])  34.6 us
    ppermute x33, waiting for transfers between devices, swap(): lax.ppermute(value, BOTH, [(d, d ^ mask) for d in range(n_src * n_tgt)])  16 us
    pallas_call x1, Pallas kernels, densify(): pl.pallas_call(densify_kernel, out_shape=jax.ShapeDtypeStruct((n_rows * e...  2.52 us
    pallas_call x8, Pallas kernels, local(): pl.pallas_call(kernel, out_shape=out_shapes, in_specs=[whole] * len(args)...  2.14 us
  transfers between devices with their start and end apart: 33, of which 14 were waited for; matrix products, arithmetic and copies ran while one was open for 1% of the time, Pallas kernels for 7%

profile of v4, /device:TPU:0, one launch (start us, length us, event | category | flops | bytes accessed | tf_op | source)
XLA Modules:
  0.0 58.1 jit_solution(15905392452902778810)
XLA Ops:
  0.0 3.5 %collective-permute-start.3 = (bf16[128,256]{1,0:T(8,128)(2,1)}, bf16[128,256]{1,0:T(8,128)(2,1)S(1)}, u32[]{:S(2)}, u32[]{:S(2)}) collective-permute-start(bf16[128,256]{1,0:T(8,128)(2,1)} %refs_0_.3), channel_id=1, source_target_pairs={{0,17},{1,16},{2,19},{3,18},{4,21},{5,20},{6,23},{7,22},{8,25},{9,... | collective-permute-start | bytes 196616 | tf_op jit(solution)/shard_map/ppermute | solution.py:126
  3.6 2.5 %collective-permute-start.2 = (bf16[128,256]{1,0:T(8,128)(2,1)}, bf16[128,256]{1,0:T(8,128)(2,1)S(1)}, u32[]{:S(2)}, u32[]{:S(2)}) collective-permute-start(bf16[128,256]{1,0:T(8,128)(2,1)} %refs_0_.3), channel_id=1, source_target_pairs={{0,12},{1,13},{2,14},{3,15},{4,8},{5,9},{6,10},{7,11},{8,4},{9,5},... | collective-permute-start | bytes 196616 | tf_op jit(solution)/shard_map/ppermute | solution.py:126
  6.1 0.4 collective-permute-start.1
  6.5 0.5 collective-permute-start
  7.7 0.7 %multiply_add_fusion = s32[1,1,144]{2,1,0:T(1,128)S(1)} fusion(s32[1,1,144]{2,1,0:T(1,128)} %param.12, s32[1,1,144]{2,1,0:T(1,128)} %param.11, s32[]{:T(128)S(6)} %axis_index.25, s32[]{:T(128)S(6)} %axis_index.22), kind=kLoop, calls=%fused_computation.24 | loop fusion | flops 1584 | bytes 1736 | tf_op jit(solution)/shard_map/add | solution.py:152
  8.4 2.0 %collective-permute-start.7 = (bf16[128,256]{1,0:T(8,128)(2,1)S(1)}, bf16[128,256]{1,0:T(8,128)(2,1)S(1)}, u32[]{:S(2)}, u32[]{:S(2)}) collective-permute-start(bf16[128,256]{1,0:T(8,128)(2,1)S(1)} %collective-permute-done.3), channel_id=1, source_target_pairs={{0,13},{1,12},{2,15},{3,14},{4,9},{5,8},{6,11},{7,10},{8,5},{9,4},... | collective-permute-start | bytes 196616 | tf_op jit(solution)/shard_map/ppermute | solution.py:126
  10.5 0.7 %collective-permute-start.6 = (bf16[128,256]{1,0:T(8,128)(2,1)S(1)}, bf16[128,256]{1,0:T(8,128)(2,1)S(1)}, u32[]{:S(2)}, u32[]{:S(2)}) collective-permute-start(bf16[128,256]{1,0:T(8,128)(2,1)S(1)} %collective-permute-done.3), channel_id=1, source_target_pairs={{0,9},{1,8},{2,11},{3,10},{4,13},{5,12},{6,15},{7,14},{8,1},{9,0},... | collective-permute-start | bytes 196616 | tf_op jit(solution)/shard_map/ppermute | solution.py:126
  11.4 0.5 collective-permute-start.4
  11.9 2.5 %densify.1.weights_ref = bf16[512,1024]{1,0:T(8,128)(2,1)S(1)} custom-call(s32[145]{0:T(256)S(1)} %pad_add_fusion.places_ref, bf16[1,1,144,128,128]{4,3,2,1,0:T(8,128)(2,1)} %tiles_ref.1), custom_call_target="tpu_custom_call" | custom-call | flops 2359296 | bytes 4718592 | tf_op jit(solution)/shard_map/densify/pallas_call | solution.py:57
  14.4 0.2 collective-permute-done.6.refs_6_
  14.7 0.6 %collective-permute-done.5.refs_5_ = bf16[128,256]{1,0:T(8,128)(2,1)S(1)} collective-permute-done((bf16[128,256]{1,0:T(8,128)(2,1)S(1)}, bf16[128,256]{1,0:T(8,128)(2,1)S(1)}, u32[]{:S(2)}, u32[]{:S(2)}) %collective-permute-start.5) | collective-permute-done | bytes 65568 | tf_op jit(solution)/shard_map/ppermute | solution.py:126
  15.3 0.2 late_first.3
  15.7 0.4 late_rest.3
  16.1 0.5 collective-permute-start.8
  16.6 0.3 collective-permute-done.9
  16.9 1.6 %collective-permute-start.10 = (bf16[128,256]{1,0:T(8,128)(2,1)S(1)}, bf16[128,256]{1,0:T(8,128)(2,1)S(1)}, u32[]{:S(2)}, u32[]{:S(2)}) collective-permute-start(bf16[128,256]{1,0:T(8,128)(2,1)S(1)} %add_convert_fusion.7), channel_id=1, source_target_pairs={{0,2},{1,3},{2,0},{3,1},{4,6},{5,7},{6,4},{7,5},{8,10},{9,11},{10,... | collective-permute-start | bytes 196616 | tf_op jit(solution)/shard_map/ppermute | solution.py:126
  18.5 2.7 %collective-permute-done.10 = bf16[128,256]{1,0:T(8,128)(2,1)S(1)} collective-permute-done((bf16[128,256]{1,0:T(8,128)(2,1)S(1)}, bf16[128,256]{1,0:T(8,128)(2,1)S(1)}, u32[]{:S(2)}, u32[]{:S(2)}) %collective-permute-start.10) | collective-permute-done | bytes 65568 | tf_op jit(solution)/shard_map/ppermute | solution.py:126
  21.4 1.0 %collective-permute-start.14 = (bf16[128,256]{1,0:T(8,128)(2,1)S(1)}, bf16[128,256]{1,0:T(8,128)(2,1)S(1)}, u32[]{:S(2)}, u32[]{:S(2)}) collective-permute-start(bf16[128,256]{1,0:T(8,128)(2,1)S(1)} %fusion.5.refs_0_), channel_id=1, source_target_pairs={{0,17},{1,16},{2,19},{3,18},{4,21},{5,20},{6,23},{7,22},{8,25},{9,... | collective-permute-start | bytes 196616 | tf_op jit(solution)/shard_map/ppermute | solution.py:126
  22.4 2.5 %collective-permute-start.13 = (bf16[128,256]{1,0:T(8,128)(2,1)S(1)}, bf16[128,256]{1,0:T(8,128)(2,1)S(1)}, u32[]{:S(2)}, u32[]{:S(2)}) collective-permute-start(bf16[128,256]{1,0:T(8,128)(2,1)S(1)} %fusion.5.refs_0_), channel_id=1, source_target_pairs={{0,12},{1,13},{2,14},{3,15},{4,8},{5,9},{6,10},{7,11},{8,4},{9,5},... | collective-permute-start | bytes 196616 | tf_op jit(solution)/shard_map/ppermute | solution.py:126
  25.1 0.8 %collective-permute-start.11 = (bf16[128,256]{1,0:T(8,128)(2,1)S(1)}, bf16[128,256]{1,0:T(8,128)(2,1)S(1)}, u32[]{:S(2)}, u32[]{:S(2)}) collective-permute-start(bf16[128,256]{1,0:T(8,128)(2,1)S(1)} %fusion.5.refs_0_), channel_id=1, source_target_pairs={{0,4},{1,5},{2,6},{3,7},{4,0},{5,1},{6,2},{7,3},{8,12},{9,13},{10,... | collective-permute-start | bytes 196616 | tf_op jit(solution)/shard_map/ppermute | solution.py:126
  25.9 0.3 collective-permute-done.14
  26.2 2.5 %collective-permute-start.18 = (bf16[128,256]{1,0:T(8,128)(2,1)S(1)}, bf16[128,256]{1,0:T(8,128)(2,1)S(1)}, u32[]{:S(2)}, u32[]{:S(2)}) collective-permute-start(bf16[128,256]{1,0:T(8,128)(2,1)S(1)} %collective-permute-done.14), channel_id=1, source_target_pairs={{0,13},{1,12},{2,15},{3,14},{4,9},{5,8},{6,11},{7,10},{8,5},{9,4},... | collective-permute-start | bytes 196616 | tf_op jit(solution)/shard_map/ppermute | solution.py:126
  28.7 1.0 %collective-permute-start.16 = (bf16[128,256]{1,0:T(8,128)(2,1)S(1)}, bf16[128,256]{1,0:T(8,128)(2,1)S(1)}, u32[]{:S(2)}, u32[]{:S(2)}) collective-permute-start(bf16[128,256]{1,0:T(8,128)(2,1)S(1)} %collective-permute-done.14), channel_id=1, source_target_pairs={{0,5},{1,4},{2,7},{3,6},{4,1},{5,0},{6,3},{7,2},{8,13},{9,12},{10,... | collective-permute-start | bytes 196616 | tf_op jit(solution)/shard_map/ppermute | solution.py:126
  29.7 0.3 collective-permute-start.15
  30.1 0.3 early.2.refs_0_
  30.4 0.8 %collective-permute-done.18.refs_4_ = bf16[128,256]{1,0:T(8,128)(2,1)S(1)} collective-permute-done((bf16[128,256]{1,0:T(8,128)(2,1)S(1)}, bf16[128,256]{1,0:T(8,128)(2,1)S(1)}, u32[]{:S(2)}, u32[]{:S(2)}) %collective-permute-start.18) | collective-permute-done | bytes 65568 | tf_op jit(solution)/shard_map/ppermute | solution.py:126
  31.1 1.5 %collective-permute-done.17.refs_3_ = bf16[128,256]{1,0:T(8,128)(2,1)S(1)} collective-permute-done((bf16[128,256]{1,0:T(8,128)(2,1)S(1)}, bf16[128,256]{1,0:T(8,128)(2,1)S(1)}, u32[]{:S(2)}, u32[]{:S(2)}) %collective-permute-start.17) | collective-permute-done | bytes 65568 | tf_op jit(solution)/shard_map/ppermute | solution.py:126
  32.9 0.4 collective-permute-start.20
  33.3 0.3 late_rest.4
  33.5 0.3 collective-permute-start.19
  33.8 0.4 collective-permute-done.20
  34.2 1.8 %collective-permute-start.21 = (bf16[128,256]{1,0:T(8,128)(2,1)S(1)}, bf16[128,256]{1,0:T(8,128)(2,1)S(1)}, u32[]{:S(2)}, u32[]{:S(2)}) collective-permute-start(bf16[128,256]{1,0:T(8,128)(2,1)S(1)} %add_convert_fusion.4), channel_id=1, source_target_pairs={{0,2},{1,3},{2,0},{3,1},{4,6},{5,7},{6,4},{7,5},{8,10},{9,11},{10,... | collective-permute-start | bytes 196616 | tf_op jit(solution)/shard_map/ppermute | solution.py:126
  36.0 2.5 %collective-permute-done.21 = bf16[128,256]{1,0:T(8,128)(2,1)S(1)} collective-permute-done((bf16[128,256]{1,0:T(8,128)(2,1)S(1)}, bf16[128,256]{1,0:T(8,128)(2,1)S(1)}, u32[]{:S(2)}, u32[]{:S(2)}) %collective-permute-start.21) | collective-permute-done | bytes 65568 | tf_op jit(solution)/shard_map/ppermute | solution.py:126
  38.8 2.0 %collective-permute-start.25 = (bf16[128,256]{1,0:T(8,128)(2,1)S(1)}, bf16[128,256]{1,0:T(8,128)(2,1)S(1)}, u32[]{:S(2)}, u32[]{:S(2)}) collective-permute-start(bf16[128,256]{1,0:T(8,128)(2,1)S(1)} %fusion.4.refs_0_), channel_id=1, source_target_pairs={{0,17},{1,16},{2,19},{3,18},{4,21},{5,20},{6,23},{7,22},{8,25},{9,... | collective-permute-start | bytes 196616 | tf_op jit(solution)/shard_map/ppermute | solution.py:126
  40.7 2.6 %collective-permute-start.24 = (bf16[128,256]{1,0:T(8,128)(2,1)S(1)}, bf16[128,256]{1,0:T(8,128)(2,1)S(1)}, u32[]{:S(2)}, u32[]{:S(2)}) collective-permute-start(bf16[128,256]{1,0:T(8,128)(2,1)S(1)} %fusion.4.refs_0_), channel_id=1, source_target_pairs={{0,12},{1,13},{2,14},{3,15},{4,8},{5,9},{6,10},{7,11},{8,4},{9,5},... | collective-permute-start | bytes 196616 | tf_op jit(solution)/shard_map/ppermute | solution.py:126
  43.3 0.9 %collective-permute-start.22 = (bf16[128,256]{1,0:T(8,128)(2,1)S(1)}, bf16[128,256]{1,0:T(8,128)(2,1)S(1)}, u32[]{:S(2)}, u32[]{:S(2)}) collective-permute-start(bf16[128,256]{1,0:T(8,128)(2,1)S(1)} %fusion.4.refs_0_), channel_id=1, source_target_pairs={{0,4},{1,5},{2,6},{3,7},{4,0},{5,1},{6,2},{7,3},{8,12},{9,13},{10,... | collective-permute-start | bytes 196616 | tf_op jit(solution)/shard_map/ppermute | solution.py:126
  44.2 2.9 %collective-permute-start.29 = (bf16[128,256]{1,0:T(8,128)(2,1)S(1)}, bf16[128,256]{1,0:T(8,128)(2,1)S(1)}, u32[]{:S(2)}, u32[]{:S(2)}) collective-permute-start(bf16[128,256]{1,0:T(8,128)(2,1)S(1)} %collective-permute-done.25), channel_id=1, source_target_pairs={{0,13},{1,12},{2,15},{3,14},{4,9},{5,8},{6,11},{7,10},{8,5},{9,4},... | collective-permute-start | bytes 196616 | tf_op jit(solution)/shard_map/ppermute | solution.py:126
  47.1 0.8 %collective-permute-start.27 = (bf16[128,256]{1,0:T(8,128)(2,1)S(1)}, bf16[128,256]{1,0:T(8,128)(2,1)S(1)}, u32[]{:S(2)}, u32[]{:S(2)}) collective-permute-start(bf16[128,256]{1,0:T(8,128)(2,1)S(1)} %collective-permute-done.25), channel_id=1, source_target_pairs={{0,5},{1,4},{2,7},{3,6},{4,1},{5,0},{6,3},{7,2},{8,13},{9,12},{10,... | collective-permute-start | bytes 196616 | tf_op jit(solution)/shard_map/ppermute | solution.py:126
  48.2 0.3 early.3.refs_0_
  48.5 1.0 %collective-permute-done.29.refs_4_ = bf16[128,256]{1,0:T(8,128)(2,1)S(1)} collective-permute-done((bf16[128,256]{1,0:T(8,128)(2,1)S(1)}, bf16[128,256]{1,0:T(8,128)(2,1)S(1)}, u32[]{:S(2)}, u32[]{:S(2)}) %collective-permute-start.29) | collective-permute-done | bytes 65568 | tf_op jit(solution)/shard_map/ppermute | solution.py:126
  49.4 2.0 %collective-permute-done.28.refs_3_ = bf16[128,256]{1,0:T(8,128)(2,1)S(1)} collective-permute-done((bf16[128,256]{1,0:T(8,128)(2,1)S(1)}, bf16[128,256]{1,0:T(8,128)(2,1)S(1)}, u32[]{:S(2)}, u32[]{:S(2)}) %collective-permute-start.28) | collective-permute-done | bytes 65568 | tf_op jit(solution)/shard_map/ppermute | solution.py:126
  51.5 0.2 late_first.5
  51.8 0.3 late_rest.5
  52.1 0.5 collective-permute-start.30
  52.6 0.4 collective-permute-done.31
  53.0 1.3 %collective-permute-start.32 = (bf16[128,256]{1,0:T(8,128)(2,1)S(1)}, bf16[128,256]{1,0:T(8,128)(2,1)S(1)}, u32[]{:S(2)}, u32[]{:S(2)}) collective-permute-start(bf16[128,256]{1,0:T(8,128)(2,1)S(1)} %add_convert_fusion.1), channel_id=1, source_target_pairs={{0,2},{1,3},{2,0},{3,1},{4,6},{5,7},{6,4},{7,5},{8,10},{9,11},{10,... | collective-permute-start | bytes 196616 | tf_op jit(solution)/shard_map/ppermute | solution.py:126
  54.3 3.1 %collective-permute-done.32 = bf16[128,256]{1,0:T(8,128)(2,1)S(1)} collective-permute-done((bf16[128,256]{1,0:T(8,128)(2,1)S(1)}, bf16[128,256]{1,0:T(8,128)(2,1)S(1)}, u32[]{:S(2)}, u32[]{:S(2)}) %collective-permute-start.32) | collective-permute-done | bytes 65568 | tf_op jit(solution)/shard_map/ppermute | solution.py:126
  57.3 0.8 %fusion.3 = bf16[128,256]{1,0:T(8,128)(2,1)} fusion(bf16[256,256]{1,0:T(8,128)(2,1)S(1)} %copy-done, bf16[128,256]{1,0:T(8,128)(2,1)S(1)} %copy-done.1, bf16[128,256]{1,0:T(8,128)(2,1)S(1)} %collective-permute-done.32, bf16[128,256]{1,0:T(8,128)(2,1)S(1)} %collective-permute-done.30, bf16[128,256]{1,0:T(8,128)(2,1)S(1)} %get-tuple-element.20, ...), kind=kOutput, calls=%fused_computation.6 | convolution fusion | flops 17203200 | bytes 459776 | tf_op jit(solution)/shard_map/dot_general | solution.py:182
  (43 shorter events, 1.7 us)
Async XLA Ops:
  0.0 21.2 %copy-start = (bf16[256,256]{1,0:T(8,128)(2,1)S(1)}, bf16[256,256]{1,0:T(8,128)(2,1)}, u32[]{:S(2)}) copy-start(bf16[256,256]{1,0:T(8,128)(2,1)} %param.9) | copy-start | bytes 393220
  0.0 15.3 %copy-start.1 = (bf16[128,256]{1,0:T(8,128)(2,1)S(1)}, bf16[128,256]{1,0:T(8,128)(2,1)}, u32[]{:S(2)}) copy-start(bf16[128,256]{1,0:T(8,128)(2,1)} %refs_0_.3) | copy-start | bytes 196612
  0.0 18.5 %copy-start.2 = (s32[128]{0:T(128)S(1)}, s32[128]{0:T(128)}, u32[]{:S(2)}) copy-start(s32[128]{0:T(128)} %param.8) | copy-start | bytes 1540
  0.0 8.4 %collective-permute-start.3 = (bf16[128,256]{1,0:T(8,128)(2,1)}, bf16[128,256]{1,0:T(8,128)(2,1)S(1)}, u32[]{:S(2)}, u32[]{:S(2)}) collective-permute-start(bf16[128,256]{1,0:T(8,128)(2,1)} %refs_0_.3), channel_id=1, source_target_pairs={{0,17},{1,16},{2,19},{3,18},{4,21},{5,20},{6,23},{7,22},{8,25},{9,... | collective-permute-start | bytes 196616 | tf_op jit(solution)/shard_map/ppermute | solution.py:126
  3.6 7.6 %collective-permute-start.2 = (bf16[128,256]{1,0:T(8,128)(2,1)}, bf16[128,256]{1,0:T(8,128)(2,1)S(1)}, u32[]{:S(2)}, u32[]{:S(2)}) collective-permute-start(bf16[128,256]{1,0:T(8,128)(2,1)} %refs_0_.3), channel_id=1, source_target_pairs={{0,12},{1,13},{2,14},{3,15},{4,8},{5,9},{6,10},{7,11},{8,4},{9,5},... | collective-permute-start | bytes 196616 | tf_op jit(solution)/shard_map/ppermute | solution.py:126
  6.1 5.3 %collective-permute-start.1 = (bf16[128,256]{1,0:T(8,128)(2,1)}, bf16[128,256]{1,0:T(8,128)(2,1)S(1)}, u32[]{:S(2)}, u32[]{:S(2)}) collective-permute-start(bf16[128,256]{1,0:T(8,128)(2,1)} %refs_0_.3), channel_id=1, source_target_pairs={{0,8},{1,9},{2,10},{3,11},{4,12},{5,13},{6,14},{7,15},{8,0},{9,1},... | collective-permute-start | bytes 196616 | tf_op jit(solution)/shard_map/ppermute | solution.py:126
  6.5 7.9 %collective-permute-start = (bf16[128,256]{1,0:T(8,128)(2,1)}, bf16[128,256]{1,0:T(8,128)(2,1)S(1)}, u32[]{:S(2)}, u32[]{:S(2)}) collective-permute-start(bf16[128,256]{1,0:T(8,128)(2,1)} %refs_0_.3), channel_id=1, source_target_pairs={{0,4},{1,5},{2,6},{3,7},{4,0},{5,1},{6,2},{7,3},{8,12},{9,13},{10,... | collective-permute-start | bytes 196616 | tf_op jit(solution)/shard_map/ppermute | solution.py:126
  8.4 6.0 %collective-permute-start.7 = (bf16[128,256]{1,0:T(8,128)(2,1)S(1)}, bf16[128,256]{1,0:T(8,128)(2,1)S(1)}, u32[]{:S(2)}, u32[]{:S(2)}) collective-permute-start(bf16[128,256]{1,0:T(8,128)(2,1)S(1)} %collective-permute-done.3), channel_id=1, source_target_pairs={{0,13},{1,12},{2,15},{3,14},{4,9},{5,8},{6,11},{7,10},{8,5},{9,4},... | collective-permute-start | bytes 196616 | tf_op jit(solution)/shard_map/ppermute | solution.py:126
  10.5 4.2 %collective-permute-start.6 = (bf16[128,256]{1,0:T(8,128)(2,1)S(1)}, bf16[128,256]{1,0:T(8,128)(2,1)S(1)}, u32[]{:S(2)}, u32[]{:S(2)}) collective-permute-start(bf16[128,256]{1,0:T(8,128)(2,1)S(1)} %collective-permute-done.3), channel_id=1, source_target_pairs={{0,9},{1,8},{2,11},{3,10},{4,13},{5,12},{6,15},{7,14},{8,1},{9,0},... | collective-permute-start | bytes 196616 | tf_op jit(solution)/shard_map/ppermute | solution.py:126
  11.2 4.1 %collective-permute-start.5 = (bf16[128,256]{1,0:T(8,128)(2,1)S(1)}, bf16[128,256]{1,0:T(8,128)(2,1)S(1)}, u32[]{:S(2)}, u32[]{:S(2)}) collective-permute-start(bf16[128,256]{1,0:T(8,128)(2,1)S(1)} %collective-permute-done.3), channel_id=1, source_target_pairs={{0,5},{1,4},{2,7},{3,6},{4,1},{5,0},{6,3},{7,2},{8,13},{9,12},{10,... | collective-permute-start | bytes 196616 | tf_op jit(solution)/shard_map/ppermute | solution.py:126
  11.4 4.0 %collective-permute-start.4 = (bf16[128,256]{1,0:T(8,128)(2,1)S(1)}, bf16[128,256]{1,0:T(8,128)(2,1)S(1)}, u32[]{:S(2)}, u32[]{:S(2)}) collective-permute-start(bf16[128,256]{1,0:T(8,128)(2,1)S(1)} %collective-permute-done.3), channel_id=1, source_target_pairs={{0,1},{1,0},{2,3},{3,2},{4,5},{5,4},{6,7},{7,6},{8,9},{9,8},{10,11... | collective-permute-start | bytes 196616 | tf_op jit(solution)/shard_map/ppermute | solution.py:126
  15.5 1.3 %collective-permute-start.9 = (bf16[128,256]{1,0:T(8,128)(2,1)S(1)}, bf16[128,256]{1,0:T(8,128)(2,1)S(1)}, u32[]{:S(2)}, u32[]{:S(2)}) collective-permute-start(bf16[128,256]{1,0:T(8,128)(2,1)S(1)} %late_first.3), channel_id=1, source_target_pairs={{0,1},{1,0},{2,3},{3,2},{4,5},{5,4},{6,7},{7,6},{8,9},{9,8},{10,11... | collective-permute-start | bytes 196616 | tf_op jit(solution)/shard_map/ppermute | solution.py:126
  16.1 2.4 %collective-permute-start.8 = (bf16[128,256]{1,0:T(8,128)(2,1)S(1)}, bf16[128,256]{1,0:T(8,128)(2,1)S(1)}, u32[]{:S(2)}, u32[]{:S(2)}) collective-permute-start(bf16[128,256]{1,0:T(8,128)(2,1)S(1)} %get-tuple-element.15), channel_id=1, source_target_pairs={{0,1},{1,0},{2,3},{3,2},{4,5},{5,4},{6,7},{7,6},{8,9},{9,8},{10,11... | collective-permute-start | bytes 196616 | tf_op jit(solution)/shard_map/ppermute | solution.py:126
  16.9 4.3 %collective-permute-start.10 = (bf16[128,256]{1,0:T(8,128)(2,1)S(1)}, bf16[128,256]{1,0:T(8,128)(2,1)S(1)}, u32[]{:S(2)}, u32[]{:S(2)}) collective-permute-start(bf16[128,256]{1,0:T(8,128)(2,1)S(1)} %add_convert_fusion.7), channel_id=1, source_target_pairs={{0,2},{1,3},{2,0},{3,1},{4,6},{5,7},{6,4},{7,5},{8,10},{9,11},{10,... | collective-permute-start | bytes 196616 | tf_op jit(solution)/shard_map/ppermute | solution.py:126
  21.4 4.8 %collective-permute-start.14 = (bf16[128,256]{1,0:T(8,128)(2,1)S(1)}, bf16[128,256]{1,0:T(8,128)(2,1)S(1)}, u32[]{:S(2)}, u32[]{:S(2)}) collective-permute-start(bf16[128,256]{1,0:T(8,128)(2,1)S(1)} %fusion.5.refs_0_), channel_id=1, source_target_pairs={{0,17},{1,16},{2,19},{3,18},{4,21},{5,20},{6,23},{7,22},{8,25},{9,... | collective-permute-start | bytes 196616 | tf_op jit(solution)/shard_map/ppermute | solution.py:126
  22.4 6.3 %collective-permute-start.13 = (bf16[128,256]{1,0:T(8,128)(2,1)S(1)}, bf16[128,256]{1,0:T(8,128)(2,1)S(1)}, u32[]{:S(2)}, u32[]{:S(2)}) collective-permute-start(bf16[128,256]{1,0:T(8,128)(2,1)S(1)} %fusion.5.refs_0_), channel_id=1, source_target_pairs={{0,12},{1,13},{2,14},{3,15},{4,8},{5,9},{6,10},{7,11},{8,4},{9,5},... | collective-permute-start | bytes 196616 | tf_op jit(solution)/shard_map/ppermute | solution.py:126
  25.0 4.8 %collective-permute-start.12 = (bf16[128,256]{1,0:T(8,128)(2,1)S(1)}, bf16[128,256]{1,0:T(8,128)(2,1)S(1)}, u32[]{:S(2)}, u32[]{:S(2)}) collective-permute-start(bf16[128,256]{1,0:T(8,128)(2,1)S(1)} %fusion.5.refs_0_), channel_id=1, source_target_pairs={{0,8},{1,9},{2,10},{3,11},{4,12},{5,13},{6,14},{7,15},{8,0},{9,1},... | collective-permute-start | bytes 196616 | tf_op jit(solution)/shard_map/ppermute | solution.py:126
  25.1 4.9 %collective-permute-start.11 = (bf16[128,256]{1,0:T(8,128)(2,1)S(1)}, bf16[128,256]{1,0:T(8,128)(2,1)S(1)}, u32[]{:S(2)}, u32[]{:S(2)}) collective-permute-start(bf16[128,256]{1,0:T(8,128)(2,1)S(1)} %fusion.5.refs_0_), channel_id=1, source_target_pairs={{0,4},{1,5},{2,6},{3,7},{4,0},{5,1},{6,2},{7,3},{8,12},{9,13},{10,... | collective-permute-start | bytes 196616 | tf_op jit(solution)/shard_map/ppermute | solution.py:126
  26.2 4.9 %collective-permute-start.18 = (bf16[128,256]{1,0:T(8,128)(2,1)S(1)}, bf16[128,256]{1,0:T(8,128)(2,1)S(1)}, u32[]{:S(2)}, u32[]{:S(2)}) collective-permute-start(bf16[128,256]{1,0:T(8,128)(2,1)S(1)} %collective-permute-done.14), channel_id=1, source_target_pairs={{0,13},{1,12},{2,15},{3,14},{4,9},{5,8},{6,11},{7,10},{8,5},{9,4},... | collective-permute-start | bytes 196616 | tf_op jit(solution)/shard_map/ppermute | solution.py:126
  28.7 3.9 %collective-permute-start.17 = (bf16[128,256]{1,0:T(8,128)(2,1)S(1)}, bf16[128,256]{1,0:T(8,128)(2,1)S(1)}, u32[]{:S(2)}, u32[]{:S(2)}) collective-permute-start(bf16[128,256]{1,0:T(8,128)(2,1)S(1)} %collective-permute-done.14), channel_id=1, source_target_pairs={{0,9},{1,8},{2,11},{3,10},{4,13},{5,12},{6,15},{7,14},{8,1},{9,0},... | collective-permute-start | bytes 196616 | tf_op jit(solution)/shard_map/ppermute | solution.py:126
  28.7 4.0 %collective-permute-start.16 = (bf16[128,256]{1,0:T(8,128)(2,1)S(1)}, bf16[128,256]{1,0:T(8,128)(2,1)S(1)}, u32[]{:S(2)}, u32[]{:S(2)}) collective-permute-start(bf16[128,256]{1,0:T(8,128)(2,1)S(1)} %collective-permute-done.14), channel_id=1, source_target_pairs={{0,5},{1,4},{2,7},{3,6},{4,1},{5,0},{6,3},{7,2},{8,13},{9,12},{10,... | collective-permute-start | bytes 196616 | tf_op jit(solution)/shard_map/ppermute | solution.py:126
  29.7 2.9 %collective-permute-start.15 = (bf16[128,256]{1,0:T(8,128)(2,1)S(1)}, bf16[128,256]{1,0:T(8,128)(2,1)S(1)}, u32[]{:S(2)}, u32[]{:S(2)}) collective-permute-start(bf16[128,256]{1,0:T(8,128)(2,1)S(1)} %collective-permute-done.14), channel_id=1, source_target_pairs={{0,1},{1,0},{2,3},{3,2},{4,5},{5,4},{6,7},{7,6},{8,9},{9,8},{10,11... | collective-permute-start | bytes 196616 | tf_op jit(solution)/shard_map/ppermute | solution.py:126
  32.9 1.3 %collective-permute-start.20 = (bf16[128,256]{1,0:T(8,128)(2,1)S(1)}, bf16[128,256]{1,0:T(8,128)(2,1)S(1)}, u32[]{:S(2)}, u32[]{:S(2)}) collective-permute-start(bf16[128,256]{1,0:T(8,128)(2,1)S(1)} %late_first.4), channel_id=1, source_target_pairs={{0,1},{1,0},{2,3},{3,2},{4,5},{5,4},{6,7},{7,6},{8,9},{9,8},{10,11... | collective-permute-start | bytes 196616 | tf_op jit(solution)/shard_map/ppermute | solution.py:126
  33.5 2.5 %collective-permute-start.19 = (bf16[128,256]{1,0:T(8,128)(2,1)S(1)}, bf16[128,256]{1,0:T(8,128)(2,1)S(1)}, u32[]{:S(2)}, u32[]{:S(2)}) collective-permute-start(bf16[128,256]{1,0:T(8,128)(2,1)S(1)} %get-tuple-element.18), channel_id=1, source_target_pairs={{0,1},{1,0},{2,3},{3,2},{4,5},{5,4},{6,7},{7,6},{8,9},{9,8},{10,11... | collective-permute-start | bytes 196616 | tf_op jit(solution)/shard_map/ppermute | solution.py:126
  34.2 4.4 %collective-permute-start.21 = (bf16[128,256]{1,0:T(8,128)(2,1)S(1)}, bf16[128,256]{1,0:T(8,128)(2,1)S(1)}, u32[]{:S(2)}, u32[]{:S(2)}) collective-permute-start(bf16[128,256]{1,0:T(8,128)(2,1)S(1)} %add_convert_fusion.4), channel_id=1, source_target_pairs={{0,2},{1,3},{2,0},{3,1},{4,6},{5,7},{6,4},{7,5},{8,10},{9,11},{10,... | collective-permute-start | bytes 196616 | tf_op jit(solution)/shard_map/ppermute | solution.py:126
  38.8 5.5 %collective-permute-start.25 = (bf16[128,256]{1,0:T(8,128)(2,1)S(1)}, bf16[128,256]{1,0:T(8,128)(2,1)S(1)}, u32[]{:S(2)}, u32[]{:S(2)}) collective-permute-start(bf16[128,256]{1,0:T(8,128)(2,1)S(1)} %fusion.4.refs_0_), channel_id=1, source_target_pairs={{0,17},{1,16},{2,19},{3,18},{4,21},{5,20},{6,23},{7,22},{8,25},{9,... | collective-permute-start | bytes 196616 | tf_op jit(solution)/shard_map/ppermute | solution.py:126
  40.7 6.4 %collective-permute-start.24 = (bf16[128,256]{1,0:T(8,128)(2,1)S(1)}, bf16[128,256]{1,0:T(8,128)(2,1)S(1)}, u32[]{:S(2)}, u32[]{:S(2)}) collective-permute-start(bf16[128,256]{1,0:T(8,128)(2,1)S(1)} %fusion.4.refs_0_), channel_id=1, source_target_pairs={{0,12},{1,13},{2,14},{3,15},{4,8},{5,9},{6,10},{7,11},{8,4},{9,5},... | collective-permute-start | bytes 196616 | tf_op jit(solution)/shard_map/ppermute | solution.py:126
  43.3 4.7 %collective-permute-start.23 = (bf16[128,256]{1,0:T(8,128)(2,1)S(1)}, bf16[128,256]{1,0:T(8,128)(2,1)S(1)}, u32[]{:S(2)}, u32[]{:S(2)}) collective-permute-start(bf16[128,256]{1,0:T(8,128)(2,1)S(1)} %fusion.4.refs_0_), channel_id=1, source_target_pairs={{0,8},{1,9},{2,10},{3,11},{4,12},{5,13},{6,14},{7,15},{8,0},{9,1},... | collective-permute-start | bytes 196616 | tf_op jit(solution)/shard_map/ppermute | solution.py:126
  43.3 4.8 %collective-permute-start.22 = (bf16[128,256]{1,0:T(8,128)(2,1)S(1)}, bf16[128,256]{1,0:T(8,128)(2,1)S(1)}, u32[]{:S(2)}, u32[]{:S(2)}) collective-permute-start(bf16[128,256]{1,0:T(8,128)(2,1)S(1)} %fusion.4.refs_0_), channel_id=1, source_target_pairs={{0,4},{1,5},{2,6},{3,7},{4,0},{5,1},{6,2},{7,3},{8,12},{9,13},{10,... | collective-permute-start | bytes 196616 | tf_op jit(solution)/shard_map/ppermute | solution.py:126
  44.2 5.2 %collective-permute-start.29 = (bf16[128,256]{1,0:T(8,128)(2,1)S(1)}, bf16[128,256]{1,0:T(8,128)(2,1)S(1)}, u32[]{:S(2)}, u32[]{:S(2)}) collective-permute-start(bf16[128,256]{1,0:T(8,128)(2,1)S(1)} %collective-permute-done.25), channel_id=1, source_target_pairs={{0,13},{1,12},{2,15},{3,14},{4,9},{5,8},{6,11},{7,10},{8,5},{9,4},... | collective-permute-start | bytes 196616 | tf_op jit(solution)/shard_map/ppermute | solution.py:126
  47.1 4.4 %collective-permute-start.28 = (bf16[128,256]{1,0:T(8,128)(2,1)S(1)}, bf16[128,256]{1,0:T(8,128)(2,1)S(1)}, u32[]{:S(2)}, u32[]{:S(2)}) collective-permute-start(bf16[128,256]{1,0:T(8,128)(2,1)S(1)} %collective-permute-done.25), channel_id=1, source_target_pairs={{0,9},{1,8},{2,11},{3,10},{4,13},{5,12},{6,15},{7,14},{8,1},{9,0},... | collective-permute-start | bytes 196616 | tf_op jit(solution)/shard_map/ppermute | solution.py:126
  47.1 4.4 %collective-permute-start.27 = (bf16[128,256]{1,0:T(8,128)(2,1)S(1)}, bf16[128,256]{1,0:T(8,128)(2,1)S(1)}, u32[]{:S(2)}, u32[]{:S(2)}) collective-permute-start(bf16[128,256]{1,0:T(8,128)(2,1)S(1)} %collective-permute-done.25), channel_id=1, source_target_pairs={{0,5},{1,4},{2,7},{3,6},{4,1},{5,0},{6,3},{7,2},{8,13},{9,12},{10,... | collective-permute-start | bytes 196616 | tf_op jit(solution)/shard_map/ppermute | solution.py:126
  48.0 3.4 %collective-permute-start.26 = (bf16[128,256]{1,0:T(8,128)(2,1)S(1)}, bf16[128,256]{1,0:T(8,128)(2,1)S(1)}, u32[]{:S(2)}, u32[]{:S(2)}) collective-permute-start(bf16[128,256]{1,0:T(8,128)(2,1)S(1)} %collective-permute-done.25), channel_id=1, source_target_pairs={{0,1},{1,0},{2,3},{3,2},{4,5},{5,4},{6,7},{7,6},{8,9},{9,8},{10,11... | collective-permute-start | bytes 196616 | tf_op jit(solution)/shard_map/ppermute | solution.py:126
  51.7 1.3 %collective-permute-start.31 = (bf16[128,256]{1,0:T(8,128)(2,1)S(1)}, bf16[128,256]{1,0:T(8,128)(2,1)S(1)}, u32[]{:S(2)}, u32[]{:S(2)}) collective-permute-start(bf16[128,256]{1,0:T(8,128)(2,1)S(1)} %late_first.5), channel_id=1, source_target_pairs={{0,1},{1,0},{2,3},{3,2},{4,5},{5,4},{6,7},{7,6},{8,9},{9,8},{10,11... | collective-permute-start | bytes 196616 | tf_op jit(solution)/shard_map/ppermute | solution.py:126
  52.1 2.2 %collective-permute-start.30 = (bf16[128,256]{1,0:T(8,128)(2,1)S(1)}, bf16[128,256]{1,0:T(8,128)(2,1)S(1)}, u32[]{:S(2)}, u32[]{:S(2)}) collective-permute-start(bf16[128,256]{1,0:T(8,128)(2,1)S(1)} %get-tuple-element.21), channel_id=1, source_target_pairs={{0,1},{1,0},{2,3},{3,2},{4,5},{5,4},{6,7},{7,6},{8,9},{9,8},{10,11... | collective-permute-start | bytes 196616 | tf_op jit(solution)/shard_map/ppermute | solution.py:126
  53.0 4.3 %collective-permute-start.32 = (bf16[128,256]{1,0:T(8,128)(2,1)S(1)}, bf16[128,256]{1,0:T(8,128)(2,1)S(1)}, u32[]{:S(2)}, u32[]{:S(2)}) collective-permute-start(bf16[128,256]{1,0:T(8,128)(2,1)S(1)} %add_convert_fusion.1), channel_id=1, source_target_pairs={{0,2},{1,3},{2,0},{3,1},{4,6},{5,7},{6,4},{7,5},{8,10},{9,11},{10,... | collective-permute-start | bytes 196616 | tf_op jit(solution)/shard_map/ppermute | solution.py:126

commit v5 on v4

--- a/solution.py
+++ b/solution.py
@@ -9,42 +9,28 @@
 
 STEPS = 3
 ROW_TILES = 4
-CHUNK = 16
 UNROLL = 4
 LOCAL = 32
 BOTH = ("src", "tgt")
 
 
-def densify_kernel(places_ref, tiles_ref, out_ref, held_ref, total_ref, sems):
+def densify_kernel(places_ref, tiles_ref, out_ref, total_ref):
     group = pl.program_id(0)
-    slots, edge = held_ref.shape[:2]
+    slots, edge = tiles_ref.shape[2:4]
     places = total_ref.shape[0] - 1
     columns = out_ref.shape[1] // edge
     count = places_ref[slots]
-
-    def copy(c):
-        part = pl.ds(c * CHUNK, CHUNK)
-        return pltpu.make_async_copy(tiles_ref.at[0, 0, part], held_ref.at[part], sems.at[c])
-
-    for c in range(slots // CHUNK):
-        pl.when((group == 0) & (c * CHUNK < count))(lambda c=c: copy(c).start())
     total_ref[...] = jnp.zeros_like(total_ref)
 
-    def absorb(c):
-        pl.when(group == 0)(lambda: copy(c).wait())
+    def some(k, carry):
+        for i in range(UNROLL):
+            slot = k * UNROLL + i
+            place = places_ref[slot] - group * places
+            place = jnp.where((place >= 0) & (place < places), place, places)
+            total_ref[place] += tiles_ref[0, 0, slot].astype(jnp.float32)
+        return carry
 
-        def some(k, carry):
-            for i in range(UNROLL):
-                slot = c * CHUNK + k * UNROLL + i
-                place = places_ref[slot] - group * places
-                place = jnp.where((place >= 0) & (place < places), place, places)
-                total_ref[place] += held_ref[slot].astype(jnp.float32)
-            return carry
-
-        lax.fori_loop(0, CHUNK // UNROLL, some, 0)
-
-    for c in range(slots // CHUNK):
-        pl.when(c * CHUNK < count)(lambda c=c: absorb(c))
+    lax.fori_loop(0, pl.cdiv(count, UNROLL), some, 0)
     for place in range(places):
         i, j = divmod(place, columns)
         out_ref[i * edge:(i + 1) * edge, j * edge:(j + 1) * edge] = total_ref[place].astype(out_ref.dtype)
@@ -52,20 +38,18 @@
 
 def densify(places, tiles, n_rows, n_cols):
     slots, edge = tiles.shape[2:4]
-    assert slots % CHUNK == 0
+    assert slots % UNROLL == 0
     row_tiles = min(ROW_TILES, n_rows)
     return pl.pallas_call(
         densify_kernel,
         out_shape=jax.ShapeDtypeStruct((n_rows * edge, n_cols * edge), jnp.bfloat16),
         grid=(n_rows // row_tiles,),
-        in_specs=[pl.BlockSpec(memory_space=pltpu.SMEM), pl.BlockSpec(memory_space=pltpu.HBM)],
+        in_specs=[pl.BlockSpec(memory_space=pltpu.SMEM), pl.BlockSpec(memory_space=pltpu.VMEM)],
         out_specs=pl.BlockSpec((row_tiles * edge, n_cols * edge), lambda g: (g, 0)),
         scratch_shapes=[
-            pltpu.VMEM((slots, edge, edge), jnp.bfloat16),
             pltpu.VMEM((row_tiles * n_cols + 1, edge, edge), jnp.float32),
-            pltpu.SemaphoreType.DMA((slots // CHUNK,)),
         ],
-        compiler_params=pltpu.CompilerParams(vmem_limit_bytes=52 * 2**20),
+        compiler_params=pltpu.CompilerParams(vmem_limit_bytes=24 * 2**20),
         cost_estimate=pl.CostEstimate(flops=slots * edge * edge, bytes_accessed=2 * slots * edge * edge, transcendentals=0),
         name="densify",
     )(places, tiles)
@@ -89,6 +73,11 @@
             lhs = weights_ref[at, weights_ref.shape[1] - block.shape[0]:]
             term = jnp.dot(lhs, block, preferred_element_type=jnp.float32)
             out_ref[start:start + size] = (refs[0][at] + term if begun else term).astype(out_ref.dtype)
+
+
+def place_kernel(past, count_ref, place_ref, out_ref):
+    slot = lax.broadcasted_iota(jnp.int32, place_ref.shape, 1)
+    out_ref[...] = jnp.where(slot < count_ref[...], place_ref[...], past)
 
 
 def row_groups(rows):
@@ -146,11 +135,12 @@
                 beyond |= {k | m: swap(value, m, 0) for k, value in beyond.items() for m in masks}
         return [close[m] for m in sorted(close)], [beyond[m] for m in sorted(beyond)]
 
-    row, column = tile_target[0, 0] ^ lax.axis_index("tgt"), tile_source[0, 0] ^ lax.axis_index("src")
+    row, column = tile_target[0] ^ lax.axis_index("tgt"), tile_source[0] ^ lax.axis_index("src")
     row = sum(jnp.where(row & b != 0, n_tgt // (2 * b), 0) for b in tgt_bits)
-    live = jnp.arange(row.shape[0]) < tile_count[0, 0]
-    places = jnp.where(live, row * n_src + column, n_tgt * n_src)
-    weights = densify(jnp.concatenate([places, tile_count[0]]), tile_values, n_tgt, n_src)
+    places = local(
+        functools.partial(place_kernel, n_tgt * n_src), "places", jax.ShapeDtypeStruct(row.shape, jnp.int32), 2 * 10**10, tile_count, row * n_src + column
+    )
+    weights = densify(jnp.concatenate([places[0], tile_count[0]]), tile_values, n_tgt, n_src)
     openness = ((256.0 - stubborn.astype(jnp.float32)) / 256.0)[:, None]
     base = (1.0 - openness) * initial.astype(jnp.float32)
 

time: 58.1 us -> 57.7 us (level)
  Pallas kernels: 4.66 us -> 3.39 us
  waiting for transfers between devices: 16 us -> 17.2 us
    pallas_call x1, Pallas kernels: 2.52 us -> 1.19 us  [densify(): pl.pallas_call(densify_kernel, out_shape=jax.ShapeDtypeStruct((n_rows * e...]
    ppermute x33, waiting for transfers between devices: 16 us -> 17.2 us  [swap(): lax.ppermute(value, BOTH, [(d, d ^ mask) for d in range(n_src * n_tgt)])]
    pallas_call x8 -> x9, Pallas kernels: 2.14 us -> 2.2 us  [local(): pl.pallas_call(kernel, out_shape=out_shapes, in_specs=[whole] * len(args)...]
  transfers between devices with their start and end apart: 33 -> 33, of which waited for: 14 -> 15; matrix products, arithmetic and copies ran while one was open for 1% -> 1% of each run, Pallas kernels for 7% -> 5%
where the time goes in v5:
time: 57.7 us; the launch traced here: 57.5 us
  starting transfers between devices  34.2 us (59%)
  waiting for transfers between devices  17.2 us (30%)
  Pallas kernels  3.39 us (6%)
  matrix products  1.15 us (2%)
  other arithmetic  0.84 us (1%)
  between operations  0.79 us (1%)
    ppermute x33, starting transfers between devices, swap(): lax.ppermute(value, BOTH, [(d, d ^ mask) for d in range(n_src * n_tgt)])  34.2 us
    ppermute x33, waiting for transfers between devices, swap(): lax.ppermute(value, BOTH, [(d, d ^ mask) for d in range(n_src * n_tgt)])  17.2 us
    pallas_call x9, Pallas kernels, local(): pl.pallas_call(kernel, out_shape=out_shapes, in_specs=[whole] * len(args)...  2.2 us
    pallas_call x1, Pallas kernels, densify(): pl.pallas_call(densify_kernel, out_shape=jax.ShapeDtypeStruct((n_rows * e...  1.19 us
  transfers between devices with their start and end apart: 33, of which 15 were waited for; matrix products, arithmetic and copies ran while one was open for 1% of the time, Pallas kernels for 5%

profile of v5, /device:TPU:0, one launch (start us, length us, event | category | flops | bytes accessed | tf_op | source)
XLA Modules:
  0.0 57.5 jit_solution(12692422022277228737)
XLA Ops:
  0.0 3.5 %collective-permute-start.3 = (bf16[128,256]{1,0:T(8,128)(2,1)}, bf16[128,256]{1,0:T(8,128)(2,1)S(1)}, u32[]{:S(2)}, u32[]{:S(2)}) collective-permute-start(bf16[128,256]{1,0:T(8,128)(2,1)} %refs_0_.3), channel_id=1, source_target_pairs={{0,17},{1,16},{2,19},{3,18},{4,21},{5,20},{6,23},{7,22},{8,25},{9,... | collective-permute-start | bytes 196616 | tf_op jit(solution)/shard_map/ppermute | solution.py:115
  3.5 2.5 %collective-permute-start.2 = (bf16[128,256]{1,0:T(8,128)(2,1)}, bf16[128,256]{1,0:T(8,128)(2,1)S(1)}, u32[]{:S(2)}, u32[]{:S(2)}) collective-permute-start(bf16[128,256]{1,0:T(8,128)(2,1)} %refs_0_.3), channel_id=1, source_target_pairs={{0,12},{1,13},{2,14},{3,15},{4,8},{5,9},{6,10},{7,11},{8,4},{9,5},... | collective-permute-start | bytes 196616 | tf_op jit(solution)/shard_map/ppermute | solution.py:115
  6.0 0.4 collective-permute-start.1
  6.4 0.5 collective-permute-start
  7.6 0.7 %add_bitcast_fusion.place_ref = s32[1,144]{1,0:T(1,128)S(1)} fusion(s32[1,1,144]{2,1,0:T(1,128)} %param.12, s32[1,1,144]{2,1,0:T(1,128)} %param.11, s32[]{:T(128)S(6)} %axis_index.25, s32[]{:T(128)S(6)} %axis_index.22), kind=kLoop, calls=%fused_computation.23 | loop fusion | flops 1584 | bytes 1736 | tf_op jit(solution)/shard_map/add | solution.py:141
  8.4 2.0 %collective-permute-start.7 = (bf16[128,256]{1,0:T(8,128)(2,1)S(1)}, bf16[128,256]{1,0:T(8,128)(2,1)S(1)}, u32[]{:S(2)}, u32[]{:S(2)}) collective-permute-start(bf16[128,256]{1,0:T(8,128)(2,1)S(1)} %collective-permute-done.3), channel_id=1, source_target_pairs={{0,13},{1,12},{2,15},{3,14},{4,9},{5,8},{6,11},{7,10},{8,5},{9,4},... | collective-permute-start | bytes 196616 | tf_op jit(solution)/shard_map/ppermute | solution.py:115
  10.5 0.7 %collective-permute-start.6 = (bf16[128,256]{1,0:T(8,128)(2,1)S(1)}, bf16[128,256]{1,0:T(8,128)(2,1)S(1)}, u32[]{:S(2)}, u32[]{:S(2)}) collective-permute-start(bf16[128,256]{1,0:T(8,128)(2,1)S(1)} %collective-permute-done.3), channel_id=1, source_target_pairs={{0,9},{1,8},{2,11},{3,10},{4,13},{5,12},{6,15},{7,14},{8,1},{9,0},... | collective-permute-start | bytes 196616 | tf_op jit(solution)/shard_map/ppermute | solution.py:115
  11.4 0.5 collective-permute-start.4
  11.9 1.2 %densify.1.weights_ref = bf16[512,1024]{1,0:T(8,128)(2,1)S(1)} custom-call(s32[145]{0:T(256)S(1)} %pad_add_fusion.places_ref, bf16[1,1,144,128,128]{4,3,2,1,0:T(8,128)(2,1)S(1)} %copy-done.1), custom_call_target="tpu_custom_call" | custom-call | flops 2359296 | bytes 4718592 | tf_op jit(solution)/shard_map/densify/pallas_call | solution.py:43
  13.1 0.5 collective-permute-done.7.refs_7_
  13.6 1.1 %collective-permute-done.6.refs_6_ = bf16[128,256]{1,0:T(8,128)(2,1)S(1)} collective-permute-done((bf16[128,256]{1,0:T(8,128)(2,1)S(1)}, bf16[128,256]{1,0:T(8,128)(2,1)S(1)}, u32[]{:S(2)}, u32[]{:S(2)}) %collective-permute-start.6) | collective-permute-done | bytes 65568 | tf_op jit(solution)/shard_map/ppermute | solution.py:115
  14.7 0.7 %collective-permute-done.5.refs_5_ = bf16[128,256]{1,0:T(8,128)(2,1)S(1)} collective-permute-done((bf16[128,256]{1,0:T(8,128)(2,1)S(1)}, bf16[128,256]{1,0:T(8,128)(2,1)S(1)}, u32[]{:S(2)}, u32[]{:S(2)}) %collective-permute-start.5) | collective-permute-done | bytes 65568 | tf_op jit(solution)/shard_map/ppermute | solution.py:115
  15.4 0.2 late_first.3
  15.8 0.4 late_rest.3
  16.2 0.5 collective-permute-start.8
  16.7 0.3 collective-permute-done.9
  17.0 1.6 %collective-permute-start.10 = (bf16[128,256]{1,0:T(8,128)(2,1)S(1)}, bf16[128,256]{1,0:T(8,128)(2,1)S(1)}, u32[]{:S(2)}, u32[]{:S(2)}) collective-permute-start(bf16[128,256]{1,0:T(8,128)(2,1)S(1)} %add_convert_fusion.7), channel_id=1, source_target_pairs={{0,2},{1,3},{2,0},{3,1},{4,6},{5,7},{6,4},{7,5},{8,10},{9,11},{10,... | collective-permute-start | bytes 196616 | tf_op jit(solution)/shard_map/ppermute | solution.py:115
  18.6 2.7 %collective-permute-done.10 = bf16[128,256]{1,0:T(8,128)(2,1)S(1)} collective-permute-done((bf16[128,256]{1,0:T(8,128)(2,1)S(1)}, bf16[128,256]{1,0:T(8,128)(2,1)S(1)}, u32[]{:S(2)}, u32[]{:S(2)}) %collective-permute-start.10) | collective-permute-done | bytes 65568 | tf_op jit(solution)/shard_map/ppermute | solution.py:115
  21.5 0.9 %collective-permute-start.14 = (bf16[128,256]{1,0:T(8,128)(2,1)S(1)}, bf16[128,256]{1,0:T(8,128)(2,1)S(1)}, u32[]{:S(2)}, u32[]{:S(2)}) collective-permute-start(bf16[128,256]{1,0:T(8,128)(2,1)S(1)} %fusion.5.refs_0_), channel_id=1, source_target_pairs={{0,17},{1,16},{2,19},{3,18},{4,21},{5,20},{6,23},{7,22},{8,25},{9,... | collective-permute-start | bytes 196616 | tf_op jit(solution)/shard_map/ppermute | solution.py:115
  22.4 2.5 %collective-permute-start.13 = (bf16[128,256]{1,0:T(8,128)(2,1)S(1)}, bf16[128,256]{1,0:T(8,128)(2,1)S(1)}, u32[]{:S(2)}, u32[]{:S(2)}) collective-permute-start(bf16[128,256]{1,0:T(8,128)(2,1)S(1)} %fusion.5.refs_0_), channel_id=1, source_target_pairs={{0,12},{1,13},{2,14},{3,15},{4,8},{5,9},{6,10},{7,11},{8,4},{9,5},... | collective-permute-start | bytes 196616 | tf_op jit(solution)/shard_map/ppermute | solution.py:115
  24.9 1.0 %collective-permute-start.11 = (bf16[128,256]{1,0:T(8,128)(2,1)S(1)}, bf16[128,256]{1,0:T(8,128)(2,1)S(1)}, u32[]{:S(2)}, u32[]{:S(2)}) collective-permute-start(bf16[128,256]{1,0:T(8,128)(2,1)S(1)} %fusion.5.refs_0_), channel_id=1, source_target_pairs={{0,4},{1,5},{2,6},{3,7},{4,0},{5,1},{6,2},{7,3},{8,12},{9,13},{10,... | collective-permute-start | bytes 196616 | tf_op jit(solution)/shard_map/ppermute | solution.py:115
  25.9 0.3 collective-permute-done.14
  26.2 2.6 %collective-permute-start.18 = (bf16[128,256]{1,0:T(8,128)(2,1)S(1)}, bf16[128,256]{1,0:T(8,128)(2,1)S(1)}, u32[]{:S(2)}, u32[]{:S(2)}) collective-permute-start(bf16[128,256]{1,0:T(8,128)(2,1)S(1)} %collective-permute-done.14), channel_id=1, source_target_pairs={{0,13},{1,12},{2,15},{3,14},{4,9},{5,8},{6,11},{7,10},{8,5},{9,4},... | collective-permute-start | bytes 196616 | tf_op jit(solution)/shard_map/ppermute | solution.py:115
  28.8 1.0 %collective-permute-start.16 = (bf16[128,256]{1,0:T(8,128)(2,1)S(1)}, bf16[128,256]{1,0:T(8,128)(2,1)S(1)}, u32[]{:S(2)}, u32[]{:S(2)}) collective-permute-start(bf16[128,256]{1,0:T(8,128)(2,1)S(1)} %collective-permute-done.14), channel_id=1, source_target_pairs={{0,5},{1,4},{2,7},{3,6},{4,1},{5,0},{6,3},{7,2},{8,13},{9,12},{10,... | collective-permute-start | bytes 196616 | tf_op jit(solution)/shard_map/ppermute | solution.py:115
  29.7 0.3 early.2.refs_0_
  30.0 1.2 %collective-permute-done.18.refs_4_ = bf16[128,256]{1,0:T(8,128)(2,1)S(1)} collective-permute-done((bf16[128,256]{1,0:T(8,128)(2,1)S(1)}, bf16[128,256]{1,0:T(8,128)(2,1)S(1)}, u32[]{:S(2)}, u32[]{:S(2)}) %collective-permute-start.18) | collective-permute-done | bytes 65568 | tf_op jit(solution)/shard_map/ppermute | solution.py:115
  31.2 1.4 %collective-permute-done.17.refs_3_ = bf16[128,256]{1,0:T(8,128)(2,1)S(1)} collective-permute-done((bf16[128,256]{1,0:T(8,128)(2,1)S(1)}, bf16[128,256]{1,0:T(8,128)(2,1)S(1)}, u32[]{:S(2)}, u32[]{:S(2)}) %collective-permute-start.17) | collective-permute-done | bytes 65568 | tf_op jit(solution)/shard_map/ppermute | solution.py:115
  32.8 0.4 collective-permute-start.20
  33.2 0.3 late_rest.4
  33.5 0.2 collective-permute-start.19
  33.7 0.4 collective-permute-done.20
  34.2 1.6 %collective-permute-start.21 = (bf16[128,256]{1,0:T(8,128)(2,1)S(1)}, bf16[128,256]{1,0:T(8,128)(2,1)S(1)}, u32[]{:S(2)}, u32[]{:S(2)}) collective-permute-start(bf16[128,256]{1,0:T(8,128)(2,1)S(1)} %add_convert_fusion.4), channel_id=1, source_target_pairs={{0,2},{1,3},{2,0},{3,1},{4,6},{5,7},{6,4},{7,5},{8,10},{9,11},{10,... | collective-permute-start | bytes 196616 | tf_op jit(solution)/shard_map/ppermute | solution.py:115
  35.8 2.8 %collective-permute-done.21 = bf16[128,256]{1,0:T(8,128)(2,1)S(1)} collective-permute-done((bf16[128,256]{1,0:T(8,128)(2,1)S(1)}, bf16[128,256]{1,0:T(8,128)(2,1)S(1)}, u32[]{:S(2)}, u32[]{:S(2)}) %collective-permute-start.21) | collective-permute-done | bytes 65568 | tf_op jit(solution)/shard_map/ppermute | solution.py:115
  38.8 1.3 %collective-permute-start.25 = (bf16[128,256]{1,0:T(8,128)(2,1)S(1)}, bf16[128,256]{1,0:T(8,128)(2,1)S(1)}, u32[]{:S(2)}, u32[]{:S(2)}) collective-permute-start(bf16[128,256]{1,0:T(8,128)(2,1)S(1)} %fusion.4.refs_0_), channel_id=1, source_target_pairs={{0,17},{1,16},{2,19},{3,18},{4,21},{5,20},{6,23},{7,22},{8,25},{9,... | collective-permute-start | bytes 196616 | tf_op jit(solution)/shard_map/ppermute | solution.py:115
  40.0 2.8 %collective-permute-start.24 = (bf16[128,256]{1,0:T(8,128)(2,1)S(1)}, bf16[128,256]{1,0:T(8,128)(2,1)S(1)}, u32[]{:S(2)}, u32[]{:S(2)}) collective-permute-start(bf16[128,256]{1,0:T(8,128)(2,1)S(1)} %fusion.4.refs_0_), channel_id=1, source_target_pairs={{0,12},{1,13},{2,14},{3,15},{4,8},{5,9},{6,10},{7,11},{8,4},{9,5},... | collective-permute-start | bytes 196616 | tf_op jit(solution)/shard_map/ppermute | solution.py:115
  42.9 1.1 %collective-permute-start.22 = (bf16[128,256]{1,0:T(8,128)(2,1)S(1)}, bf16[128,256]{1,0:T(8,128)(2,1)S(1)}, u32[]{:S(2)}, u32[]{:S(2)}) collective-permute-start(bf16[128,256]{1,0:T(8,128)(2,1)S(1)} %fusion.4.refs_0_), channel_id=1, source_target_pairs={{0,4},{1,5},{2,6},{3,7},{4,0},{5,1},{6,2},{7,3},{8,12},{9,13},{10,... | collective-permute-start | bytes 196616 | tf_op jit(solution)/shard_map/ppermute | solution.py:115
  44.1 2.7 %collective-permute-start.29 = (bf16[128,256]{1,0:T(8,128)(2,1)S(1)}, bf16[128,256]{1,0:T(8,128)(2,1)S(1)}, u32[]{:S(2)}, u32[]{:S(2)}) collective-permute-start(bf16[128,256]{1,0:T(8,128)(2,1)S(1)} %collective-permute-done.25), channel_id=1, source_target_pairs={{0,13},{1,12},{2,15},{3,14},{4,9},{5,8},{6,11},{7,10},{8,5},{9,4},... | collective-permute-start | bytes 196616 | tf_op jit(solution)/shard_map/ppermute | solution.py:115
  46.8 1.0 %collective-permute-start.27 = (bf16[128,256]{1,0:T(8,128)(2,1)S(1)}, bf16[128,256]{1,0:T(8,128)(2,1)S(1)}, u32[]{:S(2)}, u32[]{:S(2)}) collective-permute-start(bf16[128,256]{1,0:T(8,128)(2,1)S(1)} %collective-permute-done.25), channel_id=1, source_target_pairs={{0,5},{1,4},{2,7},{3,6},{4,1},{5,0},{6,3},{7,2},{8,13},{9,12},{10,... | collective-permute-start | bytes 196616 | tf_op jit(solution)/shard_map/ppermute | solution.py:115
  48.0 0.3 early.3.refs_0_
  48.3 1.0 %collective-permute-done.29.refs_4_ = bf16[128,256]{1,0:T(8,128)(2,1)S(1)} collective-permute-done((bf16[128,256]{1,0:T(8,128)(2,1)S(1)}, bf16[128,256]{1,0:T(8,128)(2,1)S(1)}, u32[]{:S(2)}, u32[]{:S(2)}) %collective-permute-start.29) | collective-permute-done | bytes 65568 | tf_op jit(solution)/shard_map/ppermute | solution.py:115
  49.3 1.4 %collective-permute-done.28.refs_3_ = bf16[128,256]{1,0:T(8,128)(2,1)S(1)} collective-permute-done((bf16[128,256]{1,0:T(8,128)(2,1)S(1)}, bf16[128,256]{1,0:T(8,128)(2,1)S(1)}, u32[]{:S(2)}, u32[]{:S(2)}) %collective-permute-start.28) | collective-permute-done | bytes 65568 | tf_op jit(solution)/shard_map/ppermute | solution.py:115
  51.0 0.4 collective-permute-start.31
  51.4 0.3 late_rest.5
  51.7 0.3 collective-permute-start.30
  52.0 0.4 collective-permute-done.31
  52.4 1.6 %collective-permute-start.32 = (bf16[128,256]{1,0:T(8,128)(2,1)S(1)}, bf16[128,256]{1,0:T(8,128)(2,1)S(1)}, u32[]{:S(2)}, u32[]{:S(2)}) collective-permute-start(bf16[128,256]{1,0:T(8,128)(2,1)S(1)} %add_convert_fusion.1), channel_id=1, source_target_pairs={{0,2},{1,3},{2,0},{3,1},{4,6},{5,7},{6,4},{7,5},{8,10},{9,11},{10,... | collective-permute-start | bytes 196616 | tf_op jit(solution)/shard_map/ppermute | solution.py:115
  54.0 2.8 %collective-permute-done.32 = bf16[128,256]{1,0:T(8,128)(2,1)S(1)} collective-permute-done((bf16[128,256]{1,0:T(8,128)(2,1)S(1)}, bf16[128,256]{1,0:T(8,128)(2,1)S(1)}, u32[]{:S(2)}, u32[]{:S(2)}) %collective-permute-start.32) | collective-permute-done | bytes 65568 | tf_op jit(solution)/shard_map/ppermute | solution.py:115
  56.7 0.8 %fusion.3 = bf16[128,256]{1,0:T(8,128)(2,1)} fusion(bf16[256,256]{1,0:T(8,128)(2,1)S(1)} %copy-done, bf16[128,256]{1,0:T(8,128)(2,1)S(1)} %copy-done.2, bf16[128,256]{1,0:T(8,128)(2,1)S(1)} %collective-permute-done.32, bf16[128,256]{1,0:T(8,128)(2,1)S(1)} %collective-permute-done.30, bf16[128,256]{1,0:T(8,128)(2,1)S(1)} %get-tuple-element.20, ...), kind=kOutput, calls=%fused_computation.6 | convolution fusion | flops 17203200 | bytes 459776 | tf_op jit(solution)/shard_map/dot_general | solution.py:172
  (45 shorter events, 1.9 us)
Async XLA Ops:
  0.0 21.3 %copy-start = (bf16[256,256]{1,0:T(8,128)(2,1)S(1)}, bf16[256,256]{1,0:T(8,128)(2,1)}, u32[]{:S(2)}) copy-start(bf16[256,256]{1,0:T(8,128)(2,1)} %param.9) | copy-start | bytes 393220
  0.0 8.4 %collective-permute-start.3 = (bf16[128,256]{1,0:T(8,128)(2,1)}, bf16[128,256]{1,0:T(8,128)(2,1)S(1)}, u32[]{:S(2)}, u32[]{:S(2)}) collective-permute-start(bf16[128,256]{1,0:T(8,128)(2,1)} %refs_0_.3), channel_id=1, source_target_pairs={{0,17},{1,16},{2,19},{3,18},{4,21},{5,20},{6,23},{7,22},{8,25},{9,... | collective-permute-start | bytes 196616 | tf_op jit(solution)/shard_map/ppermute | solution.py:115
  3.5 7.7 %collective-permute-start.2 = (bf16[128,256]{1,0:T(8,128)(2,1)}, bf16[128,256]{1,0:T(8,128)(2,1)S(1)}, u32[]{:S(2)}, u32[]{:S(2)}) collective-permute-start(bf16[128,256]{1,0:T(8,128)(2,1)} %refs_0_.3), channel_id=1, source_target_pairs={{0,12},{1,13},{2,14},{3,15},{4,8},{5,9},{6,10},{7,11},{8,4},{9,5},... | collective-permute-start | bytes 196616 | tf_op jit(solution)/shard_map/ppermute | solution.py:115
  6.0 5.4 %collective-permute-start.1 = (bf16[128,256]{1,0:T(8,128)(2,1)}, bf16[128,256]{1,0:T(8,128)(2,1)S(1)}, u32[]{:S(2)}, u32[]{:S(2)}) collective-permute-start(bf16[128,256]{1,0:T(8,128)(2,1)} %refs_0_.3), channel_id=1, source_target_pairs={{0,8},{1,9},{2,10},{3,11},{4,12},{5,13},{6,14},{7,15},{8,0},{9,1},... | collective-permute-start | bytes 196616 | tf_op jit(solution)/shard_map/ppermute | solution.py:115
  6.4 6.7 %collective-permute-start = (bf16[128,256]{1,0:T(8,128)(2,1)}, bf16[128,256]{1,0:T(8,128)(2,1)S(1)}, u32[]{:S(2)}, u32[]{:S(2)}) collective-permute-start(bf16[128,256]{1,0:T(8,128)(2,1)} %refs_0_.3), channel_id=1, source_target_pairs={{0,4},{1,5},{2,6},{3,7},{4,0},{5,1},{6,2},{7,3},{8,12},{9,13},{10,... | collective-permute-start | bytes 196616 | tf_op jit(solution)/shard_map/ppermute | solution.py:115
  8.3 3.6 %copy-start.1 = (bf16[1,1,144,128,128]{4,3,2,1,0:T(8,128)(2,1)S(1)}, bf16[1,1,144,128,128]{4,3,2,1,0:T(8,128)(2,1)}, u32[]{:S(2)}) copy-start(bf16[1,1,144,128,128]{4,3,2,1,0:T(8,128)(2,1)} %tiles_ref.1) | copy-start | bytes 14155780
  8.4 7.0 %copy-start.2 = (bf16[128,256]{1,0:T(8,128)(2,1)S(1)}, bf16[128,256]{1,0:T(8,128)(2,1)}, u32[]{:S(2)}) copy-start(bf16[128,256]{1,0:T(8,128)(2,1)} %refs_0_.3) | copy-start | bytes 196612
  8.4 10.1 %copy-start.3 = (s32[128]{0:T(128)S(1)}, s32[128]{0:T(128)}, u32[]{:S(2)}) copy-start(s32[128]{0:T(128)} %param.8) | copy-start | bytes 1540
  8.4 5.2 %collective-permute-start.7 = (bf16[128,256]{1,0:T(8,128)(2,1)S(1)}, bf16[128,256]{1,0:T(8,128)(2,1)S(1)}, u32[]{:S(2)}, u32[]{:S(2)}) collective-permute-start(bf16[128,256]{1,0:T(8,128)(2,1)S(1)} %collective-permute-done.3), channel_id=1, source_target_pairs={{0,13},{1,12},{2,15},{3,14},{4,9},{5,8},{6,11},{7,10},{8,5},{9,4},... | collective-permute-start | bytes 196616 | tf_op jit(solution)/shard_map/ppermute | solution.py:115
  10.5 4.2 %collective-permute-start.6 = (bf16[128,256]{1,0:T(8,128)(2,1)S(1)}, bf16[128,256]{1,0:T(8,128)(2,1)S(1)}, u32[]{:S(2)}, u32[]{:S(2)}) collective-permute-start(bf16[128,256]{1,0:T(8,128)(2,1)S(1)} %collective-permute-done.3), channel_id=1, source_target_pairs={{0,9},{1,8},{2,11},{3,10},{4,13},{5,12},{6,15},{7,14},{8,1},{9,0},... | collective-permute-start | bytes 196616 | tf_op jit(solution)/shard_map/ppermute | solution.py:115
  11.2 4.2 %collective-permute-start.5 = (bf16[128,256]{1,0:T(8,128)(2,1)S(1)}, bf16[128,256]{1,0:T(8,128)(2,1)S(1)}, u32[]{:S(2)}, u32[]{:S(2)}) collective-permute-start(bf16[128,256]{1,0:T(8,128)(2,1)S(1)} %collective-permute-done.3), channel_id=1, source_target_pairs={{0,5},{1,4},{2,7},{3,6},{4,1},{5,0},{6,3},{7,2},{8,13},{9,12},{10,... | collective-permute-start | bytes 196616 | tf_op jit(solution)/shard_map/ppermute | solution.py:115
  11.4 4.0 %collective-permute-start.4 = (bf16[128,256]{1,0:T(8,128)(2,1)S(1)}, bf16[128,256]{1,0:T(8,128)(2,1)S(1)}, u32[]{:S(2)}, u32[]{:S(2)}) collective-permute-start(bf16[128,256]{1,0:T(8,128)(2,1)S(1)} %collective-permute-done.3), channel_id=1, source_target_pairs={{0,1},{1,0},{2,3},{3,2},{4,5},{5,4},{6,7},{7,6},{8,9},{9,8},{10,11... | collective-permute-start | bytes 196616 | tf_op jit(solution)/shard_map/ppermute | solution.py:115
  15.6 1.3 %collective-permute-start.9 = (bf16[128,256]{1,0:T(8,128)(2,1)S(1)}, bf16[128,256]{1,0:T(8,128)(2,1)S(1)}, u32[]{:S(2)}, u32[]{:S(2)}) collective-permute-start(bf16[128,256]{1,0:T(8,128)(2,1)S(1)} %late_first.3), channel_id=1, source_target_pairs={{0,1},{1,0},{2,3},{3,2},{4,5},{5,4},{6,7},{7,6},{8,9},{9,8},{10,11... | collective-permute-start | bytes 196616 | tf_op jit(solution)/shard_map/ppermute | solution.py:115
  16.2 2.4 %collective-permute-start.8 = (bf16[128,256]{1,0:T(8,128)(2,1)S(1)}, bf16[128,256]{1,0:T(8,128)(2,1)S(1)}, u32[]{:S(2)}, u32[]{:S(2)}) collective-permute-start(bf16[128,256]{1,0:T(8,128)(2,1)S(1)} %get-tuple-element.15), channel_id=1, source_target_pairs={{0,1},{1,0},{2,3},{3,2},{4,5},{5,4},{6,7},{7,6},{8,9},{9,8},{10,11... | collective-permute-start | bytes 196616 | tf_op jit(solution)/shard_map/ppermute | solution.py:115
  17.0 4.3 %collective-permute-start.10 = (bf16[128,256]{1,0:T(8,128)(2,1)S(1)}, bf16[128,256]{1,0:T(8,128)(2,1)S(1)}, u32[]{:S(2)}, u32[]{:S(2)}) collective-permute-start(bf16[128,256]{1,0:T(8,128)(2,1)S(1)} %add_convert_fusion.7), channel_id=1, source_target_pairs={{0,2},{1,3},{2,0},{3,1},{4,6},{5,7},{6,4},{7,5},{8,10},{9,11},{10,... | collective-permute-start | bytes 196616 | tf_op jit(solution)/shard_map/ppermute | solution.py:115
  21.5 4.7 %collective-permute-start.14 = (bf16[128,256]{1,0:T(8,128)(2,1)S(1)}, bf16[128,256]{1,0:T(8,128)(2,1)S(1)}, u32[]{:S(2)}, u32[]{:S(2)}) collective-permute-start(bf16[128,256]{1,0:T(8,128)(2,1)S(1)} %fusion.5.refs_0_), channel_id=1, source_target_pairs={{0,17},{1,16},{2,19},{3,18},{4,21},{5,20},{6,23},{7,22},{8,25},{9,... | collective-permute-start | bytes 196616 | tf_op jit(solution)/shard_map/ppermute | solution.py:115
  22.4 6.4 %collective-permute-start.13 = (bf16[128,256]{1,0:T(8,128)(2,1)S(1)}, bf16[128,256]{1,0:T(8,128)(2,1)S(1)}, u32[]{:S(2)}, u32[]{:S(2)}) collective-permute-start(bf16[128,256]{1,0:T(8,128)(2,1)S(1)} %fusion.5.refs_0_), channel_id=1, source_target_pairs={{0,12},{1,13},{2,14},{3,15},{4,8},{5,9},{6,10},{7,11},{8,4},{9,5},... | collective-permute-start | bytes 196616 | tf_op jit(solution)/shard_map/ppermute | solution.py:115
  24.9 4.8 %collective-permute-start.12 = (bf16[128,256]{1,0:T(8,128)(2,1)S(1)}, bf16[128,256]{1,0:T(8,128)(2,1)S(1)}, u32[]{:S(2)}, u32[]{:S(2)}) collective-permute-start(bf16[128,256]{1,0:T(8,128)(2,1)S(1)} %fusion.5.refs_0_), channel_id=1, source_target_pairs={{0,8},{1,9},{2,10},{3,11},{4,12},{5,13},{6,14},{7,15},{8,0},{9,1},... | collective-permute-start | bytes 196616 | tf_op jit(solution)/shard_map/ppermute | solution.py:115
  24.9 4.8 %collective-permute-start.11 = (bf16[128,256]{1,0:T(8,128)(2,1)S(1)}, bf16[128,256]{1,0:T(8,128)(2,1)S(1)}, u32[]{:S(2)}, u32[]{:S(2)}) collective-permute-start(bf16[128,256]{1,0:T(8,128)(2,1)S(1)} %fusion.5.refs_0_), channel_id=1, source_target_pairs={{0,4},{1,5},{2,6},{3,7},{4,0},{5,1},{6,2},{7,3},{8,12},{9,13},{10,... | collective-permute-start | bytes 196616 | tf_op jit(solution)/shard_map/ppermute | solution.py:115
  26.2 5.1 %collective-permute-start.18 = (bf16[128,256]{1,0:T(8,128)(2,1)S(1)}, bf16[128,256]{1,0:T(8,128)(2,1)S(1)}, u32[]{:S(2)}, u32[]{:S(2)}) collective-permute-start(bf16[128,256]{1,0:T(8,128)(2,1)S(1)} %collective-permute-done.14), channel_id=1, source_target_pairs={{0,13},{1,12},{2,15},{3,14},{4,9},{5,8},{6,11},{7,10},{8,5},{9,4},... | collective-permute-start | bytes 196616 | tf_op jit(solution)/shard_map/ppermute | solution.py:115
  28.8 3.8 %collective-permute-start.17 = (bf16[128,256]{1,0:T(8,128)(2,1)S(1)}, bf16[128,256]{1,0:T(8,128)(2,1)S(1)}, u32[]{:S(2)}, u32[]{:S(2)}) collective-permute-start(bf16[128,256]{1,0:T(8,128)(2,1)S(1)} %collective-permute-done.14), channel_id=1, source_target_pairs={{0,9},{1,8},{2,11},{3,10},{4,13},{5,12},{6,15},{7,14},{8,1},{9,0},... | collective-permute-start | bytes 196616 | tf_op jit(solution)/shard_map/ppermute | solution.py:115
  28.8 3.8 %collective-permute-start.16 = (bf16[128,256]{1,0:T(8,128)(2,1)S(1)}, bf16[128,256]{1,0:T(8,128)(2,1)S(1)}, u32[]{:S(2)}, u32[]{:S(2)}) collective-permute-start(bf16[128,256]{1,0:T(8,128)(2,1)S(1)} %collective-permute-done.14), channel_id=1, source_target_pairs={{0,5},{1,4},{2,7},{3,6},{4,1},{5,0},{6,3},{7,2},{8,13},{9,12},{10,... | collective-permute-start | bytes 196616 | tf_op jit(solution)/shard_map/ppermute | solution.py:115
  29.7 2.9 %collective-permute-start.15 = (bf16[128,256]{1,0:T(8,128)(2,1)S(1)}, bf16[128,256]{1,0:T(8,128)(2,1)S(1)}, u32[]{:S(2)}, u32[]{:S(2)}) collective-permute-start(bf16[128,256]{1,0:T(8,128)(2,1)S(1)} %collective-permute-done.14), channel_id=1, source_target_pairs={{0,1},{1,0},{2,3},{3,2},{4,5},{5,4},{6,7},{7,6},{8,9},{9,8},{10,11... | collective-permute-start | bytes 196616 | tf_op jit(solution)/shard_map/ppermute | solution.py:115
  32.8 1.3 %collective-permute-start.20 = (bf16[128,256]{1,0:T(8,128)(2,1)S(1)}, bf16[128,256]{1,0:T(8,128)(2,1)S(1)}, u32[]{:S(2)}, u32[]{:S(2)}) collective-permute-start(bf16[128,256]{1,0:T(8,128)(2,1)S(1)} %late_first.4), channel_id=1, source_target_pairs={{0,1},{1,0},{2,3},{3,2},{4,5},{5,4},{6,7},{7,6},{8,9},{9,8},{10,11... | collective-permute-start | bytes 196616 | tf_op jit(solution)/shard_map/ppermute | solution.py:115
  33.5 2.2 %collective-permute-start.19 = (bf16[128,256]{1,0:T(8,128)(2,1)S(1)}, bf16[128,256]{1,0:T(8,128)(2,1)S(1)}, u32[]{:S(2)}, u32[]{:S(2)}) collective-permute-start(bf16[128,256]{1,0:T(8,128)(2,1)S(1)} %get-tuple-element.18), channel_id=1, source_target_pairs={{0,1},{1,0},{2,3},{3,2},{4,5},{5,4},{6,7},{7,6},{8,9},{9,8},{10,11... | collective-permute-start | bytes 196616 | tf_op jit(solution)/shard_map/ppermute | solution.py:115
  34.2 4.4 %collective-permute-start.21 = (bf16[128,256]{1,0:T(8,128)(2,1)S(1)}, bf16[128,256]{1,0:T(8,128)(2,1)S(1)}, u32[]{:S(2)}, u32[]{:S(2)}) collective-permute-start(bf16[128,256]{1,0:T(8,128)(2,1)S(1)} %add_convert_fusion.4), channel_id=1, source_target_pairs={{0,2},{1,3},{2,0},{3,1},{4,6},{5,7},{6,4},{7,5},{8,10},{9,11},{10,... | collective-permute-start | bytes 196616 | tf_op jit(solution)/shard_map/ppermute | solution.py:115
  38.8 5.3 %collective-permute-start.25 = (bf16[128,256]{1,0:T(8,128)(2,1)S(1)}, bf16[128,256]{1,0:T(8,128)(2,1)S(1)}, u32[]{:S(2)}, u32[]{:S(2)}) collective-permute-start(bf16[128,256]{1,0:T(8,128)(2,1)S(1)} %fusion.4.refs_0_), channel_id=1, source_target_pairs={{0,17},{1,16},{2,19},{3,18},{4,21},{5,20},{6,23},{7,22},{8,25},{9,... | collective-permute-start | bytes 196616 | tf_op jit(solution)/shard_map/ppermute | solution.py:115
  40.0 6.8 %collective-permute-start.24 = (bf16[128,256]{1,0:T(8,128)(2,1)S(1)}, bf16[128,256]{1,0:T(8,128)(2,1)S(1)}, u32[]{:S(2)}, u32[]{:S(2)}) collective-permute-start(bf16[128,256]{1,0:T(8,128)(2,1)S(1)} %fusion.4.refs_0_), channel_id=1, source_target_pairs={{0,12},{1,13},{2,14},{3,15},{4,8},{5,9},{6,10},{7,11},{8,4},{9,5},... | collective-permute-start | bytes 196616 | tf_op jit(solution)/shard_map/ppermute | solution.py:115
  42.8 5.1 %collective-permute-start.23 = (bf16[128,256]{1,0:T(8,128)(2,1)S(1)}, bf16[128,256]{1,0:T(8,128)(2,1)S(1)}, u32[]{:S(2)}, u32[]{:S(2)}) collective-permute-start(bf16[128,256]{1,0:T(8,128)(2,1)S(1)} %fusion.4.refs_0_), channel_id=1, source_target_pairs={{0,8},{1,9},{2,10},{3,11},{4,12},{5,13},{6,14},{7,15},{8,0},{9,1},... | collective-permute-start | bytes 196616 | tf_op jit(solution)/shard_map/ppermute | solution.py:115
  42.9 5.1 %collective-permute-start.22 = (bf16[128,256]{1,0:T(8,128)(2,1)S(1)}, bf16[128,256]{1,0:T(8,128)(2,1)S(1)}, u32[]{:S(2)}, u32[]{:S(2)}) collective-permute-start(bf16[128,256]{1,0:T(8,128)(2,1)S(1)} %fusion.4.refs_0_), channel_id=1, source_target_pairs={{0,4},{1,5},{2,6},{3,7},{4,0},{5,1},{6,2},{7,3},{8,12},{9,13},{10,... | collective-permute-start | bytes 196616 | tf_op jit(solution)/shard_map/ppermute | solution.py:115
  44.1 5.2 %collective-permute-start.29 = (bf16[128,256]{1,0:T(8,128)(2,1)S(1)}, bf16[128,256]{1,0:T(8,128)(2,1)S(1)}, u32[]{:S(2)}, u32[]{:S(2)}) collective-permute-start(bf16[128,256]{1,0:T(8,128)(2,1)S(1)} %collective-permute-done.25), channel_id=1, source_target_pairs={{0,13},{1,12},{2,15},{3,14},{4,9},{5,8},{6,11},{7,10},{8,5},{9,4},... | collective-permute-start | bytes 196616 | tf_op jit(solution)/shard_map/ppermute | solution.py:115
  46.8 3.8 %collective-permute-start.28 = (bf16[128,256]{1,0:T(8,128)(2,1)S(1)}, bf16[128,256]{1,0:T(8,128)(2,1)S(1)}, u32[]{:S(2)}, u32[]{:S(2)}) collective-permute-start(bf16[128,256]{1,0:T(8,128)(2,1)S(1)} %collective-permute-done.25), channel_id=1, source_target_pairs={{0,9},{1,8},{2,11},{3,10},{4,13},{5,12},{6,15},{7,14},{8,1},{9,0},... | collective-permute-start | bytes 196616 | tf_op jit(solution)/shard_map/ppermute | solution.py:115
  46.8 4.0 %collective-permute-start.27 = (bf16[128,256]{1,0:T(8,128)(2,1)S(1)}, bf16[128,256]{1,0:T(8,128)(2,1)S(1)}, u32[]{:S(2)}, u32[]{:S(2)}) collective-permute-start(bf16[128,256]{1,0:T(8,128)(2,1)S(1)} %collective-permute-done.25), channel_id=1, source_target_pairs={{0,5},{1,4},{2,7},{3,6},{4,1},{5,0},{6,3},{7,2},{8,13},{9,12},{10,... | collective-permute-start | bytes 196616 | tf_op jit(solution)/shard_map/ppermute | solution.py:115
  47.9 3.0 %collective-permute-start.26 = (bf16[128,256]{1,0:T(8,128)(2,1)S(1)}, bf16[128,256]{1,0:T(8,128)(2,1)S(1)}, u32[]{:S(2)}, u32[]{:S(2)}) collective-permute-start(bf16[128,256]{1,0:T(8,128)(2,1)S(1)} %collective-permute-done.25), channel_id=1, source_target_pairs={{0,1},{1,0},{2,3},{3,2},{4,5},{5,4},{6,7},{7,6},{8,9},{9,8},{10,11... | collective-permute-start | bytes 196616 | tf_op jit(solution)/shard_map/ppermute | solution.py:115
  51.0 1.3 %collective-permute-start.31 = (bf16[128,256]{1,0:T(8,128)(2,1)S(1)}, bf16[128,256]{1,0:T(8,128)(2,1)S(1)}, u32[]{:S(2)}, u32[]{:S(2)}) collective-permute-start(bf16[128,256]{1,0:T(8,128)(2,1)S(1)} %late_first.5), channel_id=1, source_target_pairs={{0,1},{1,0},{2,3},{3,2},{4,5},{5,4},{6,7},{7,6},{8,9},{9,8},{10,11... | collective-permute-start | bytes 196616 | tf_op jit(solution)/shard_map/ppermute | solution.py:115
  51.7 2.3 %collective-permute-start.30 = (bf16[128,256]{1,0:T(8,128)(2,1)S(1)}, bf16[128,256]{1,0:T(8,128)(2,1)S(1)}, u32[]{:S(2)}, u32[]{:S(2)}) collective-permute-start(bf16[128,256]{1,0:T(8,128)(2,1)S(1)} %get-tuple-element.21), channel_id=1, source_target_pairs={{0,1},{1,0},{2,3},{3,2},{4,5},{5,4},{6,7},{7,6},{8,9},{9,8},{10,11... | collective-permute-start | bytes 196616 | tf_op jit(solution)/shard_map/ppermute | solution.py:115
  52.4 4.4 %collective-permute-start.32 = (bf16[128,256]{1,0:T(8,128)(2,1)S(1)}, bf16[128,256]{1,0:T(8,128)(2,1)S(1)}, u32[]{:S(2)}, u32[]{:S(2)}) collective-permute-start(bf16[128,256]{1,0:T(8,128)(2,1)S(1)} %add_convert_fusion.1), channel_id=1, source_target_pairs={{0,2},{1,3},{2,0},{3,1},{4,6},{5,7},{6,4},{7,5},{8,10},{9,11},{10,... | collective-permute-start | bytes 196616 | tf_op jit(solution)/shard_map/ppermute | solution.py:115

commit v6 on v5

--- a/solution.py
+++ b/solution.py
@@ -73,6 +73,14 @@
             lhs = weights_ref[at, weights_ref.shape[1] - block.shape[0]:]
             term = jnp.dot(lhs, block, preferred_element_type=jnp.float32)
             out_ref[start:start + size] = (refs[0][at] + term if begun else term).astype(out_ref.dtype)
+
+
+def update_kernel(coupling_ref, openness_ref, initial_ref, *refs):
+    terms, out_ref = refs[:-1], refs[-1]
+    influence = sum(ref[...].astype(jnp.float32) for ref in terms).astype(jnp.bfloat16)
+    coupled = jnp.dot(influence, coupling_ref[...], preferred_element_type=jnp.float32)
+    openness, initial = openness_ref[...], initial_ref[...].astype(jnp.float32)
+    out_ref[...] = (openness * coupled + (1.0 - openness) * initial).astype(out_ref.dtype)
 
 
 def place_kernel(past, count_ref, place_ref, out_ref):
@@ -164,13 +172,15 @@
         (sent,) = finish("late_first", 3)
         received = swap(sent, 0, tgt_bits[0])
         kept, mine, sent = finish("late_rest", 1, 0, 2)
-        other = swap(add(kept, received), 0, tgt_bits[1])
-        terms = add(add(mine, swap(sent, 0, tgt_bits[0])), other)
+        terms = [mine, swap(sent, 0, tgt_bits[0]), swap(add(kept, received), 0, tgt_bits[1])]
         for bit in tgt_bits[2:]:
-            half = terms.shape[0] // 2
-            terms = add(terms[:half], swap(terms[half:], 0, bit))
-        coupled = jnp.dot(terms, coupling, preferred_element_type=jnp.float32)
-        opinion = (openness * coupled + base).astype(jnp.bfloat16)
+            total = functools.reduce(add, terms)
+            half = total.shape[0] // 2
+            terms = [total[:half], swap(total[half:], 0, bit)]
+        if step < STEPS - 1:
+            opinion = local(update_kernel, "update", jax.ShapeDtypeStruct(initial.shape, jnp.bfloat16), 2 * own_rows * topics**2, coupling, openness, initial, *terms)
+    coupled = jnp.dot(functools.reduce(add, terms), coupling, preferred_element_type=jnp.float32)
+    opinion = (openness * coupled + base).astype(jnp.bfloat16)
     return opinion
 
 

time: 57.7 us -> 57.7 us (level)
    pallas_call x9 -> x11, Pallas kernels: 2.2 us -> 2.53 us  [local(): pl.pallas_call(kernel, out_shape=out_shapes, in_specs=[whole] * len(args)...]
  transfers between devices with their start and end apart: 33 -> 33, of which waited for: 15 -> 15; matrix products, arithmetic and copies ran while one was open for 1% -> 2% of each run, Pallas kernels for 5% -> 5%
where the time goes in v6:
time: 57.7 us; the launch traced here: 57.5 us
  starting transfers between devices  34.2 us (59%)
  waiting for transfers between devices  17 us (29%)
  Pallas kernels  3.82 us (7%)
  other arithmetic  0.84 us (1%)
  matrix products  0.81 us (1%)
  between operations  0.8 us (1%)
    ppermute x33, starting transfers between devices, swap(): lax.ppermute(value, BOTH, [(d, d ^ mask) for d in range(n_src * n_tgt)])  34.2 us
    ppermute x33, waiting for transfers between devices, swap(): lax.ppermute(value, BOTH, [(d, d ^ mask) for d in range(n_src * n_tgt)])  17 us
    pallas_call x11, Pallas kernels, local(): pl.pallas_call(kernel, out_shape=out_shapes, in_specs=[whole] * len(args)...  2.53 us
    pallas_call x1, Pallas kernels, densify(): pl.pallas_call(densify_kernel, out_shape=jax.ShapeDtypeStruct((n_rows * e...  1.29 us
  transfers between devices with their start and end apart: 33, of which 15 were waited for; matrix products, arithmetic and copies ran while one was open for 2% of the time, Pallas kernels for 5%

profile of v6, /device:TPU:0, one launch (start us, length us, event | category | flops | bytes accessed | tf_op | source)
XLA Modules:
  0.0 57.5 jit_solution(13401164136028174519)
XLA Ops:
  0.0 3.5 %collective-permute-start.3 = (bf16[128,256]{1,0:T(8,128)(2,1)}, bf16[128,256]{1,0:T(8,128)(2,1)S(1)}, u32[]{:S(2)}, u32[]{:S(2)}) collective-permute-start(bf16[128,256]{1,0:T(8,128)(2,1)} %initial_ref.3), channel_id=1, source_target_pairs={{0,17},{1,16},{2,19},{3,18},{4,21},{5,20},{6,23},{7,22},{8,25},{9,... | collective-permute-start | bytes 196616 | tf_op jit(solution)/shard_map/ppermute | solution.py:123
  3.5 2.5 %collective-permute-start.2 = (bf16[128,256]{1,0:T(8,128)(2,1)}, bf16[128,256]{1,0:T(8,128)(2,1)S(1)}, u32[]{:S(2)}, u32[]{:S(2)}) collective-permute-start(bf16[128,256]{1,0:T(8,128)(2,1)} %initial_ref.3), channel_id=1, source_target_pairs={{0,12},{1,13},{2,14},{3,15},{4,8},{5,9},{6,10},{7,11},{8,4},{9,5},... | collective-permute-start | bytes 196616 | tf_op jit(solution)/shard_map/ppermute | solution.py:123
  6.0 0.4 collective-permute-start.1
  6.4 0.5 collective-permute-start
  7.6 0.7 %add_bitcast_fusion.place_ref = s32[1,144]{1,0:T(1,128)S(1)} fusion(s32[1,1,144]{2,1,0:T(1,128)} %param.12, s32[1,1,144]{2,1,0:T(1,128)} %param.11, s32[]{:T(128)S(6)} %axis_index.25, s32[]{:T(128)S(6)} %axis_index.22), kind=kLoop, calls=%fused_computation.12 | loop fusion | flops 1584 | bytes 1736 | tf_op jit(solution)/shard_map/add | solution.py:149
  8.4 2.0 %collective-permute-start.7 = (bf16[128,256]{1,0:T(8,128)(2,1)S(1)}, bf16[128,256]{1,0:T(8,128)(2,1)S(1)}, u32[]{:S(2)}, u32[]{:S(2)}) collective-permute-start(bf16[128,256]{1,0:T(8,128)(2,1)S(1)} %collective-permute-done.3), channel_id=1, source_target_pairs={{0,13},{1,12},{2,15},{3,14},{4,9},{5,8},{6,11},{7,10},{8,5},{9,4},... | collective-permute-start | bytes 196616 | tf_op jit(solution)/shard_map/ppermute | solution.py:123
  10.5 0.7 %collective-permute-start.6 = (bf16[128,256]{1,0:T(8,128)(2,1)S(1)}, bf16[128,256]{1,0:T(8,128)(2,1)S(1)}, u32[]{:S(2)}, u32[]{:S(2)}) collective-permute-start(bf16[128,256]{1,0:T(8,128)(2,1)S(1)} %collective-permute-done.3), channel_id=1, source_target_pairs={{0,9},{1,8},{2,11},{3,10},{4,13},{5,12},{6,15},{7,14},{8,1},{9,0},... | collective-permute-start | bytes 196616 | tf_op jit(solution)/shard_map/ppermute | solution.py:123
  11.4 0.5 collective-permute-start.4
  11.9 1.3 %densify.1.weights_ref = bf16[512,1024]{1,0:T(8,128)(2,1)S(1)} custom-call(s32[145]{0:T(256)S(1)} %pad_add_fusion.places_ref, bf16[1,1,144,128,128]{4,3,2,1,0:T(8,128)(2,1)S(1)} %copy-done), custom_call_target="tpu_custom_call" | custom-call | flops 2359296 | bytes 4718592 | tf_op jit(solution)/shard_map/densify/pallas_call | solution.py:43
  13.2 0.4 collective-permute-done.7.refs_7_
  13.6 1.1 %collective-permute-done.6.refs_6_ = bf16[128,256]{1,0:T(8,128)(2,1)S(1)} collective-permute-done((bf16[128,256]{1,0:T(8,128)(2,1)S(1)}, bf16[128,256]{1,0:T(8,128)(2,1)S(1)}, u32[]{:S(2)}, u32[]{:S(2)}) %collective-permute-start.6) | collective-permute-done | bytes 65568 | tf_op jit(solution)/shard_map/ppermute | solution.py:123
  14.7 0.7 %collective-permute-done.5.refs_5_ = bf16[128,256]{1,0:T(8,128)(2,1)S(1)} collective-permute-done((bf16[128,256]{1,0:T(8,128)(2,1)S(1)}, bf16[128,256]{1,0:T(8,128)(2,1)S(1)}, u32[]{:S(2)}, u32[]{:S(2)}) %collective-permute-start.5) | collective-permute-done | bytes 65568 | tf_op jit(solution)/shard_map/ppermute | solution.py:123
  15.4 0.2 late_first.3
  15.8 0.4 late_rest.3
  16.2 0.5 collective-permute-start.8
  16.7 0.3 collective-permute-done.9
  17.0 1.6 %collective-permute-start.10 = (bf16[128,256]{1,0:T(8,128)(2,1)S(1)}, bf16[128,256]{1,0:T(8,128)(2,1)S(1)}, u32[]{:S(2)}, u32[]{:S(2)}) collective-permute-start(bf16[128,256]{1,0:T(8,128)(2,1)S(1)} %add_convert_fusion.4), channel_id=1, source_target_pairs={{0,2},{1,3},{2,0},{3,1},{4,6},{5,7},{6,4},{7,5},{8,10},{9,11},{10,... | collective-permute-start | bytes 196616 | tf_op jit(solution)/shard_map/ppermute | solution.py:123
  18.7 2.6 %collective-permute-done.10.refs_2_ = bf16[128,256]{1,0:T(8,128)(2,1)S(1)} collective-permute-done((bf16[128,256]{1,0:T(8,128)(2,1)S(1)}, bf16[128,256]{1,0:T(8,128)(2,1)S(1)}, u32[]{:S(2)}, u32[]{:S(2)}) %collective-permute-start.10) | collective-permute-done | bytes 65568 | tf_op jit(solution)/shard_map/ppermute | solution.py:123
  21.5 0.9 %collective-permute-start.14 = (bf16[128,256]{1,0:T(8,128)(2,1)S(1)}, bf16[128,256]{1,0:T(8,128)(2,1)S(1)}, u32[]{:S(2)}, u32[]{:S(2)}) collective-permute-start(bf16[128,256]{1,0:T(8,128)(2,1)S(1)} %update.2.refs_0_), channel_id=1, source_target_pairs={{0,17},{1,16},{2,19},{3,18},{4,21},{5,20},{6,23},{7,22},{8,25},{9,... | collective-permute-start | bytes 196616 | tf_op jit(solution)/shard_map/ppermute | solution.py:123
  22.4 2.5 %collective-permute-start.13 = (bf16[128,256]{1,0:T(8,128)(2,1)S(1)}, bf16[128,256]{1,0:T(8,128)(2,1)S(1)}, u32[]{:S(2)}, u32[]{:S(2)}) collective-permute-start(bf16[128,256]{1,0:T(8,128)(2,1)S(1)} %update.2.refs_0_), channel_id=1, source_target_pairs={{0,12},{1,13},{2,14},{3,15},{4,8},{5,9},{6,10},{7,11},{8,4},{9,5},... | collective-permute-start | bytes 196616 | tf_op jit(solution)/shard_map/ppermute | solution.py:123
  24.9 1.0 %collective-permute-start.11 = (bf16[128,256]{1,0:T(8,128)(2,1)S(1)}, bf16[128,256]{1,0:T(8,128)(2,1)S(1)}, u32[]{:S(2)}, u32[]{:S(2)}) collective-permute-start(bf16[128,256]{1,0:T(8,128)(2,1)S(1)} %update.2.refs_0_), channel_id=1, source_target_pairs={{0,4},{1,5},{2,6},{3,7},{4,0},{5,1},{6,2},{7,3},{8,12},{9,13},{10,... | collective-permute-start | bytes 196616 | tf_op jit(solution)/shard_map/ppermute | solution.py:123
  25.9 0.3 collective-permute-done.14
  26.2 2.6 %collective-permute-start.18 = (bf16[128,256]{1,0:T(8,128)(2,1)S(1)}, bf16[128,256]{1,0:T(8,128)(2,1)S(1)}, u32[]{:S(2)}, u32[]{:S(2)}) collective-permute-start(bf16[128,256]{1,0:T(8,128)(2,1)S(1)} %collective-permute-done.14), channel_id=1, source_target_pairs={{0,13},{1,12},{2,15},{3,14},{4,9},{5,8},{6,11},{7,10},{8,5},{9,4},... | collective-permute-start | bytes 196616 | tf_op jit(solution)/shard_map/ppermute | solution.py:123
  28.8 0.9 %collective-permute-start.16 = (bf16[128,256]{1,0:T(8,128)(2,1)S(1)}, bf16[128,256]{1,0:T(8,128)(2,1)S(1)}, u32[]{:S(2)}, u32[]{:S(2)}) collective-permute-start(bf16[128,256]{1,0:T(8,128)(2,1)S(1)} %collective-permute-done.14), channel_id=1, source_target_pairs={{0,5},{1,4},{2,7},{3,6},{4,1},{5,0},{6,3},{7,2},{8,13},{9,12},{10,... | collective-permute-start | bytes 196616 | tf_op jit(solution)/shard_map/ppermute | solution.py:123
  29.7 0.3 early.2.refs_0_
  30.0 1.2 %collective-permute-done.18.refs_4_ = bf16[128,256]{1,0:T(8,128)(2,1)S(1)} collective-permute-done((bf16[128,256]{1,0:T(8,128)(2,1)S(1)}, bf16[128,256]{1,0:T(8,128)(2,1)S(1)}, u32[]{:S(2)}, u32[]{:S(2)}) %collective-permute-start.18) | collective-permute-done | bytes 65568 | tf_op jit(solution)/shard_map/ppermute | solution.py:123
  31.3 1.4 %collective-permute-done.17.refs_3_ = bf16[128,256]{1,0:T(8,128)(2,1)S(1)} collective-permute-done((bf16[128,256]{1,0:T(8,128)(2,1)S(1)}, bf16[128,256]{1,0:T(8,128)(2,1)S(1)}, u32[]{:S(2)}, u32[]{:S(2)}) %collective-permute-start.17) | collective-permute-done | bytes 65568 | tf_op jit(solution)/shard_map/ppermute | solution.py:123
  32.8 0.4 collective-permute-start.20
  33.3 0.3 late_rest.4
  33.5 0.2 collective-permute-start.19
  33.7 0.4 collective-permute-done.20
  34.2 1.6 %collective-permute-start.21 = (bf16[128,256]{1,0:T(8,128)(2,1)S(1)}, bf16[128,256]{1,0:T(8,128)(2,1)S(1)}, u32[]{:S(2)}, u32[]{:S(2)}) collective-permute-start(bf16[128,256]{1,0:T(8,128)(2,1)S(1)} %add_convert_fusion.3), channel_id=1, source_target_pairs={{0,2},{1,3},{2,0},{3,1},{4,6},{5,7},{6,4},{7,5},{8,10},{9,11},{10,... | collective-permute-start | bytes 196616 | tf_op jit(solution)/shard_map/ppermute | solution.py:123
  35.8 2.8 %collective-permute-done.21.refs_2_ = bf16[128,256]{1,0:T(8,128)(2,1)S(1)} collective-permute-done((bf16[128,256]{1,0:T(8,128)(2,1)S(1)}, bf16[128,256]{1,0:T(8,128)(2,1)S(1)}, u32[]{:S(2)}, u32[]{:S(2)}) %collective-permute-start.21) | collective-permute-done | bytes 65568 | tf_op jit(solution)/shard_map/ppermute | solution.py:123
  38.8 1.2 %collective-permute-start.25 = (bf16[128,256]{1,0:T(8,128)(2,1)S(1)}, bf16[128,256]{1,0:T(8,128)(2,1)S(1)}, u32[]{:S(2)}, u32[]{:S(2)}) collective-permute-start(bf16[128,256]{1,0:T(8,128)(2,1)S(1)} %update.3.refs_0_), channel_id=1, source_target_pairs={{0,17},{1,16},{2,19},{3,18},{4,21},{5,20},{6,23},{7,22},{8,25},{9,... | collective-permute-start | bytes 196616 | tf_op jit(solution)/shard_map/ppermute | solution.py:123
  40.0 2.8 %collective-permute-start.24 = (bf16[128,256]{1,0:T(8,128)(2,1)S(1)}, bf16[128,256]{1,0:T(8,128)(2,1)S(1)}, u32[]{:S(2)}, u32[]{:S(2)}) collective-permute-start(bf16[128,256]{1,0:T(8,128)(2,1)S(1)} %update.3.refs_0_), channel_id=1, source_target_pairs={{0,12},{1,13},{2,14},{3,15},{4,8},{5,9},{6,10},{7,11},{8,4},{9,5},... | collective-permute-start | bytes 196616 | tf_op jit(solution)/shard_map/ppermute | solution.py:123
  42.9 1.1 %collective-permute-start.22 = (bf16[128,256]{1,0:T(8,128)(2,1)S(1)}, bf16[128,256]{1,0:T(8,128)(2,1)S(1)}, u32[]{:S(2)}, u32[]{:S(2)}) collective-permute-start(bf16[128,256]{1,0:T(8,128)(2,1)S(1)} %update.3.refs_0_), channel_id=1, source_target_pairs={{0,4},{1,5},{2,6},{3,7},{4,0},{5,1},{6,2},{7,3},{8,12},{9,13},{10,... | collective-permute-start | bytes 196616 | tf_op jit(solution)/shard_map/ppermute | solution.py:123
  44.1 2.8 %collective-permute-start.29 = (bf16[128,256]{1,0:T(8,128)(2,1)S(1)}, bf16[128,256]{1,0:T(8,128)(2,1)S(1)}, u32[]{:S(2)}, u32[]{:S(2)}) collective-permute-start(bf16[128,256]{1,0:T(8,128)(2,1)S(1)} %collective-permute-done.25), channel_id=1, source_target_pairs={{0,13},{1,12},{2,15},{3,14},{4,9},{5,8},{6,11},{7,10},{8,5},{9,4},... | collective-permute-start | bytes 196616 | tf_op jit(solution)/shard_map/ppermute | solution.py:123
  46.9 1.0 %collective-permute-start.27 = (bf16[128,256]{1,0:T(8,128)(2,1)S(1)}, bf16[128,256]{1,0:T(8,128)(2,1)S(1)}, u32[]{:S(2)}, u32[]{:S(2)}) collective-permute-start(bf16[128,256]{1,0:T(8,128)(2,1)S(1)} %collective-permute-done.25), channel_id=1, source_target_pairs={{0,5},{1,4},{2,7},{3,6},{4,1},{5,0},{6,3},{7,2},{8,13},{9,12},{10,... | collective-permute-start | bytes 196616 | tf_op jit(solution)/shard_map/ppermute | solution.py:123
  48.0 0.3 early.3.refs_0_
  48.3 1.0 %collective-permute-done.29.refs_4_ = bf16[128,256]{1,0:T(8,128)(2,1)S(1)} collective-permute-done((bf16[128,256]{1,0:T(8,128)(2,1)S(1)}, bf16[128,256]{1,0:T(8,128)(2,1)S(1)}, u32[]{:S(2)}, u32[]{:S(2)}) %collective-permute-start.29) | collective-permute-done | bytes 65568 | tf_op jit(solution)/shard_map/ppermute | solution.py:123
  49.3 1.4 %collective-permute-done.28.refs_3_ = bf16[128,256]{1,0:T(8,128)(2,1)S(1)} collective-permute-done((bf16[128,256]{1,0:T(8,128)(2,1)S(1)}, bf16[128,256]{1,0:T(8,128)(2,1)S(1)}, u32[]{:S(2)}, u32[]{:S(2)}) %collective-permute-start.28) | collective-permute-done | bytes 65568 | tf_op jit(solution)/shard_map/ppermute | solution.py:123
  51.0 0.4 collective-permute-start.31
  51.4 0.3 late_rest.5
  51.7 0.2 collective-permute-start.30
  51.9 0.4 collective-permute-done.31
  52.3 1.6 %collective-permute-start.32 = (bf16[128,256]{1,0:T(8,128)(2,1)S(1)}, bf16[128,256]{1,0:T(8,128)(2,1)S(1)}, u32[]{:S(2)}, u32[]{:S(2)}) collective-permute-start(bf16[128,256]{1,0:T(8,128)(2,1)S(1)} %add_convert_fusion.1), channel_id=1, source_target_pairs={{0,2},{1,3},{2,0},{3,1},{4,6},{5,7},{6,4},{7,5},{8,10},{9,11},{10,... | collective-permute-start | bytes 196616 | tf_op jit(solution)/shard_map/ppermute | solution.py:123
  53.9 2.8 %collective-permute-done.32 = bf16[128,256]{1,0:T(8,128)(2,1)S(1)} collective-permute-done((bf16[128,256]{1,0:T(8,128)(2,1)S(1)}, bf16[128,256]{1,0:T(8,128)(2,1)S(1)}, u32[]{:S(2)}, u32[]{:S(2)}) %collective-permute-start.32) | collective-permute-done | bytes 65568 | tf_op jit(solution)/shard_map/ppermute | solution.py:123
  56.7 0.8 %fusion.1 = bf16[128,256]{1,0:T(8,128)(2,1)} fusion(bf16[256,256]{1,0:T(8,128)(2,1)S(1)} %copy-done.2, bf16[128,256]{1,0:T(8,128)(2,1)S(1)} %copy-done.1, bf16[128,256]{1,0:T(8,128)(2,1)S(1)} %collective-permute-done.32, bf16[128,256]{1,0:T(8,128)(2,1)S(1)} %collective-permute-done.30, bf16[128,256]{1,0:T(8,128)(2,1)S(1)} %get-tuple-element.20, ...), kind=kOutput, calls=%fused_computation.2 | convolution fusion | flops 17203200 | bytes 459776 | tf_op jit(solution)/shard_map/dot_general | solution.py:182
  (46 shorter events, 1.9 us)
Async XLA Ops:
  0.0 8.4 %collective-permute-start.3 = (bf16[128,256]{1,0:T(8,128)(2,1)}, bf16[128,256]{1,0:T(8,128)(2,1)S(1)}, u32[]{:S(2)}, u32[]{:S(2)}) collective-permute-start(bf16[128,256]{1,0:T(8,128)(2,1)} %initial_ref.3), channel_id=1, source_target_pairs={{0,17},{1,16},{2,19},{3,18},{4,21},{5,20},{6,23},{7,22},{8,25},{9,... | collective-permute-start | bytes 196616 | tf_op jit(solution)/shard_map/ppermute | solution.py:123
  3.5 7.7 %collective-permute-start.2 = (bf16[128,256]{1,0:T(8,128)(2,1)}, bf16[128,256]{1,0:T(8,128)(2,1)S(1)}, u32[]{:S(2)}, u32[]{:S(2)}) collective-permute-start(bf16[128,256]{1,0:T(8,128)(2,1)} %initial_ref.3), channel_id=1, source_target_pairs={{0,12},{1,13},{2,14},{3,15},{4,8},{5,9},{6,10},{7,11},{8,4},{9,5},... | collective-permute-start | bytes 196616 | tf_op jit(solution)/shard_map/ppermute | solution.py:123
  6.0 5.4 %collective-permute-start.1 = (bf16[128,256]{1,0:T(8,128)(2,1)}, bf16[128,256]{1,0:T(8,128)(2,1)S(1)}, u32[]{:S(2)}, u32[]{:S(2)}) collective-permute-start(bf16[128,256]{1,0:T(8,128)(2,1)} %initial_ref.3), channel_id=1, source_target_pairs={{0,8},{1,9},{2,10},{3,11},{4,12},{5,13},{6,14},{7,15},{8,0},{9,1},... | collective-permute-start | bytes 196616 | tf_op jit(solution)/shard_map/ppermute | solution.py:123
  6.4 6.8 %collective-permute-start = (bf16[128,256]{1,0:T(8,128)(2,1)}, bf16[128,256]{1,0:T(8,128)(2,1)S(1)}, u32[]{:S(2)}, u32[]{:S(2)}) collective-permute-start(bf16[128,256]{1,0:T(8,128)(2,1)} %initial_ref.3), channel_id=1, source_target_pairs={{0,4},{1,5},{2,6},{3,7},{4,0},{5,1},{6,2},{7,3},{8,12},{9,13},{10,... | collective-permute-start | bytes 196616 | tf_op jit(solution)/shard_map/ppermute | solution.py:123
  8.3 3.6 %copy-start = (bf16[1,1,144,128,128]{4,3,2,1,0:T(8,128)(2,1)S(1)}, bf16[1,1,144,128,128]{4,3,2,1,0:T(8,128)(2,1)}, u32[]{:S(2)}) copy-start(bf16[1,1,144,128,128]{4,3,2,1,0:T(8,128)(2,1)} %tiles_ref.1) | copy-start | bytes 14155780
  8.4 7.0 %copy-start.1 = (bf16[128,256]{1,0:T(8,128)(2,1)S(1)}, bf16[128,256]{1,0:T(8,128)(2,1)}, u32[]{:S(2)}) copy-start(bf16[128,256]{1,0:T(8,128)(2,1)} %initial_ref.3) | copy-start | bytes 196612
  8.4 10.2 %copy-start.3 = (s32[128]{0:T(128)S(1)}, s32[128]{0:T(128)}, u32[]{:S(2)}) copy-start(s32[128]{0:T(128)} %param.8) | copy-start | bytes 1540
  8.4 12.9 %copy-start.2 = (bf16[256,256]{1,0:T(8,128)(2,1)S(1)}, bf16[256,256]{1,0:T(8,128)(2,1)}, u32[]{:S(2)}) copy-start(bf16[256,256]{1,0:T(8,128)(2,1)} %coupling_ref.3) | copy-start | bytes 393220
  8.4 5.2 %collective-permute-start.7 = (bf16[128,256]{1,0:T(8,128)(2,1)S(1)}, bf16[128,256]{1,0:T(8,128)(2,1)S(1)}, u32[]{:S(2)}, u32[]{:S(2)}) collective-permute-start(bf16[128,256]{1,0:T(8,128)(2,1)S(1)} %collective-permute-done.3), channel_id=1, source_target_pairs={{0,13},{1,12},{2,15},{3,14},{4,9},{5,8},{6,11},{7,10},{8,5},{9,4},... | collective-permute-start | bytes 196616 | tf_op jit(solution)/shard_map/ppermute | solution.py:123
  10.5 4.2 %collective-permute-start.6 = (bf16[128,256]{1,0:T(8,128)(2,1)S(1)}, bf16[128,256]{1,0:T(8,128)(2,1)S(1)}, u32[]{:S(2)}, u32[]{:S(2)}) collective-permute-start(bf16[128,256]{1,0:T(8,128)(2,1)S(1)} %collective-permute-done.3), channel_id=1, source_target_pairs={{0,9},{1,8},{2,11},{3,10},{4,13},{5,12},{6,15},{7,14},{8,1},{9,0},... | collective-permute-start | bytes 196616 | tf_op jit(solution)/shard_map/ppermute | solution.py:123
  11.2 4.2 %collective-permute-start.5 = (bf16[128,256]{1,0:T(8,128)(2,1)S(1)}, bf16[128,256]{1,0:T(8,128)(2,1)S(1)}, u32[]{:S(2)}, u32[]{:S(2)}) collective-permute-start(bf16[128,256]{1,0:T(8,128)(2,1)S(1)} %collective-permute-done.3), channel_id=1, source_target_pairs={{0,5},{1,4},{2,7},{3,6},{4,1},{5,0},{6,3},{7,2},{8,13},{9,12},{10,... | collective-permute-start | bytes 196616 | tf_op jit(solution)/shard_map/ppermute | solution.py:123
  11.4 4.0 %collective-permute-start.4 = (bf16[128,256]{1,0:T(8,128)(2,1)S(1)}, bf16[128,256]{1,0:T(8,128)(2,1)S(1)}, u32[]{:S(2)}, u32[]{:S(2)}) collective-permute-start(bf16[128,256]{1,0:T(8,128)(2,1)S(1)} %collective-permute-done.3), channel_id=1, source_target_pairs={{0,1},{1,0},{2,3},{3,2},{4,5},{5,4},{6,7},{7,6},{8,9},{9,8},{10,11... | collective-permute-start | bytes 196616 | tf_op jit(solution)/shard_map/ppermute | solution.py:123
  15.6 1.3 %collective-permute-start.9 = (bf16[128,256]{1,0:T(8,128)(2,1)S(1)}, bf16[128,256]{1,0:T(8,128)(2,1)S(1)}, u32[]{:S(2)}, u32[]{:S(2)}) collective-permute-start(bf16[128,256]{1,0:T(8,128)(2,1)S(1)} %late_first.3), channel_id=1, source_target_pairs={{0,1},{1,0},{2,3},{3,2},{4,5},{5,4},{6,7},{7,6},{8,9},{9,8},{10,11... | collective-permute-start | bytes 196616 | tf_op jit(solution)/shard_map/ppermute | solution.py:123
  16.2 2.5 %collective-permute-start.8 = (bf16[128,256]{1,0:T(8,128)(2,1)S(1)}, bf16[128,256]{1,0:T(8,128)(2,1)S(1)}, u32[]{:S(2)}, u32[]{:S(2)}) collective-permute-start(bf16[128,256]{1,0:T(8,128)(2,1)S(1)} %get-tuple-element.15), channel_id=1, source_target_pairs={{0,1},{1,0},{2,3},{3,2},{4,5},{5,4},{6,7},{7,6},{8,9},{9,8},{10,11... | collective-permute-start | bytes 196616 | tf_op jit(solution)/shard_map/ppermute | solution.py:123
  17.0 4.3 %collective-permute-start.10 = (bf16[128,256]{1,0:T(8,128)(2,1)S(1)}, bf16[128,256]{1,0:T(8,128)(2,1)S(1)}, u32[]{:S(2)}, u32[]{:S(2)}) collective-permute-start(bf16[128,256]{1,0:T(8,128)(2,1)S(1)} %add_convert_fusion.4), channel_id=1, source_target_pairs={{0,2},{1,3},{2,0},{3,1},{4,6},{5,7},{6,4},{7,5},{8,10},{9,11},{10,... | collective-permute-start | bytes 196616 | tf_op jit(solution)/shard_map/ppermute | solution.py:123
  21.5 4.7 %collective-permute-start.14 = (bf16[128,256]{1,0:T(8,128)(2,1)S(1)}, bf16[128,256]{1,0:T(8,128)(2,1)S(1)}, u32[]{:S(2)}, u32[]{:S(2)}) collective-permute-start(bf16[128,256]{1,0:T(8,128)(2,1)S(1)} %update.2.refs_0_), channel_id=1, source_target_pairs={{0,17},{1,16},{2,19},{3,18},{4,21},{5,20},{6,23},{7,22},{8,25},{9,... | collective-permute-start | bytes 196616 | tf_op jit(solution)/shard_map/ppermute | solution.py:123
  22.4 6.4 %collective-permute-start.13 = (bf16[128,256]{1,0:T(8,128)(2,1)S(1)}, bf16[128,256]{1,0:T(8,128)(2,1)S(1)}, u32[]{:S(2)}, u32[]{:S(2)}) collective-permute-start(bf16[128,256]{1,0:T(8,128)(2,1)S(1)} %update.2.refs_0_), channel_id=1, source_target_pairs={{0,12},{1,13},{2,14},{3,15},{4,8},{5,9},{6,10},{7,11},{8,4},{9,5},... | collective-permute-start | bytes 196616 | tf_op jit(solution)/shard_map/ppermute | solution.py:123
  24.9 4.8 %collective-permute-start.12 = (bf16[128,256]{1,0:T(8,128)(2,1)S(1)}, bf16[128,256]{1,0:T(8,128)(2,1)S(1)}, u32[]{:S(2)}, u32[]{:S(2)}) collective-permute-start(bf16[128,256]{1,0:T(8,128)(2,1)S(1)} %update.2.refs_0_), channel_id=1, source_target_pairs={{0,8},{1,9},{2,10},{3,11},{4,12},{5,13},{6,14},{7,15},{8,0},{9,1},... | collective-permute-start | bytes 196616 | tf_op jit(solution)/shard_map/ppermute | solution.py:123
  24.9 4.8 %collective-permute-start.11 = (bf16[128,256]{1,0:T(8,128)(2,1)S(1)}, bf16[128,256]{1,0:T(8,128)(2,1)S(1)}, u32[]{:S(2)}, u32[]{:S(2)}) collective-permute-start(bf16[128,256]{1,0:T(8,128)(2,1)S(1)} %update.2.refs_0_), channel_id=1, source_target_pairs={{0,4},{1,5},{2,6},{3,7},{4,0},{5,1},{6,2},{7,3},{8,12},{9,13},{10,... | collective-permute-start | bytes 196616 | tf_op jit(solution)/shard_map/ppermute | solution.py:123
  26.2 5.1 %collective-permute-start.18 = (bf16[128,256]{1,0:T(8,128)(2,1)S(1)}, bf16[128,256]{1,0:T(8,128)(2,1)S(1)}, u32[]{:S(2)}, u32[]{:S(2)}) collective-permute-start(bf16[128,256]{1,0:T(8,128)(2,1)S(1)} %collective-permute-done.14), channel_id=1, source_target_pairs={{0,13},{1,12},{2,15},{3,14},{4,9},{5,8},{6,11},{7,10},{8,5},{9,4},... | collective-permute-start | bytes 196616 | tf_op jit(solution)/shard_map/ppermute | solution.py:123
  28.8 3.8 %collective-permute-start.17 = (bf16[128,256]{1,0:T(8,128)(2,1)S(1)}, bf16[128,256]{1,0:T(8,128)(2,1)S(1)}, u32[]{:S(2)}, u32[]{:S(2)}) collective-permute-start(bf16[128,256]{1,0:T(8,128)(2,1)S(1)} %collective-permute-done.14), channel_id=1, source_target_pairs={{0,9},{1,8},{2,11},{3,10},{4,13},{5,12},{6,15},{7,14},{8,1},{9,0},... | collective-permute-start | bytes 196616 | tf_op jit(solution)/shard_map/ppermute | solution.py:123
  28.8 3.8 %collective-permute-start.16 = (bf16[128,256]{1,0:T(8,128)(2,1)S(1)}, bf16[128,256]{1,0:T(8,128)(2,1)S(1)}, u32[]{:S(2)}, u32[]{:S(2)}) collective-permute-start(bf16[128,256]{1,0:T(8,128)(2,1)S(1)} %collective-permute-done.14), channel_id=1, source_target_pairs={{0,5},{1,4},{2,7},{3,6},{4,1},{5,0},{6,3},{7,2},{8,13},{9,12},{10,... | collective-permute-start | bytes 196616 | tf_op jit(solution)/shard_map/ppermute | solution.py:123
  29.7 2.9 %collective-permute-start.15 = (bf16[128,256]{1,0:T(8,128)(2,1)S(1)}, bf16[128,256]{1,0:T(8,128)(2,1)S(1)}, u32[]{:S(2)}, u32[]{:S(2)}) collective-permute-start(bf16[128,256]{1,0:T(8,128)(2,1)S(1)} %collective-permute-done.14), channel_id=1, source_target_pairs={{0,1},{1,0},{2,3},{3,2},{4,5},{5,4},{6,7},{7,6},{8,9},{9,8},{10,11... | collective-permute-start | bytes 196616 | tf_op jit(solution)/shard_map/ppermute | solution.py:123
  32.8 1.3 %collective-permute-start.20 = (bf16[128,256]{1,0:T(8,128)(2,1)S(1)}, bf16[128,256]{1,0:T(8,128)(2,1)S(1)}, u32[]{:S(2)}, u32[]{:S(2)}) collective-permute-start(bf16[128,256]{1,0:T(8,128)(2,1)S(1)} %late_first.4), channel_id=1, source_target_pairs={{0,1},{1,0},{2,3},{3,2},{4,5},{5,4},{6,7},{7,6},{8,9},{9,8},{10,11... | collective-permute-start | bytes 196616 | tf_op jit(solution)/shard_map/ppermute | solution.py:123
  33.5 2.2 %collective-permute-start.19 = (bf16[128,256]{1,0:T(8,128)(2,1)S(1)}, bf16[128,256]{1,0:T(8,128)(2,1)S(1)}, u32[]{:S(2)}, u32[]{:S(2)}) collective-permute-start(bf16[128,256]{1,0:T(8,128)(2,1)S(1)} %get-tuple-element.18), channel_id=1, source_target_pairs={{0,1},{1,0},{2,3},{3,2},{4,5},{5,4},{6,7},{7,6},{8,9},{9,8},{10,11... | collective-permute-start | bytes 196616 | tf_op jit(solution)/shard_map/ppermute | solution.py:123
  34.2 4.4 %collective-permute-start.21 = (bf16[128,256]{1,0:T(8,128)(2,1)S(1)}, bf16[128,256]{1,0:T(8,128)(2,1)S(1)}, u32[]{:S(2)}, u32[]{:S(2)}) collective-permute-start(bf16[128,256]{1,0:T(8,128)(2,1)S(1)} %add_convert_fusion.3), channel_id=1, source_target_pairs={{0,2},{1,3},{2,0},{3,1},{4,6},{5,7},{6,4},{7,5},{8,10},{9,11},{10,... | collective-permute-start | bytes 196616 | tf_op jit(solution)/shard_map/ppermute | solution.py:123
  38.8 5.3 %collective-permute-start.25 = (bf16[128,256]{1,0:T(8,128)(2,1)S(1)}, bf16[128,256]{1,0:T(8,128)(2,1)S(1)}, u32[]{:S(2)}, u32[]{:S(2)}) collective-permute-start(bf16[128,256]{1,0:T(8,128)(2,1)S(1)} %update.3.refs_0_), channel_id=1, source_target_pairs={{0,17},{1,16},{2,19},{3,18},{4,21},{5,20},{6,23},{7,22},{8,25},{9,... | collective-permute-start | bytes 196616 | tf_op jit(solution)/shard_map/ppermute | solution.py:123
  40.0 6.8 %collective-permute-start.24 = (bf16[128,256]{1,0:T(8,128)(2,1)S(1)}, bf16[128,256]{1,0:T(8,128)(2,1)S(1)}, u32[]{:S(2)}, u32[]{:S(2)}) collective-permute-start(bf16[128,256]{1,0:T(8,128)(2,1)S(1)} %update.3.refs_0_), channel_id=1, source_target_pairs={{0,12},{1,13},{2,14},{3,15},{4,8},{5,9},{6,10},{7,11},{8,4},{9,5},... | collective-permute-start | bytes 196616 | tf_op jit(solution)/shard_map/ppermute | solution.py:123
  42.8 5.1 %collective-permute-start.23 = (bf16[128,256]{1,0:T(8,128)(2,1)S(1)}, bf16[128,256]{1,0:T(8,128)(2,1)S(1)}, u32[]{:S(2)}, u32[]{:S(2)}) collective-permute-start(bf16[128,256]{1,0:T(8,128)(2,1)S(1)} %update.3.refs_0_), channel_id=1, source_target_pairs={{0,8},{1,9},{2,10},{3,11},{4,12},{5,13},{6,14},{7,15},{8,0},{9,1},... | collective-permute-start | bytes 196616 | tf_op jit(solution)/shard_map/ppermute | solution.py:123
  42.9 5.1 %collective-permute-start.22 = (bf16[128,256]{1,0:T(8,128)(2,1)S(1)}, bf16[128,256]{1,0:T(8,128)(2,1)S(1)}, u32[]{:S(2)}, u32[]{:S(2)}) collective-permute-start(bf16[128,256]{1,0:T(8,128)(2,1)S(1)} %update.3.refs_0_), channel_id=1, source_target_pairs={{0,4},{1,5},{2,6},{3,7},{4,0},{5,1},{6,2},{7,3},{8,12},{9,13},{10,... | collective-permute-start | bytes 196616 | tf_op jit(solution)/shard_map/ppermute | solution.py:123
  44.1 5.2 %collective-permute-start.29 = (bf16[128,256]{1,0:T(8,128)(2,1)S(1)}, bf16[128,256]{1,0:T(8,128)(2,1)S(1)}, u32[]{:S(2)}, u32[]{:S(2)}) collective-permute-start(bf16[128,256]{1,0:T(8,128)(2,1)S(1)} %collective-permute-done.25), channel_id=1, source_target_pairs={{0,13},{1,12},{2,15},{3,14},{4,9},{5,8},{6,11},{7,10},{8,5},{9,4},... | collective-permute-start | bytes 196616 | tf_op jit(solution)/shard_map/ppermute | solution.py:123
  46.8 3.8 %collective-permute-start.28 = (bf16[128,256]{1,0:T(8,128)(2,1)S(1)}, bf16[128,256]{1,0:T(8,128)(2,1)S(1)}, u32[]{:S(2)}, u32[]{:S(2)}) collective-permute-start(bf16[128,256]{1,0:T(8,128)(2,1)S(1)} %collective-permute-done.25), channel_id=1, source_target_pairs={{0,9},{1,8},{2,11},{3,10},{4,13},{5,12},{6,15},{7,14},{8,1},{9,0},... | collective-permute-start | bytes 196616 | tf_op jit(solution)/shard_map/ppermute | solution.py:123
  46.9 3.9 %collective-permute-start.27 = (bf16[128,256]{1,0:T(8,128)(2,1)S(1)}, bf16[128,256]{1,0:T(8,128)(2,1)S(1)}, u32[]{:S(2)}, u32[]{:S(2)}) collective-permute-start(bf16[128,256]{1,0:T(8,128)(2,1)S(1)} %collective-permute-done.25), channel_id=1, source_target_pairs={{0,5},{1,4},{2,7},{3,6},{4,1},{5,0},{6,3},{7,2},{8,13},{9,12},{10,... | collective-permute-start | bytes 196616 | tf_op jit(solution)/shard_map/ppermute | solution.py:123
  47.9 2.9 %collective-permute-start.26 = (bf16[128,256]{1,0:T(8,128)(2,1)S(1)}, bf16[128,256]{1,0:T(8,128)(2,1)S(1)}, u32[]{:S(2)}, u32[]{:S(2)}) collective-permute-start(bf16[128,256]{1,0:T(8,128)(2,1)S(1)} %collective-permute-done.25), channel_id=1, source_target_pairs={{0,1},{1,0},{2,3},{3,2},{4,5},{5,4},{6,7},{7,6},{8,9},{9,8},{10,11... | collective-permute-start | bytes 196616 | tf_op jit(solution)/shard_map/ppermute | solution.py:123
  51.0 1.3 %collective-permute-start.31 = (bf16[128,256]{1,0:T(8,128)(2,1)S(1)}, bf16[128,256]{1,0:T(8,128)(2,1)S(1)}, u32[]{:S(2)}, u32[]{:S(2)}) collective-permute-start(bf16[128,256]{1,0:T(8,128)(2,1)S(1)} %late_first.5), channel_id=1, source_target_pairs={{0,1},{1,0},{2,3},{3,2},{4,5},{5,4},{6,7},{7,6},{8,9},{9,8},{10,11... | collective-permute-start | bytes 196616 | tf_op jit(solution)/shard_map/ppermute | solution.py:123
  51.7 2.3 %collective-permute-start.30 = (bf16[128,256]{1,0:T(8,128)(2,1)S(1)}, bf16[128,256]{1,0:T(8,128)(2,1)S(1)}, u32[]{:S(2)}, u32[]{:S(2)}) collective-permute-start(bf16[128,256]{1,0:T(8,128)(2,1)S(1)} %get-tuple-element.21), channel_id=1, source_target_pairs={{0,1},{1,0},{2,3},{3,2},{4,5},{5,4},{6,7},{7,6},{8,9},{9,8},{10,11... | collective-permute-start | bytes 196616 | tf_op jit(solution)/shard_map/ppermute | solution.py:123
  52.3 4.4 %collective-permute-start.32 = (bf16[128,256]{1,0:T(8,128)(2,1)S(1)}, bf16[128,256]{1,0:T(8,128)(2,1)S(1)}, u32[]{:S(2)}, u32[]{:S(2)}) collective-permute-start(bf16[128,256]{1,0:T(8,128)(2,1)S(1)} %add_convert_fusion.1), channel_id=1, source_target_pairs={{0,2},{1,3},{2,0},{3,1},{4,6},{5,7},{6,4},{7,5},{8,10},{9,11},{10,... | collective-permute-start | bytes 196616 | tf_op jit(solution)/shard_map/ppermute | solution.py:123

commit v7 on v6

--- a/solution.py
+++ b/solution.py
@@ -26,7 +26,7 @@
         for i in range(UNROLL):
             slot = k * UNROLL + i
             place = places_ref[slot] - group * places
-            place = jnp.where((place >= 0) & (place < places), place, places)
+            place = jnp.where((slot < count) & (place >= 0) & (place < places), place, places)
             total_ref[place] += tiles_ref[0, 0, slot].astype(jnp.float32)
         return carry
 
@@ -83,9 +83,8 @@
     out_ref[...] = (openness * coupled + (1.0 - openness) * initial).astype(out_ref.dtype)
 
 
-def place_kernel(past, count_ref, place_ref, out_ref):
-    slot = lax.broadcasted_iota(jnp.int32, place_ref.shape, 1)
-    out_ref[...] = jnp.where(slot < count_ref[...], place_ref[...], past)
+def place_kernel(row_ref, column_ref, out_ref):
+    out_ref[...] = row_ref[...] + column_ref[...]
 
 
 def row_groups(rows):
@@ -144,9 +143,9 @@
         return [close[m] for m in sorted(close)], [beyond[m] for m in sorted(beyond)]
 
     row, column = tile_target[0] ^ lax.axis_index("tgt"), tile_source[0] ^ lax.axis_index("src")
-    row = sum(jnp.where(row & b != 0, n_tgt // (2 * b), 0) for b in tgt_bits)
+    row = sum(jnp.where(row & b != 0, n_src * n_tgt // (2 * b), 0) for b in tgt_bits)
     places = local(
-        functools.partial(place_kernel, n_tgt * n_src), "places", jax.ShapeDtypeStruct(row.shape, jnp.int32), 2 * 10**10, tile_count, row * n_src + column
+        place_kernel, "places", jax.ShapeDtypeStruct(row.shape, jnp.int32), 2 * 10**10, row, column
     )
     weights = densify(jnp.concatenate([places[0], tile_count[0]]), tile_values, n_tgt, n_src)
     openness = ((256.0 - stubborn.astype(jnp.float32)) / 256.0)[:, None]

time: 57.7 us -> 57.7 us (level)
  Pallas kernels: 3.82 us -> 4.6 us
  waiting for transfers between devices: 17 us -> 16.3 us
    pallas_call x1, Pallas kernels: 1.29 us -> 2.15 us  [densify(): pl.pallas_call(densify_kernel, out_shape=jax.ShapeDtypeStruct((n_rows * e...]
    add x1 -> x0, other arithmetic: 0.71 us -> none  [shards(): row * n_src + column]
    xor x0 -> x1, other arithmetic: none -> 0.7 us  [shards(): tile_source[0] ^ lax.axis_index('src')]
    ppermute x33, waiting for transfers between devices: 17 us -> 16.3 us  [swap(): lax.ppermute(value, BOTH, [(d, d ^ mask) for d in range(n_src * n_tgt)])]
  transfers between devices with their start and end apart: 33 -> 33, of which waited for: 15 -> 14; matrix products, arithmetic and copies ran while one was open for 2% -> 2% of each run, Pallas kernels for 5% -> 6%
where the time goes in v7:
time: 57.7 us; the launch traced here: 57.6 us
  starting transfers between devices  33.9 us (59%)
  waiting for transfers between devices  16.3 us (28%)
  Pallas kernels  4.6 us (8%)
  between operations  0.98 us (2%)
  other arithmetic  0.84 us (1%)
  matrix products  0.81 us (1%)
    ppermute x33, starting transfers between devices, swap(): lax.ppermute(value, BOTH, [(d, d ^ mask) for d in range(n_src * n_tgt)])  33.9 us
    ppermute x33, waiting for transfers between devices, swap(): lax.ppermute(value, BOTH, [(d, d ^ mask) for d in range(n_src * n_tgt)])  16.3 us
    pallas_call x11, Pallas kernels, local(): pl.pallas_call(kernel, out_shape=out_shapes, in_specs=[whole] * len(args)...  2.45 us
    pallas_call x1, Pallas kernels, densify(): pl.pallas_call(densify_kernel, out_shape=jax.ShapeDtypeStruct((n_rows * e...  2.15 us
  transfers between devices with their start and end apart: 33, of which 14 were waited for; matrix products, arithmetic and copies ran while one was open for 2% of the time, Pallas kernels for 6%

profile of v7, /device:TPU:0, one launch (start us, length us, event | category | flops | bytes accessed | tf_op | source)
XLA Modules:
  0.0 57.6 jit_solution(3141960749407521030)
XLA Ops:
  0.0 3.5 %collective-permute-start.3 = (bf16[128,256]{1,0:T(8,128)(2,1)}, bf16[128,256]{1,0:T(8,128)(2,1)S(1)}, u32[]{:S(2)}, u32[]{:S(2)}) collective-permute-start(bf16[128,256]{1,0:T(8,128)(2,1)} %initial_ref.3), channel_id=1, source_target_pairs={{0,17},{1,16},{2,19},{3,18},{4,21},{5,20},{6,23},{7,22},{8,25},{9,... | collective-permute-start | bytes 196616 | tf_op jit(solution)/shard_map/ppermute | solution.py:122
  3.5 2.5 %collective-permute-start.2 = (bf16[128,256]{1,0:T(8,128)(2,1)}, bf16[128,256]{1,0:T(8,128)(2,1)S(1)}, u32[]{:S(2)}, u32[]{:S(2)}) collective-permute-start(bf16[128,256]{1,0:T(8,128)(2,1)} %initial_ref.3), channel_id=1, source_target_pairs={{0,12},{1,13},{2,14},{3,15},{4,8},{5,9},{6,10},{7,11},{8,4},{9,5},... | collective-permute-start | bytes 196616 | tf_op jit(solution)/shard_map/ppermute | solution.py:122
  6.0 0.4 collective-permute-start.1
  6.4 0.5 collective-permute-start
  7.0 0.7 %xor_bitcast_fusion = (s32[1,144]{1,0:T(1,128)S(1)}, s32[1,144]{1,0:T(1,128)S(1)}) fusion(s32[1,1,144]{2,1,0:T(1,128)} %param.12, s32[]{:T(128)S(6)} %axis_index.25, s32[1,1,144]{2,1,0:T(1,128)} %param.11, s32[]{:T(128)S(6)} %axis_index.22), kind=kLoop, calls=%fused_computation.12 | loop fusion | flops 1296 | bytes 2312 | tf_op jit(solution)/shard_map/xor | solution.py:145
  8.5 2.0 %collective-permute-start.7 = (bf16[128,256]{1,0:T(8,128)(2,1)S(1)}, bf16[128,256]{1,0:T(8,128)(2,1)S(1)}, u32[]{:S(2)}, u32[]{:S(2)}) collective-permute-start(bf16[128,256]{1,0:T(8,128)(2,1)S(1)} %collective-permute-done.3), channel_id=1, source_target_pairs={{0,13},{1,12},{2,15},{3,14},{4,9},{5,8},{6,11},{7,10},{8,5},{9,4},... | collective-permute-start | bytes 196616 | tf_op jit(solution)/shard_map/ppermute | solution.py:122
  10.6 0.7 %collective-permute-start.6 = (bf16[128,256]{1,0:T(8,128)(2,1)S(1)}, bf16[128,256]{1,0:T(8,128)(2,1)S(1)}, u32[]{:S(2)}, u32[]{:S(2)}) collective-permute-start(bf16[128,256]{1,0:T(8,128)(2,1)S(1)} %collective-permute-done.3), channel_id=1, source_target_pairs={{0,9},{1,8},{2,11},{3,10},{4,13},{5,12},{6,15},{7,14},{8,1},{9,0},... | collective-permute-start | bytes 196616 | tf_op jit(solution)/shard_map/ppermute | solution.py:122
  11.3 0.2 collective-permute-start.5
  11.5 0.5 collective-permute-start.4
  12.0 2.2 %densify.1.weights_ref = bf16[512,1024]{1,0:T(8,128)(2,1)S(1)} custom-call(s32[145]{0:T(256)S(1)} %pad_add_fusion.places_ref, bf16[1,1,144,128,128]{4,3,2,1,0:T(8,128)(2,1)S(1)} %copy-done), custom_call_target="tpu_custom_call" | custom-call | flops 2359296 | bytes 4718592 | tf_op jit(solution)/shard_map/densify/pallas_call | solution.py:43
  14.2 0.6 %collective-permute-done.6.refs_6_ = bf16[128,256]{1,0:T(8,128)(2,1)S(1)} collective-permute-done((bf16[128,256]{1,0:T(8,128)(2,1)S(1)}, bf16[128,256]{1,0:T(8,128)(2,1)S(1)}, u32[]{:S(2)}, u32[]{:S(2)}) %collective-permute-start.6) | collective-permute-done | bytes 65568 | tf_op jit(solution)/shard_map/ppermute | solution.py:122
  14.8 0.8 %collective-permute-done.5.refs_5_ = bf16[128,256]{1,0:T(8,128)(2,1)S(1)} collective-permute-done((bf16[128,256]{1,0:T(8,128)(2,1)S(1)}, bf16[128,256]{1,0:T(8,128)(2,1)S(1)}, u32[]{:S(2)}, u32[]{:S(2)}) %collective-permute-start.5) | collective-permute-done | bytes 65568 | tf_op jit(solution)/shard_map/ppermute | solution.py:122
  15.5 0.2 late_first.3
  16.0 0.4 late_rest.3
  16.3 0.5 collective-permute-start.8
  16.8 0.3 collective-permute-done.9
  17.1 1.6 %collective-permute-start.10 = (bf16[128,256]{1,0:T(8,128)(2,1)S(1)}, bf16[128,256]{1,0:T(8,128)(2,1)S(1)}, u32[]{:S(2)}, u32[]{:S(2)}) collective-permute-start(bf16[128,256]{1,0:T(8,128)(2,1)S(1)} %add_convert_fusion.4), channel_id=1, source_target_pairs={{0,2},{1,3},{2,0},{3,1},{4,6},{5,7},{6,4},{7,5},{8,10},{9,11},{10,... | collective-permute-start | bytes 196616 | tf_op jit(solution)/shard_map/ppermute | solution.py:122
  18.8 2.6 %collective-permute-done.10.refs_2_ = bf16[128,256]{1,0:T(8,128)(2,1)S(1)} collective-permute-done((bf16[128,256]{1,0:T(8,128)(2,1)S(1)}, bf16[128,256]{1,0:T(8,128)(2,1)S(1)}, u32[]{:S(2)}, u32[]{:S(2)}) %collective-permute-start.10) | collective-permute-done | bytes 65568 | tf_op jit(solution)/shard_map/ppermute | solution.py:122
  21.6 0.7 %collective-permute-start.14 = (bf16[128,256]{1,0:T(8,128)(2,1)S(1)}, bf16[128,256]{1,0:T(8,128)(2,1)S(1)}, u32[]{:S(2)}, u32[]{:S(2)}) collective-permute-start(bf16[128,256]{1,0:T(8,128)(2,1)S(1)} %update.2.refs_0_), channel_id=1, source_target_pairs={{0,17},{1,16},{2,19},{3,18},{4,21},{5,20},{6,23},{7,22},{8,25},{9,... | collective-permute-start | bytes 196616 | tf_op jit(solution)/shard_map/ppermute | solution.py:122
  22.4 2.5 %collective-permute-start.13 = (bf16[128,256]{1,0:T(8,128)(2,1)S(1)}, bf16[128,256]{1,0:T(8,128)(2,1)S(1)}, u32[]{:S(2)}, u32[]{:S(2)}) collective-permute-start(bf16[128,256]{1,0:T(8,128)(2,1)S(1)} %update.2.refs_0_), channel_id=1, source_target_pairs={{0,12},{1,13},{2,14},{3,15},{4,8},{5,9},{6,10},{7,11},{8,4},{9,5},... | collective-permute-start | bytes 196616 | tf_op jit(solution)/shard_map/ppermute | solution.py:122
  24.9 1.0 %collective-permute-start.11 = (bf16[128,256]{1,0:T(8,128)(2,1)S(1)}, bf16[128,256]{1,0:T(8,128)(2,1)S(1)}, u32[]{:S(2)}, u32[]{:S(2)}) collective-permute-start(bf16[128,256]{1,0:T(8,128)(2,1)S(1)} %update.2.refs_0_), channel_id=1, source_target_pairs={{0,4},{1,5},{2,6},{3,7},{4,0},{5,1},{6,2},{7,3},{8,12},{9,13},{10,... | collective-permute-start | bytes 196616 | tf_op jit(solution)/shard_map/ppermute | solution.py:122
  25.9 0.4 collective-permute-done.14
  26.3 2.6 %collective-permute-start.18 = (bf16[128,256]{1,0:T(8,128)(2,1)S(1)}, bf16[128,256]{1,0:T(8,128)(2,1)S(1)}, u32[]{:S(2)}, u32[]{:S(2)}) collective-permute-start(bf16[128,256]{1,0:T(8,128)(2,1)S(1)} %collective-permute-done.14), channel_id=1, source_target_pairs={{0,13},{1,12},{2,15},{3,14},{4,9},{5,8},{6,11},{7,10},{8,5},{9,4},... | collective-permute-start | bytes 196616 | tf_op jit(solution)/shard_map/ppermute | solution.py:122
  28.9 0.9 %collective-permute-start.16 = (bf16[128,256]{1,0:T(8,128)(2,1)S(1)}, bf16[128,256]{1,0:T(8,128)(2,1)S(1)}, u32[]{:S(2)}, u32[]{:S(2)}) collective-permute-start(bf16[128,256]{1,0:T(8,128)(2,1)S(1)} %collective-permute-done.14), channel_id=1, source_target_pairs={{0,5},{1,4},{2,7},{3,6},{4,1},{5,0},{6,3},{7,2},{8,13},{9,12},{10,... | collective-permute-start | bytes 196616 | tf_op jit(solution)/shard_map/ppermute | solution.py:122
  29.8 0.3 early.2.refs_0_
  30.1 1.3 %collective-permute-done.18.refs_4_ = bf16[128,256]{1,0:T(8,128)(2,1)S(1)} collective-permute-done((bf16[128,256]{1,0:T(8,128)(2,1)S(1)}, bf16[128,256]{1,0:T(8,128)(2,1)S(1)}, u32[]{:S(2)}, u32[]{:S(2)}) %collective-permute-start.18) | collective-permute-done | bytes 65568 | tf_op jit(solution)/shard_map/ppermute | solution.py:122
  31.4 1.3 %collective-permute-done.17.refs_3_ = bf16[128,256]{1,0:T(8,128)(2,1)S(1)} collective-permute-done((bf16[128,256]{1,0:T(8,128)(2,1)S(1)}, bf16[128,256]{1,0:T(8,128)(2,1)S(1)}, u32[]{:S(2)}, u32[]{:S(2)}) %collective-permute-start.17) | collective-permute-done | bytes 65568 | tf_op jit(solution)/shard_map/ppermute | solution.py:122
  33.0 0.4 collective-permute-start.20
  33.4 0.3 late_rest.4
  33.7 0.2 collective-permute-start.19
  33.9 0.4 collective-permute-done.20
  34.3 1.6 %collective-permute-start.21 = (bf16[128,256]{1,0:T(8,128)(2,1)S(1)}, bf16[128,256]{1,0:T(8,128)(2,1)S(1)}, u32[]{:S(2)}, u32[]{:S(2)}) collective-permute-start(bf16[128,256]{1,0:T(8,128)(2,1)S(1)} %add_convert_fusion.3), channel_id=1, source_target_pairs={{0,2},{1,3},{2,0},{3,1},{4,6},{5,7},{6,4},{7,5},{8,10},{9,11},{10,... | collective-permute-start | bytes 196616 | tf_op jit(solution)/shard_map/ppermute | solution.py:122
  35.9 2.8 %collective-permute-done.21.refs_2_ = bf16[128,256]{1,0:T(8,128)(2,1)S(1)} collective-permute-done((bf16[128,256]{1,0:T(8,128)(2,1)S(1)}, bf16[128,256]{1,0:T(8,128)(2,1)S(1)}, u32[]{:S(2)}, u32[]{:S(2)}) %collective-permute-start.21) | collective-permute-done | bytes 65568 | tf_op jit(solution)/shard_map/ppermute | solution.py:122
  38.9 1.1 %collective-permute-start.25 = (bf16[128,256]{1,0:T(8,128)(2,1)S(1)}, bf16[128,256]{1,0:T(8,128)(2,1)S(1)}, u32[]{:S(2)}, u32[]{:S(2)}) collective-permute-start(bf16[128,256]{1,0:T(8,128)(2,1)S(1)} %update.3.refs_0_), channel_id=1, source_target_pairs={{0,17},{1,16},{2,19},{3,18},{4,21},{5,20},{6,23},{7,22},{8,25},{9,... | collective-permute-start | bytes 196616 | tf_op jit(solution)/shard_map/ppermute | solution.py:122
  40.0 2.8 %collective-permute-start.24 = (bf16[128,256]{1,0:T(8,128)(2,1)S(1)}, bf16[128,256]{1,0:T(8,128)(2,1)S(1)}, u32[]{:S(2)}, u32[]{:S(2)}) collective-permute-start(bf16[128,256]{1,0:T(8,128)(2,1)S(1)} %update.3.refs_0_), channel_id=1, source_target_pairs={{0,12},{1,13},{2,14},{3,15},{4,8},{5,9},{6,10},{7,11},{8,4},{9,5},... | collective-permute-start | bytes 196616 | tf_op jit(solution)/shard_map/ppermute | solution.py:122
  42.9 1.2 %collective-permute-start.22 = (bf16[128,256]{1,0:T(8,128)(2,1)S(1)}, bf16[128,256]{1,0:T(8,128)(2,1)S(1)}, u32[]{:S(2)}, u32[]{:S(2)}) collective-permute-start(bf16[128,256]{1,0:T(8,128)(2,1)S(1)} %update.3.refs_0_), channel_id=1, source_target_pairs={{0,4},{1,5},{2,6},{3,7},{4,0},{5,1},{6,2},{7,3},{8,12},{9,13},{10,... | collective-permute-start | bytes 196616 | tf_op jit(solution)/shard_map/ppermute | solution.py:122
  44.1 2.6 %collective-permute-start.29 = (bf16[128,256]{1,0:T(8,128)(2,1)S(1)}, bf16[128,256]{1,0:T(8,128)(2,1)S(1)}, u32[]{:S(2)}, u32[]{:S(2)}) collective-permute-start(bf16[128,256]{1,0:T(8,128)(2,1)S(1)} %collective-permute-done.25), channel_id=1, source_target_pairs={{0,13},{1,12},{2,15},{3,14},{4,9},{5,8},{6,11},{7,10},{8,5},{9,4},... | collective-permute-start | bytes 196616 | tf_op jit(solution)/shard_map/ppermute | solution.py:122
  46.7 1.2 %collective-permute-start.27 = (bf16[128,256]{1,0:T(8,128)(2,1)S(1)}, bf16[128,256]{1,0:T(8,128)(2,1)S(1)}, u32[]{:S(2)}, u32[]{:S(2)}) collective-permute-start(bf16[128,256]{1,0:T(8,128)(2,1)S(1)} %collective-permute-done.25), channel_id=1, source_target_pairs={{0,5},{1,4},{2,7},{3,6},{4,1},{5,0},{6,3},{7,2},{8,13},{9,12},{10,... | collective-permute-start | bytes 196616 | tf_op jit(solution)/shard_map/ppermute | solution.py:122
  48.0 0.3 early.3.refs_0_
  48.3 0.9 %collective-permute-done.29.refs_4_ = bf16[128,256]{1,0:T(8,128)(2,1)S(1)} collective-permute-done((bf16[128,256]{1,0:T(8,128)(2,1)S(1)}, bf16[128,256]{1,0:T(8,128)(2,1)S(1)}, u32[]{:S(2)}, u32[]{:S(2)}) %collective-permute-start.29) | collective-permute-done | bytes 65568 | tf_op jit(solution)/shard_map/ppermute | solution.py:122
  49.2 1.2 %collective-permute-done.28.refs_3_ = bf16[128,256]{1,0:T(8,128)(2,1)S(1)} collective-permute-done((bf16[128,256]{1,0:T(8,128)(2,1)S(1)}, bf16[128,256]{1,0:T(8,128)(2,1)S(1)}, u32[]{:S(2)}, u32[]{:S(2)}) %collective-permute-start.28) | collective-permute-done | bytes 65568 | tf_op jit(solution)/shard_map/ppermute | solution.py:122
  50.6 0.2 late_first.5
  50.8 0.6 %collective-permute-start.31 = (bf16[128,256]{1,0:T(8,128)(2,1)S(1)}, bf16[128,256]{1,0:T(8,128)(2,1)S(1)}, u32[]{:S(2)}, u32[]{:S(2)}) collective-permute-start(bf16[128,256]{1,0:T(8,128)(2,1)S(1)} %late_first.5), channel_id=1, source_target_pairs={{0,1},{1,0},{2,3},{3,2},{4,5},{5,4},{6,7},{7,6},{8,9},{9,8},{10,11... | collective-permute-start | bytes 196616 | tf_op jit(solution)/shard_map/ppermute | solution.py:122
  51.4 0.3 late_rest.5
  51.8 0.5 collective-permute-done.31
  52.3 1.6 %collective-permute-start.32 = (bf16[128,256]{1,0:T(8,128)(2,1)S(1)}, bf16[128,256]{1,0:T(8,128)(2,1)S(1)}, u32[]{:S(2)}, u32[]{:S(2)}) collective-permute-start(bf16[128,256]{1,0:T(8,128)(2,1)S(1)} %add_convert_fusion.1), channel_id=1, source_target_pairs={{0,2},{1,3},{2,0},{3,1},{4,6},{5,7},{6,4},{7,5},{8,10},{9,11},{10,... | collective-permute-start | bytes 196616 | tf_op jit(solution)/shard_map/ppermute | solution.py:122
  53.9 2.8 %collective-permute-done.32 = bf16[128,256]{1,0:T(8,128)(2,1)S(1)} collective-permute-done((bf16[128,256]{1,0:T(8,128)(2,1)S(1)}, bf16[128,256]{1,0:T(8,128)(2,1)S(1)}, u32[]{:S(2)}, u32[]{:S(2)}) %collective-permute-start.32) | collective-permute-done | bytes 65568 | tf_op jit(solution)/shard_map/ppermute | solution.py:122
  56.8 0.8 %fusion.1 = bf16[128,256]{1,0:T(8,128)(2,1)} fusion(bf16[256,256]{1,0:T(8,128)(2,1)S(1)} %copy-done.2, bf16[128,256]{1,0:T(8,128)(2,1)S(1)} %copy-done.1, bf16[128,256]{1,0:T(8,128)(2,1)S(1)} %collective-permute-done.32, bf16[128,256]{1,0:T(8,128)(2,1)S(1)} %collective-permute-done.30, bf16[128,256]{1,0:T(8,128)(2,1)S(1)} %get-tuple-element.20, ...), kind=kOutput, calls=%fused_computation.2 | convolution fusion | flops 17203200 | bytes 459776 | tf_op jit(solution)/shard_map/dot_general | solution.py:181
  (46 shorter events, 1.6 us)
Async XLA Ops:
  0.0 8.5 %collective-permute-start.3 = (bf16[128,256]{1,0:T(8,128)(2,1)}, bf16[128,256]{1,0:T(8,128)(2,1)S(1)}, u32[]{:S(2)}, u32[]{:S(2)}) collective-permute-start(bf16[128,256]{1,0:T(8,128)(2,1)} %initial_ref.3), channel_id=1, source_target_pairs={{0,17},{1,16},{2,19},{3,18},{4,21},{5,20},{6,23},{7,22},{8,25},{9,... | collective-permute-start | bytes 196616 | tf_op jit(solution)/shard_map/ppermute | solution.py:122
  3.5 7.8 %collective-permute-start.2 = (bf16[128,256]{1,0:T(8,128)(2,1)}, bf16[128,256]{1,0:T(8,128)(2,1)S(1)}, u32[]{:S(2)}, u32[]{:S(2)}) collective-permute-start(bf16[128,256]{1,0:T(8,128)(2,1)} %initial_ref.3), channel_id=1, source_target_pairs={{0,12},{1,13},{2,14},{3,15},{4,8},{5,9},{6,10},{7,11},{8,4},{9,5},... | collective-permute-start | bytes 196616 | tf_op jit(solution)/shard_map/ppermute | solution.py:122
  6.0 5.5 %collective-permute-start.1 = (bf16[128,256]{1,0:T(8,128)(2,1)}, bf16[128,256]{1,0:T(8,128)(2,1)S(1)}, u32[]{:S(2)}, u32[]{:S(2)}) collective-permute-start(bf16[128,256]{1,0:T(8,128)(2,1)} %initial_ref.3), channel_id=1, source_target_pairs={{0,8},{1,9},{2,10},{3,11},{4,12},{5,13},{6,14},{7,15},{8,0},{9,1},... | collective-permute-start | bytes 196616 | tf_op jit(solution)/shard_map/ppermute | solution.py:122
  6.4 7.7 %collective-permute-start = (bf16[128,256]{1,0:T(8,128)(2,1)}, bf16[128,256]{1,0:T(8,128)(2,1)S(1)}, u32[]{:S(2)}, u32[]{:S(2)}) collective-permute-start(bf16[128,256]{1,0:T(8,128)(2,1)} %initial_ref.3), channel_id=1, source_target_pairs={{0,4},{1,5},{2,6},{3,7},{4,0},{5,1},{6,2},{7,3},{8,12},{9,13},{10,... | collective-permute-start | bytes 196616 | tf_op jit(solution)/shard_map/ppermute | solution.py:122
  7.7 4.3 %copy-start = (bf16[1,1,144,128,128]{4,3,2,1,0:T(8,128)(2,1)S(1)}, bf16[1,1,144,128,128]{4,3,2,1,0:T(8,128)(2,1)}, u32[]{:S(2)}) copy-start(bf16[1,1,144,128,128]{4,3,2,1,0:T(8,128)(2,1)} %tiles_ref.1) | copy-start | bytes 14155780
  7.7 7.9 %copy-start.1 = (bf16[128,256]{1,0:T(8,128)(2,1)S(1)}, bf16[128,256]{1,0:T(8,128)(2,1)}, u32[]{:S(2)}) copy-start(bf16[128,256]{1,0:T(8,128)(2,1)} %initial_ref.3) | copy-start | bytes 196612
  7.7 11.0 %copy-start.3 = (s32[128]{0:T(128)S(1)}, s32[128]{0:T(128)}, u32[]{:S(2)}) copy-start(s32[128]{0:T(128)} %param.8) | copy-start | bytes 1540
  7.7 13.7 %copy-start.2 = (bf16[256,256]{1,0:T(8,128)(2,1)S(1)}, bf16[256,256]{1,0:T(8,128)(2,1)}, u32[]{:S(2)}) copy-start(bf16[256,256]{1,0:T(8,128)(2,1)} %coupling_ref.3) | copy-start | bytes 393220
  8.5 5.6 %collective-permute-start.7 = (bf16[128,256]{1,0:T(8,128)(2,1)S(1)}, bf16[128,256]{1,0:T(8,128)(2,1)S(1)}, u32[]{:S(2)}, u32[]{:S(2)}) collective-permute-start(bf16[128,256]{1,0:T(8,128)(2,1)S(1)} %collective-permute-done.3), channel_id=1, source_target_pairs={{0,13},{1,12},{2,15},{3,14},{4,9},{5,8},{6,11},{7,10},{8,5},{9,4},... | collective-permute-start | bytes 196616 | tf_op jit(solution)/shard_map/ppermute | solution.py:122
  10.6 4.2 %collective-permute-start.6 = (bf16[128,256]{1,0:T(8,128)(2,1)S(1)}, bf16[128,256]{1,0:T(8,128)(2,1)S(1)}, u32[]{:S(2)}, u32[]{:S(2)}) collective-permute-start(bf16[128,256]{1,0:T(8,128)(2,1)S(1)} %collective-permute-done.3), channel_id=1, source_target_pairs={{0,9},{1,8},{2,11},{3,10},{4,13},{5,12},{6,15},{7,14},{8,1},{9,0},... | collective-permute-start | bytes 196616 | tf_op jit(solution)/shard_map/ppermute | solution.py:122
  11.3 4.3 %collective-permute-start.5 = (bf16[128,256]{1,0:T(8,128)(2,1)S(1)}, bf16[128,256]{1,0:T(8,128)(2,1)S(1)}, u32[]{:S(2)}, u32[]{:S(2)}) collective-permute-start(bf16[128,256]{1,0:T(8,128)(2,1)S(1)} %collective-permute-done.3), channel_id=1, source_target_pairs={{0,5},{1,4},{2,7},{3,6},{4,1},{5,0},{6,3},{7,2},{8,13},{9,12},{10,... | collective-permute-start | bytes 196616 | tf_op jit(solution)/shard_map/ppermute | solution.py:122
  11.5 4.1 %collective-permute-start.4 = (bf16[128,256]{1,0:T(8,128)(2,1)S(1)}, bf16[128,256]{1,0:T(8,128)(2,1)S(1)}, u32[]{:S(2)}, u32[]{:S(2)}) collective-permute-start(bf16[128,256]{1,0:T(8,128)(2,1)S(1)} %collective-permute-done.3), channel_id=1, source_target_pairs={{0,1},{1,0},{2,3},{3,2},{4,5},{5,4},{6,7},{7,6},{8,9},{9,8},{10,11... | collective-permute-start | bytes 196616 | tf_op jit(solution)/shard_map/ppermute | solution.py:122
  15.8 1.3 %collective-permute-start.9 = (bf16[128,256]{1,0:T(8,128)(2,1)S(1)}, bf16[128,256]{1,0:T(8,128)(2,1)S(1)}, u32[]{:S(2)}, u32[]{:S(2)}) collective-permute-start(bf16[128,256]{1,0:T(8,128)(2,1)S(1)} %late_first.3), channel_id=1, source_target_pairs={{0,1},{1,0},{2,3},{3,2},{4,5},{5,4},{6,7},{7,6},{8,9},{9,8},{10,11... | collective-permute-start | bytes 196616 | tf_op jit(solution)/shard_map/ppermute | solution.py:122
  16.3 2.5 %collective-permute-start.8 = (bf16[128,256]{1,0:T(8,128)(2,1)S(1)}, bf16[128,256]{1,0:T(8,128)(2,1)S(1)}, u32[]{:S(2)}, u32[]{:S(2)}) collective-permute-start(bf16[128,256]{1,0:T(8,128)(2,1)S(1)} %get-tuple-element.15), channel_id=1, source_target_pairs={{0,1},{1,0},{2,3},{3,2},{4,5},{5,4},{6,7},{7,6},{8,9},{9,8},{10,11... | collective-permute-start | bytes 196616 | tf_op jit(solution)/shard_map/ppermute | solution.py:122
  17.1 4.3 %collective-permute-start.10 = (bf16[128,256]{1,0:T(8,128)(2,1)S(1)}, bf16[128,256]{1,0:T(8,128)(2,1)S(1)}, u32[]{:S(2)}, u32[]{:S(2)}) collective-permute-start(bf16[128,256]{1,0:T(8,128)(2,1)S(1)} %add_convert_fusion.4), channel_id=1, source_target_pairs={{0,2},{1,3},{2,0},{3,1},{4,6},{5,7},{6,4},{7,5},{8,10},{9,11},{10,... | collective-permute-start | bytes 196616 | tf_op jit(solution)/shard_map/ppermute | solution.py:122
  21.6 4.7 %collective-permute-start.14 = (bf16[128,256]{1,0:T(8,128)(2,1)S(1)}, bf16[128,256]{1,0:T(8,128)(2,1)S(1)}, u32[]{:S(2)}, u32[]{:S(2)}) collective-permute-start(bf16[128,256]{1,0:T(8,128)(2,1)S(1)} %update.2.refs_0_), channel_id=1, source_target_pairs={{0,17},{1,16},{2,19},{3,18},{4,21},{5,20},{6,23},{7,22},{8,25},{9,... | collective-permute-start | bytes 196616 | tf_op jit(solution)/shard_map/ppermute | solution.py:122
  22.4 6.6 %collective-permute-start.13 = (bf16[128,256]{1,0:T(8,128)(2,1)S(1)}, bf16[128,256]{1,0:T(8,128)(2,1)S(1)}, u32[]{:S(2)}, u32[]{:S(2)}) collective-permute-start(bf16[128,256]{1,0:T(8,128)(2,1)S(1)} %update.2.refs_0_), channel_id=1, source_target_pairs={{0,12},{1,13},{2,14},{3,15},{4,8},{5,9},{6,10},{7,11},{8,4},{9,5},... | collective-permute-start | bytes 196616 | tf_op jit(solution)/shard_map/ppermute | solution.py:122
  24.9 4.9 %collective-permute-start.12 = (bf16[128,256]{1,0:T(8,128)(2,1)S(1)}, bf16[128,256]{1,0:T(8,128)(2,1)S(1)}, u32[]{:S(2)}, u32[]{:S(2)}) collective-permute-start(bf16[128,256]{1,0:T(8,128)(2,1)S(1)} %update.2.refs_0_), channel_id=1, source_target_pairs={{0,8},{1,9},{2,10},{3,11},{4,12},{5,13},{6,14},{7,15},{8,0},{9,1},... | collective-permute-start | bytes 196616 | tf_op jit(solution)/shard_map/ppermute | solution.py:122
  24.9 4.9 %collective-permute-start.11 = (bf16[128,256]{1,0:T(8,128)(2,1)S(1)}, bf16[128,256]{1,0:T(8,128)(2,1)S(1)}, u32[]{:S(2)}, u32[]{:S(2)}) collective-permute-start(bf16[128,256]{1,0:T(8,128)(2,1)S(1)} %update.2.refs_0_), channel_id=1, source_target_pairs={{0,4},{1,5},{2,6},{3,7},{4,0},{5,1},{6,2},{7,3},{8,12},{9,13},{10,... | collective-permute-start | bytes 196616 | tf_op jit(solution)/shard_map/ppermute | solution.py:122
  26.3 5.1 %collective-permute-start.18 = (bf16[128,256]{1,0:T(8,128)(2,1)S(1)}, bf16[128,256]{1,0:T(8,128)(2,1)S(1)}, u32[]{:S(2)}, u32[]{:S(2)}) collective-permute-start(bf16[128,256]{1,0:T(8,128)(2,1)S(1)} %collective-permute-done.14), channel_id=1, source_target_pairs={{0,13},{1,12},{2,15},{3,14},{4,9},{5,8},{6,11},{7,10},{8,5},{9,4},... | collective-permute-start | bytes 196616 | tf_op jit(solution)/shard_map/ppermute | solution.py:122
  28.9 3.8 %collective-permute-start.17 = (bf16[128,256]{1,0:T(8,128)(2,1)S(1)}, bf16[128,256]{1,0:T(8,128)(2,1)S(1)}, u32[]{:S(2)}, u32[]{:S(2)}) collective-permute-start(bf16[128,256]{1,0:T(8,128)(2,1)S(1)} %collective-permute-done.14), channel_id=1, source_target_pairs={{0,9},{1,8},{2,11},{3,10},{4,13},{5,12},{6,15},{7,14},{8,1},{9,0},... | collective-permute-start | bytes 196616 | tf_op jit(solution)/shard_map/ppermute | solution.py:122
  28.9 3.8 %collective-permute-start.16 = (bf16[128,256]{1,0:T(8,128)(2,1)S(1)}, bf16[128,256]{1,0:T(8,128)(2,1)S(1)}, u32[]{:S(2)}, u32[]{:S(2)}) collective-permute-start(bf16[128,256]{1,0:T(8,128)(2,1)S(1)} %collective-permute-done.14), channel_id=1, source_target_pairs={{0,5},{1,4},{2,7},{3,6},{4,1},{5,0},{6,3},{7,2},{8,13},{9,12},{10,... | collective-permute-start | bytes 196616 | tf_op jit(solution)/shard_map/ppermute | solution.py:122
  29.8 2.9 %collective-permute-start.15 = (bf16[128,256]{1,0:T(8,128)(2,1)S(1)}, bf16[128,256]{1,0:T(8,128)(2,1)S(1)}, u32[]{:S(2)}, u32[]{:S(2)}) collective-permute-start(bf16[128,256]{1,0:T(8,128)(2,1)S(1)} %collective-permute-done.14), channel_id=1, source_target_pairs={{0,1},{1,0},{2,3},{3,2},{4,5},{5,4},{6,7},{7,6},{8,9},{9,8},{10,11... | collective-permute-start | bytes 196616 | tf_op jit(solution)/shard_map/ppermute | solution.py:122
  33.0 1.4 %collective-permute-start.20 = (bf16[128,256]{1,0:T(8,128)(2,1)S(1)}, bf16[128,256]{1,0:T(8,128)(2,1)S(1)}, u32[]{:S(2)}, u32[]{:S(2)}) collective-permute-start(bf16[128,256]{1,0:T(8,128)(2,1)S(1)} %late_first.4), channel_id=1, source_target_pairs={{0,1},{1,0},{2,3},{3,2},{4,5},{5,4},{6,7},{7,6},{8,9},{9,8},{10,11... | collective-permute-start | bytes 196616 | tf_op jit(solution)/shard_map/ppermute | solution.py:122
  33.7 2.2 %collective-permute-start.19 = (bf16[128,256]{1,0:T(8,128)(2,1)S(1)}, bf16[128,256]{1,0:T(8,128)(2,1)S(1)}, u32[]{:S(2)}, u32[]{:S(2)}) collective-permute-start(bf16[128,256]{1,0:T(8,128)(2,1)S(1)} %get-tuple-element.18), channel_id=1, source_target_pairs={{0,1},{1,0},{2,3},{3,2},{4,5},{5,4},{6,7},{7,6},{8,9},{9,8},{10,11... | collective-permute-start | bytes 196616 | tf_op jit(solution)/shard_map/ppermute | solution.py:122
  34.3 4.4 %collective-permute-start.21 = (bf16[128,256]{1,0:T(8,128)(2,1)S(1)}, bf16[128,256]{1,0:T(8,128)(2,1)S(1)}, u32[]{:S(2)}, u32[]{:S(2)}) collective-permute-start(bf16[128,256]{1,0:T(8,128)(2,1)S(1)} %add_convert_fusion.3), channel_id=1, source_target_pairs={{0,2},{1,3},{2,0},{3,1},{4,6},{5,7},{6,4},{7,5},{8,10},{9,11},{10,... | collective-permute-start | bytes 196616 | tf_op jit(solution)/shard_map/ppermute | solution.py:122
  38.9 5.2 %collective-permute-start.25 = (bf16[128,256]{1,0:T(8,128)(2,1)S(1)}, bf16[128,256]{1,0:T(8,128)(2,1)S(1)}, u32[]{:S(2)}, u32[]{:S(2)}) collective-permute-start(bf16[128,256]{1,0:T(8,128)(2,1)S(1)} %update.3.refs_0_), channel_id=1, source_target_pairs={{0,17},{1,16},{2,19},{3,18},{4,21},{5,20},{6,23},{7,22},{8,25},{9,... | collective-permute-start | bytes 196616 | tf_op jit(solution)/shard_map/ppermute | solution.py:122
  40.0 6.7 %collective-permute-start.24 = (bf16[128,256]{1,0:T(8,128)(2,1)S(1)}, bf16[128,256]{1,0:T(8,128)(2,1)S(1)}, u32[]{:S(2)}, u32[]{:S(2)}) collective-permute-start(bf16[128,256]{1,0:T(8,128)(2,1)S(1)} %update.3.refs_0_), channel_id=1, source_target_pairs={{0,12},{1,13},{2,14},{3,15},{4,8},{5,9},{6,10},{7,11},{8,4},{9,5},... | collective-permute-start | bytes 196616 | tf_op jit(solution)/shard_map/ppermute | solution.py:122
  42.8 5.1 %collective-permute-start.23 = (bf16[128,256]{1,0:T(8,128)(2,1)S(1)}, bf16[128,256]{1,0:T(8,128)(2,1)S(1)}, u32[]{:S(2)}, u32[]{:S(2)}) collective-permute-start(bf16[128,256]{1,0:T(8,128)(2,1)S(1)} %update.3.refs_0_), channel_id=1, source_target_pairs={{0,8},{1,9},{2,10},{3,11},{4,12},{5,13},{6,14},{7,15},{8,0},{9,1},... | collective-permute-start | bytes 196616 | tf_op jit(solution)/shard_map/ppermute | solution.py:122
  42.9 5.1 %collective-permute-start.22 = (bf16[128,256]{1,0:T(8,128)(2,1)S(1)}, bf16[128,256]{1,0:T(8,128)(2,1)S(1)}, u32[]{:S(2)}, u32[]{:S(2)}) collective-permute-start(bf16[128,256]{1,0:T(8,128)(2,1)S(1)} %update.3.refs_0_), channel_id=1, source_target_pairs={{0,4},{1,5},{2,6},{3,7},{4,0},{5,1},{6,2},{7,3},{8,12},{9,13},{10,... | collective-permute-start | bytes 196616 | tf_op jit(solution)/shard_map/ppermute | solution.py:122
  44.1 5.1 %collective-permute-start.29 = (bf16[128,256]{1,0:T(8,128)(2,1)S(1)}, bf16[128,256]{1,0:T(8,128)(2,1)S(1)}, u32[]{:S(2)}, u32[]{:S(2)}) collective-permute-start(bf16[128,256]{1,0:T(8,128)(2,1)S(1)} %collective-permute-done.25), channel_id=1, source_target_pairs={{0,13},{1,12},{2,15},{3,14},{4,9},{5,8},{6,11},{7,10},{8,5},{9,4},... | collective-permute-start | bytes 196616 | tf_op jit(solution)/shard_map/ppermute | solution.py:122
  46.7 3.8 %collective-permute-start.28 = (bf16[128,256]{1,0:T(8,128)(2,1)S(1)}, bf16[128,256]{1,0:T(8,128)(2,1)S(1)}, u32[]{:S(2)}, u32[]{:S(2)}) collective-permute-start(bf16[128,256]{1,0:T(8,128)(2,1)S(1)} %collective-permute-done.25), channel_id=1, source_target_pairs={{0,9},{1,8},{2,11},{3,10},{4,13},{5,12},{6,15},{7,14},{8,1},{9,0},... | collective-permute-start | bytes 196616 | tf_op jit(solution)/shard_map/ppermute | solution.py:122
  46.7 3.9 %collective-permute-start.27 = (bf16[128,256]{1,0:T(8,128)(2,1)S(1)}, bf16[128,256]{1,0:T(8,128)(2,1)S(1)}, u32[]{:S(2)}, u32[]{:S(2)}) collective-permute-start(bf16[128,256]{1,0:T(8,128)(2,1)S(1)} %collective-permute-done.25), channel_id=1, source_target_pairs={{0,5},{1,4},{2,7},{3,6},{4,1},{5,0},{6,3},{7,2},{8,13},{9,12},{10,... | collective-permute-start | bytes 196616 | tf_op jit(solution)/shard_map/ppermute | solution.py:122
  47.9 2.7 %collective-permute-start.26 = (bf16[128,256]{1,0:T(8,128)(2,1)S(1)}, bf16[128,256]{1,0:T(8,128)(2,1)S(1)}, u32[]{:S(2)}, u32[]{:S(2)}) collective-permute-start(bf16[128,256]{1,0:T(8,128)(2,1)S(1)} %collective-permute-done.25), channel_id=1, source_target_pairs={{0,1},{1,0},{2,3},{3,2},{4,5},{5,4},{6,7},{7,6},{8,9},{9,8},{10,11... | collective-permute-start | bytes 196616 | tf_op jit(solution)/shard_map/ppermute | solution.py:122
  50.8 1.5 %collective-permute-start.31 = (bf16[128,256]{1,0:T(8,128)(2,1)S(1)}, bf16[128,256]{1,0:T(8,128)(2,1)S(1)}, u32[]{:S(2)}, u32[]{:S(2)}) collective-permute-start(bf16[128,256]{1,0:T(8,128)(2,1)S(1)} %late_first.5), channel_id=1, source_target_pairs={{0,1},{1,0},{2,3},{3,2},{4,5},{5,4},{6,7},{7,6},{8,9},{9,8},{10,11... | collective-permute-start | bytes 196616 | tf_op jit(solution)/shard_map/ppermute | solution.py:122
  51.7 2.2 %collective-permute-start.30 = (bf16[128,256]{1,0:T(8,128)(2,1)S(1)}, bf16[128,256]{1,0:T(8,128)(2,1)S(1)}, u32[]{:S(2)}, u32[]{:S(2)}) collective-permute-start(bf16[128,256]{1,0:T(8,128)(2,1)S(1)} %get-tuple-element.21), channel_id=1, source_target_pairs={{0,1},{1,0},{2,3},{3,2},{4,5},{5,4},{6,7},{7,6},{8,9},{9,8},{10,11... | collective-permute-start | bytes 196616 | tf_op jit(solution)/shard_map/ppermute | solution.py:122
  52.3 4.4 %collective-permute-start.32 = (bf16[128,256]{1,0:T(8,128)(2,1)S(1)}, bf16[128,256]{1,0:T(8,128)(2,1)S(1)}, u32[]{:S(2)}, u32[]{:S(2)}) collective-permute-start(bf16[128,256]{1,0:T(8,128)(2,1)S(1)} %add_convert_fusion.1), channel_id=1, source_target_pairs={{0,2},{1,3},{2,0},{3,1},{4,6},{5,7},{6,4},{7,5},{8,10},{9,11},{10,... | collective-permute-start | bytes 196616 | tf_op jit(solution)/shard_map/ppermute | solution.py:122

commit v8 on v6

--- a/solution.py
+++ b/solution.py
@@ -83,6 +83,19 @@
     out_ref[...] = (openness * coupled + (1.0 - openness) * initial).astype(out_ref.dtype)
 
 
+def last_kernel(coupling_ref, openness_ref, initial_ref, *refs):
+    terms, (out_ref, held_ref, sems) = refs[:-3], refs[-3:]
+    rows = held_ref.shape[0] // 2
+    copies = []
+    for i in range(2):
+        at = pl.ds(i * rows, rows)
+        update_kernel(coupling_ref, openness_ref.at[at], initial_ref.at[at], *(ref.at[at] for ref in terms), held_ref.at[at])
+        copies.append(pltpu.make_async_copy(held_ref.at[at], out_ref.at[at], sems.at[i]))
+        copies[i].start()
+    for copy in copies:
+        copy.wait()
+
+
 def place_kernel(past, count_ref, place_ref, out_ref):
     slot = lax.broadcasted_iota(jnp.int32, place_ref.shape, 1)
     out_ref[...] = jnp.where(slot < count_ref[...], place_ref[...], past)
@@ -150,7 +163,6 @@
     )
     weights = densify(jnp.concatenate([places[0], tile_count[0]]), tile_values, n_tgt, n_src)
     openness = ((256.0 - stubborn.astype(jnp.float32)) / 256.0)[:, None]
-    base = (1.0 - openness) * initial.astype(jnp.float32)
 
     def add(a, b):
         return (a.astype(jnp.float32) + b.astype(jnp.float32)).astype(jnp.bfloat16)
@@ -179,9 +191,17 @@
             terms = [total[:half], swap(total[half:], 0, bit)]
         if step < STEPS - 1:
             opinion = local(update_kernel, "update", jax.ShapeDtypeStruct(initial.shape, jnp.bfloat16), 2 * own_rows * topics**2, coupling, openness, initial, *terms)
-    coupled = jnp.dot(functools.reduce(add, terms), coupling, preferred_element_type=jnp.float32)
-    opinion = (openness * coupled + base).astype(jnp.bfloat16)
-    return opinion
+    whole = pl.BlockSpec(memory_space=pltpu.VMEM)
+    return pl.pallas_call(
+        last_kernel,
+        out_shape=jax.ShapeDtypeStruct(initial.shape, jnp.bfloat16),
+        in_specs=[whole] * (3 + len(terms)),
+        out_specs=pl.BlockSpec(memory_space=pltpu.HBM),
+        scratch_shapes=[pltpu.VMEM(initial.shape, jnp.bfloat16), pltpu.SemaphoreType.DMA((2,))],
+        compiler_params=pltpu.CompilerParams(vmem_limit_bytes=LOCAL * 2**20),
+        cost_estimate=pl.CostEstimate(flops=2 * own_rows * topics**2, bytes_accessed=2 * own_rows * topics, transcendentals=0),
+        name="last",
+    )(coupling, openness, initial, *terms)
 
 
 def solution(mesh):

time: 57.7 us -> 57.7 us (level)
  matrix products: 0.81 us -> 0 us
  Pallas kernels: 3.82 us -> 4.51 us
    pallas_call x0 -> x1, Pallas kernels: none -> 0.81 us  [shards(): pl.pallas_call(last_kernel, out_shape=jax.ShapeDtypeStruct(initial.shape,...]
    dot_general x1 -> x0, matrix products: 0.81 us -> none  [shards(): jnp.dot(functools.reduce(add, terms), coupling, preferred_element_type=jn...]
where the time goes in v8:
time: 57.7 us; the launch traced here: 57.5 us
  starting transfers between devices  34.2 us (59%)
  waiting for transfers between devices  17.1 us (30%)
  Pallas kernels  4.51 us (8%)
  other arithmetic  0.84 us (1%)
  between operations  0.8 us (1%)
    ppermute x33, starting transfers between devices, swap(): lax.ppermute(value, BOTH, [(d, d ^ mask) for d in range(n_src * n_tgt)])  34.2 us
    ppermute x33, waiting for transfers between devices, swap(): lax.ppermute(value, BOTH, [(d, d ^ mask) for d in range(n_src * n_tgt)])  17.1 us
    pallas_call x11, Pallas kernels, local(): pl.pallas_call(kernel, out_shape=out_shapes, in_specs=[whole] * len(args)...  2.53 us
    pallas_call x1, Pallas kernels, densify(): pl.pallas_call(densify_kernel, out_shape=jax.ShapeDtypeStruct((n_rows * e...  1.16 us
  transfers between devices with their start and end apart: 33, of which 15 were waited for; matrix products, arithmetic and copies ran while one was open for 2% of the time, Pallas kernels for 5%

profile of v8, /device:TPU:0, one launch (start us, length us, event | category | flops | bytes accessed | tf_op | source)
XLA Modules:
  0.0 57.5 jit_solution(10526638133240104350)
XLA Ops:
  0.0 3.5 %collective-permute-start.3 = (bf16[128,256]{1,0:T(8,128)(2,1)}, bf16[128,256]{1,0:T(8,128)(2,1)S(1)}, u32[]{:S(2)}, u32[]{:S(2)}) collective-permute-start(bf16[128,256]{1,0:T(8,128)(2,1)} %initial_ref.5), channel_id=1, source_target_pairs={{0,17},{1,16},{2,19},{3,18},{4,21},{5,20},{6,23},{7,22},{8,25},{9,... | collective-permute-start | bytes 196616 | tf_op jit(solution)/shard_map/ppermute | solution.py:136
  3.5 2.5 %collective-permute-start.2 = (bf16[128,256]{1,0:T(8,128)(2,1)}, bf16[128,256]{1,0:T(8,128)(2,1)S(1)}, u32[]{:S(2)}, u32[]{:S(2)}) collective-permute-start(bf16[128,256]{1,0:T(8,128)(2,1)} %initial_ref.5), channel_id=1, source_target_pairs={{0,12},{1,13},{2,14},{3,15},{4,8},{5,9},{6,10},{7,11},{8,4},{9,5},... | collective-permute-start | bytes 196616 | tf_op jit(solution)/shard_map/ppermute | solution.py:136
  6.0 0.4 collective-permute-start.1
  6.4 0.5 collective-permute-start
  7.6 0.7 %add_bitcast_fusion.place_ref = s32[1,144]{1,0:T(1,128)S(1)} fusion(s32[1,1,144]{2,1,0:T(1,128)} %param.12, s32[1,1,144]{2,1,0:T(1,128)} %param.11, s32[]{:T(128)S(6)} %axis_index.25, s32[]{:T(128)S(6)} %axis_index.22), kind=kLoop, calls=%fused_computation.7 | loop fusion | flops 1584 | bytes 1736 | tf_op jit(solution)/shard_map/add | solution.py:162
  8.4 2.0 %collective-permute-start.7 = (bf16[128,256]{1,0:T(8,128)(2,1)S(1)}, bf16[128,256]{1,0:T(8,128)(2,1)S(1)}, u32[]{:S(2)}, u32[]{:S(2)}) collective-permute-start(bf16[128,256]{1,0:T(8,128)(2,1)S(1)} %collective-permute-done.3), channel_id=1, source_target_pairs={{0,13},{1,12},{2,15},{3,14},{4,9},{5,8},{6,11},{7,10},{8,5},{9,4},... | collective-permute-start | bytes 196616 | tf_op jit(solution)/shard_map/ppermute | solution.py:136
  10.5 0.7 %collective-permute-start.6 = (bf16[128,256]{1,0:T(8,128)(2,1)S(1)}, bf16[128,256]{1,0:T(8,128)(2,1)S(1)}, u32[]{:S(2)}, u32[]{:S(2)}) collective-permute-start(bf16[128,256]{1,0:T(8,128)(2,1)S(1)} %collective-permute-done.3), channel_id=1, source_target_pairs={{0,9},{1,8},{2,11},{3,10},{4,13},{5,12},{6,15},{7,14},{8,1},{9,0},... | collective-permute-start | bytes 196616 | tf_op jit(solution)/shard_map/ppermute | solution.py:136
  11.4 0.5 collective-permute-start.4
  11.9 1.2 %densify.1.weights_ref = bf16[512,1024]{1,0:T(8,128)(2,1)S(1)} custom-call(s32[145]{0:T(256)S(1)} %pad_add_fusion.places_ref, bf16[1,1,144,128,128]{4,3,2,1,0:T(8,128)(2,1)S(1)} %copy-done), custom_call_target="tpu_custom_call" | custom-call | flops 2359296 | bytes 4718592 | tf_op jit(solution)/shard_map/densify/pallas_call | solution.py:43
  13.1 0.5 collective-permute-done.7.refs_7_
  13.6 1.1 %collective-permute-done.6.refs_6_ = bf16[128,256]{1,0:T(8,128)(2,1)S(1)} collective-permute-done((bf16[128,256]{1,0:T(8,128)(2,1)S(1)}, bf16[128,256]{1,0:T(8,128)(2,1)S(1)}, u32[]{:S(2)}, u32[]{:S(2)}) %collective-permute-start.6) | collective-permute-done | bytes 65568 | tf_op jit(solution)/shard_map/ppermute | solution.py:136
  14.7 0.7 %collective-permute-done.5.refs_5_ = bf16[128,256]{1,0:T(8,128)(2,1)S(1)} collective-permute-done((bf16[128,256]{1,0:T(8,128)(2,1)S(1)}, bf16[128,256]{1,0:T(8,128)(2,1)S(1)}, u32[]{:S(2)}, u32[]{:S(2)}) %collective-permute-start.5) | collective-permute-done | bytes 65568 | tf_op jit(solution)/shard_map/ppermute | solution.py:136
  15.4 0.2 late_first.3
  15.8 0.4 late_rest.3
  16.2 0.5 collective-permute-start.8
  16.7 0.3 collective-permute-done.9
  17.0 1.6 %collective-permute-start.10 = (bf16[128,256]{1,0:T(8,128)(2,1)S(1)}, bf16[128,256]{1,0:T(8,128)(2,1)S(1)}, u32[]{:S(2)}, u32[]{:S(2)}) collective-permute-start(bf16[128,256]{1,0:T(8,128)(2,1)S(1)} %add_convert_fusion.2), channel_id=1, source_target_pairs={{0,2},{1,3},{2,0},{3,1},{4,6},{5,7},{6,4},{7,5},{8,10},{9,11},{10,... | collective-permute-start | bytes 196616 | tf_op jit(solution)/shard_map/ppermute | solution.py:136
  18.7 2.6 %collective-permute-done.10.refs_2_ = bf16[128,256]{1,0:T(8,128)(2,1)S(1)} collective-permute-done((bf16[128,256]{1,0:T(8,128)(2,1)S(1)}, bf16[128,256]{1,0:T(8,128)(2,1)S(1)}, u32[]{:S(2)}, u32[]{:S(2)}) %collective-permute-start.10) | collective-permute-done | bytes 65568 | tf_op jit(solution)/shard_map/ppermute | solution.py:136
  21.5 0.9 %collective-permute-start.14 = (bf16[128,256]{1,0:T(8,128)(2,1)S(1)}, bf16[128,256]{1,0:T(8,128)(2,1)S(1)}, u32[]{:S(2)}, u32[]{:S(2)}) collective-permute-start(bf16[128,256]{1,0:T(8,128)(2,1)S(1)} %update.2.refs_0_), channel_id=1, source_target_pairs={{0,17},{1,16},{2,19},{3,18},{4,21},{5,20},{6,23},{7,22},{8,25},{9,... | collective-permute-start | bytes 196616 | tf_op jit(solution)/shard_map/ppermute | solution.py:136
  22.4 2.5 %collective-permute-start.13 = (bf16[128,256]{1,0:T(8,128)(2,1)S(1)}, bf16[128,256]{1,0:T(8,128)(2,1)S(1)}, u32[]{:S(2)}, u32[]{:S(2)}) collective-permute-start(bf16[128,256]{1,0:T(8,128)(2,1)S(1)} %update.2.refs_0_), channel_id=1, source_target_pairs={{0,12},{1,13},{2,14},{3,15},{4,8},{5,9},{6,10},{7,11},{8,4},{9,5},... | collective-permute-start | bytes 196616 | tf_op jit(solution)/shard_map/ppermute | solution.py:136
  24.9 1.0 %collective-permute-start.11 = (bf16[128,256]{1,0:T(8,128)(2,1)S(1)}, bf16[128,256]{1,0:T(8,128)(2,1)S(1)}, u32[]{:S(2)}, u32[]{:S(2)}) collective-permute-start(bf16[128,256]{1,0:T(8,128)(2,1)S(1)} %update.2.refs_0_), channel_id=1, source_target_pairs={{0,4},{1,5},{2,6},{3,7},{4,0},{5,1},{6,2},{7,3},{8,12},{9,13},{10,... | collective-permute-start | bytes 196616 | tf_op jit(solution)/shard_map/ppermute | solution.py:136
  25.9 0.3 collective-permute-done.14
  26.2 2.6 %collective-permute-start.18 = (bf16[128,256]{1,0:T(8,128)(2,1)S(1)}, bf16[128,256]{1,0:T(8,128)(2,1)S(1)}, u32[]{:S(2)}, u32[]{:S(2)}) collective-permute-start(bf16[128,256]{1,0:T(8,128)(2,1)S(1)} %collective-permute-done.14), channel_id=1, source_target_pairs={{0,13},{1,12},{2,15},{3,14},{4,9},{5,8},{6,11},{7,10},{8,5},{9,4},... | collective-permute-start | bytes 196616 | tf_op jit(solution)/shard_map/ppermute | solution.py:136
  28.8 0.9 %collective-permute-start.16 = (bf16[128,256]{1,0:T(8,128)(2,1)S(1)}, bf16[128,256]{1,0:T(8,128)(2,1)S(1)}, u32[]{:S(2)}, u32[]{:S(2)}) collective-permute-start(bf16[128,256]{1,0:T(8,128)(2,1)S(1)} %collective-permute-done.14), channel_id=1, source_target_pairs={{0,5},{1,4},{2,7},{3,6},{4,1},{5,0},{6,3},{7,2},{8,13},{9,12},{10,... | collective-permute-start | bytes 196616 | tf_op jit(solution)/shard_map/ppermute | solution.py:136
  29.7 0.3 early.2.refs_0_
  30.0 1.2 %collective-permute-done.18.refs_4_ = bf16[128,256]{1,0:T(8,128)(2,1)S(1)} collective-permute-done((bf16[128,256]{1,0:T(8,128)(2,1)S(1)}, bf16[128,256]{1,0:T(8,128)(2,1)S(1)}, u32[]{:S(2)}, u32[]{:S(2)}) %collective-permute-start.18) | collective-permute-done | bytes 65568 | tf_op jit(solution)/shard_map/ppermute | solution.py:136
  31.3 1.4 %collective-permute-done.17.refs_3_ = bf16[128,256]{1,0:T(8,128)(2,1)S(1)} collective-permute-done((bf16[128,256]{1,0:T(8,128)(2,1)S(1)}, bf16[128,256]{1,0:T(8,128)(2,1)S(1)}, u32[]{:S(2)}, u32[]{:S(2)}) %collective-permute-start.17) | collective-permute-done | bytes 65568 | tf_op jit(solution)/shard_map/ppermute | solution.py:136
  32.8 0.4 collective-permute-start.20
  33.3 0.3 late_rest.4
  33.5 0.2 collective-permute-start.19
  33.7 0.4 collective-permute-done.20
  34.2 1.6 %collective-permute-start.21 = (bf16[128,256]{1,0:T(8,128)(2,1)S(1)}, bf16[128,256]{1,0:T(8,128)(2,1)S(1)}, u32[]{:S(2)}, u32[]{:S(2)}) collective-permute-start(bf16[128,256]{1,0:T(8,128)(2,1)S(1)} %add_convert_fusion.1), channel_id=1, source_target_pairs={{0,2},{1,3},{2,0},{3,1},{4,6},{5,7},{6,4},{7,5},{8,10},{9,11},{10,... | collective-permute-start | bytes 196616 | tf_op jit(solution)/shard_map/ppermute | solution.py:136
  35.8 2.8 %collective-permute-done.21.refs_2_ = bf16[128,256]{1,0:T(8,128)(2,1)S(1)} collective-permute-done((bf16[128,256]{1,0:T(8,128)(2,1)S(1)}, bf16[128,256]{1,0:T(8,128)(2,1)S(1)}, u32[]{:S(2)}, u32[]{:S(2)}) %collective-permute-start.21) | collective-permute-done | bytes 65568 | tf_op jit(solution)/shard_map/ppermute | solution.py:136
  38.8 1.2 %collective-permute-start.25 = (bf16[128,256]{1,0:T(8,128)(2,1)S(1)}, bf16[128,256]{1,0:T(8,128)(2,1)S(1)}, u32[]{:S(2)}, u32[]{:S(2)}) collective-permute-start(bf16[128,256]{1,0:T(8,128)(2,1)S(1)} %update.3.refs_0_), channel_id=1, source_target_pairs={{0,17},{1,16},{2,19},{3,18},{4,21},{5,20},{6,23},{7,22},{8,25},{9,... | collective-permute-start | bytes 196616 | tf_op jit(solution)/shard_map/ppermute | solution.py:136
  40.0 2.8 %collective-permute-start.24 = (bf16[128,256]{1,0:T(8,128)(2,1)S(1)}, bf16[128,256]{1,0:T(8,128)(2,1)S(1)}, u32[]{:S(2)}, u32[]{:S(2)}) collective-permute-start(bf16[128,256]{1,0:T(8,128)(2,1)S(1)} %update.3.refs_0_), channel_id=1, source_target_pairs={{0,12},{1,13},{2,14},{3,15},{4,8},{5,9},{6,10},{7,11},{8,4},{9,5},... | collective-permute-start | bytes 196616 | tf_op jit(solution)/shard_map/ppermute | solution.py:136
  42.9 1.1 %collective-permute-start.22 = (bf16[128,256]{1,0:T(8,128)(2,1)S(1)}, bf16[128,256]{1,0:T(8,128)(2,1)S(1)}, u32[]{:S(2)}, u32[]{:S(2)}) collective-permute-start(bf16[128,256]{1,0:T(8,128)(2,1)S(1)} %update.3.refs_0_), channel_id=1, source_target_pairs={{0,4},{1,5},{2,6},{3,7},{4,0},{5,1},{6,2},{7,3},{8,12},{9,13},{10,... | collective-permute-start | bytes 196616 | tf_op jit(solution)/shard_map/ppermute | solution.py:136
  44.1 2.8 %collective-permute-start.29 = (bf16[128,256]{1,0:T(8,128)(2,1)S(1)}, bf16[128,256]{1,0:T(8,128)(2,1)S(1)}, u32[]{:S(2)}, u32[]{:S(2)}) collective-permute-start(bf16[128,256]{1,0:T(8,128)(2,1)S(1)} %collective-permute-done.25), channel_id=1, source_target_pairs={{0,13},{1,12},{2,15},{3,14},{4,9},{5,8},{6,11},{7,10},{8,5},{9,4},... | collective-permute-start | bytes 196616 | tf_op jit(solution)/shard_map/ppermute | solution.py:136
  46.9 1.0 %collective-permute-start.27 = (bf16[128,256]{1,0:T(8,128)(2,1)S(1)}, bf16[128,256]{1,0:T(8,128)(2,1)S(1)}, u32[]{:S(2)}, u32[]{:S(2)}) collective-permute-start(bf16[128,256]{1,0:T(8,128)(2,1)S(1)} %collective-permute-done.25), channel_id=1, source_target_pairs={{0,5},{1,4},{2,7},{3,6},{4,1},{5,0},{6,3},{7,2},{8,13},{9,12},{10,... | collective-permute-start | bytes 196616 | tf_op jit(solution)/shard_map/ppermute | solution.py:136
  48.0 0.3 early.3.refs_0_
  48.3 1.0 %collective-permute-done.29.refs_4_ = bf16[128,256]{1,0:T(8,128)(2,1)S(1)} collective-permute-done((bf16[128,256]{1,0:T(8,128)(2,1)S(1)}, bf16[128,256]{1,0:T(8,128)(2,1)S(1)}, u32[]{:S(2)}, u32[]{:S(2)}) %collective-permute-start.29) | collective-permute-done | bytes 65568 | tf_op jit(solution)/shard_map/ppermute | solution.py:136
  49.3 1.4 %collective-permute-done.28.refs_3_ = bf16[128,256]{1,0:T(8,128)(2,1)S(1)} collective-permute-done((bf16[128,256]{1,0:T(8,128)(2,1)S(1)}, bf16[128,256]{1,0:T(8,128)(2,1)S(1)}, u32[]{:S(2)}, u32[]{:S(2)}) %collective-permute-start.28) | collective-permute-done | bytes 65568 | tf_op jit(solution)/shard_map/ppermute | solution.py:136
  51.0 0.4 collective-permute-start.31
  51.4 0.3 late_rest.5
  51.7 0.2 collective-permute-start.30
  51.9 0.4 collective-permute-done.31
  52.3 1.6 %collective-permute-start.32 = (bf16[128,256]{1,0:T(8,128)(2,1)S(1)}, bf16[128,256]{1,0:T(8,128)(2,1)S(1)}, u32[]{:S(2)}, u32[]{:S(2)}) collective-permute-start(bf16[128,256]{1,0:T(8,128)(2,1)S(1)} %add_convert_fusion), channel_id=1, source_target_pairs={{0,2},{1,3},{2,0},{3,1},{4,6},{5,7},{6,4},{7,5},{8,10},{9,11},{10,... | collective-permute-start | bytes 196616 | tf_op jit(solution)/shard_map/ppermute | solution.py:136
  53.9 2.8 %collective-permute-done.32.refs_2_ = bf16[128,256]{1,0:T(8,128)(2,1)S(1)} collective-permute-done((bf16[128,256]{1,0:T(8,128)(2,1)S(1)}, bf16[128,256]{1,0:T(8,128)(2,1)S(1)}, u32[]{:S(2)}, u32[]{:S(2)}) %collective-permute-start.32) | collective-permute-done | bytes 65568 | tf_op jit(solution)/shard_map/ppermute | solution.py:136
  56.7 0.8 %last.1 = bf16[128,256]{1,0:T(8,128)(2,1)} custom-call(bf16[256,256]{1,0:T(8,128)(2,1)S(1)} %copy-done.2, f32[128,1]{1,0:T(8,128)S(1)} %copy.10.openness_ref, bf16[128,256]{1,0:T(8,128)(2,1)S(1)} %copy-done.1, bf16[128,256]{1,0:T(8,128)(2,1)S(1)} %get-tuple-element.20.refs_0_, bf16[128,256]{1,0:T(8,128)(2,1)S(1)} %collective-permute-done.30.refs_1_, ...), custom_call_target="tpu_custom_call" | custom-call | flops 16777216 | bytes 65536 | tf_op jit(solution)/shard_map/last/pallas_call | solution.py:195
  (46 shorter events, 1.9 us)
Async XLA Ops:
  0.0 8.4 %collective-permute-start.3 = (bf16[128,256]{1,0:T(8,128)(2,1)}, bf16[128,256]{1,0:T(8,128)(2,1)S(1)}, u32[]{:S(2)}, u32[]{:S(2)}) collective-permute-start(bf16[128,256]{1,0:T(8,128)(2,1)} %initial_ref.5), channel_id=1, source_target_pairs={{0,17},{1,16},{2,19},{3,18},{4,21},{5,20},{6,23},{7,22},{8,25},{9,... | collective-permute-start | bytes 196616 | tf_op jit(solution)/shard_map/ppermute | solution.py:136
  3.5 7.7 %collective-permute-start.2 = (bf16[128,256]{1,0:T(8,128)(2,1)}, bf16[128,256]{1,0:T(8,128)(2,1)S(1)}, u32[]{:S(2)}, u32[]{:S(2)}) collective-permute-start(bf16[128,256]{1,0:T(8,128)(2,1)} %initial_ref.5), channel_id=1, source_target_pairs={{0,12},{1,13},{2,14},{3,15},{4,8},{5,9},{6,10},{7,11},{8,4},{9,5},... | collective-permute-start | bytes 196616 | tf_op jit(solution)/shard_map/ppermute | solution.py:136
  6.0 5.4 %collective-permute-start.1 = (bf16[128,256]{1,0:T(8,128)(2,1)}, bf16[128,256]{1,0:T(8,128)(2,1)S(1)}, u32[]{:S(2)}, u32[]{:S(2)}) collective-permute-start(bf16[128,256]{1,0:T(8,128)(2,1)} %initial_ref.5), channel_id=1, source_target_pairs={{0,8},{1,9},{2,10},{3,11},{4,12},{5,13},{6,14},{7,15},{8,0},{9,1},... | collective-permute-start | bytes 196616 | tf_op jit(solution)/shard_map/ppermute | solution.py:136
  6.4 6.6 %collective-permute-start = (bf16[128,256]{1,0:T(8,128)(2,1)}, bf16[128,256]{1,0:T(8,128)(2,1)S(1)}, u32[]{:S(2)}, u32[]{:S(2)}) collective-permute-start(bf16[128,256]{1,0:T(8,128)(2,1)} %initial_ref.5), channel_id=1, source_target_pairs={{0,4},{1,5},{2,6},{3,7},{4,0},{5,1},{6,2},{7,3},{8,12},{9,13},{10,... | collective-permute-start | bytes 196616 | tf_op jit(solution)/shard_map/ppermute | solution.py:136
  8.3 3.6 %copy-start = (bf16[1,1,144,128,128]{4,3,2,1,0:T(8,128)(2,1)S(1)}, bf16[1,1,144,128,128]{4,3,2,1,0:T(8,128)(2,1)}, u32[]{:S(2)}) copy-start(bf16[1,1,144,128,128]{4,3,2,1,0:T(8,128)(2,1)} %tiles_ref.1) | copy-start | bytes 14155780
  8.4 7.0 %copy-start.1 = (bf16[128,256]{1,0:T(8,128)(2,1)S(1)}, bf16[128,256]{1,0:T(8,128)(2,1)}, u32[]{:S(2)}) copy-start(bf16[128,256]{1,0:T(8,128)(2,1)} %initial_ref.5) | copy-start | bytes 196612
  8.4 10.2 %copy-start.3 = (s32[128]{0:T(128)S(1)}, s32[128]{0:T(128)}, u32[]{:S(2)}) copy-start(s32[128]{0:T(128)} %param.8) | copy-start | bytes 1540
  8.4 12.9 %copy-start.2 = (bf16[256,256]{1,0:T(8,128)(2,1)S(1)}, bf16[256,256]{1,0:T(8,128)(2,1)}, u32[]{:S(2)}) copy-start(bf16[256,256]{1,0:T(8,128)(2,1)} %coupling_ref.5) | copy-start | bytes 393220
  8.4 5.2 %collective-permute-start.7 = (bf16[128,256]{1,0:T(8,128)(2,1)S(1)}, bf16[128,256]{1,0:T(8,128)(2,1)S(1)}, u32[]{:S(2)}, u32[]{:S(2)}) collective-permute-start(bf16[128,256]{1,0:T(8,128)(2,1)S(1)} %collective-permute-done.3), channel_id=1, source_target_pairs={{0,13},{1,12},{2,15},{3,14},{4,9},{5,8},{6,11},{7,10},{8,5},{9,4},... | collective-permute-start | bytes 196616 | tf_op jit(solution)/shard_map/ppermute | solution.py:136
  10.5 4.2 %collective-permute-start.6 = (bf16[128,256]{1,0:T(8,128)(2,1)S(1)}, bf16[128,256]{1,0:T(8,128)(2,1)S(1)}, u32[]{:S(2)}, u32[]{:S(2)}) collective-permute-start(bf16[128,256]{1,0:T(8,128)(2,1)S(1)} %collective-permute-done.3), channel_id=1, source_target_pairs={{0,9},{1,8},{2,11},{3,10},{4,13},{5,12},{6,15},{7,14},{8,1},{9,0},... | collective-permute-start | bytes 196616 | tf_op jit(solution)/shard_map/ppermute | solution.py:136
  11.2 4.2 %collective-permute-start.5 = (bf16[128,256]{1,0:T(8,128)(2,1)S(1)}, bf16[128,256]{1,0:T(8,128)(2,1)S(1)}, u32[]{:S(2)}, u32[]{:S(2)}) collective-permute-start(bf16[128,256]{1,0:T(8,128)(2,1)S(1)} %collective-permute-done.3), channel_id=1, source_target_pairs={{0,5},{1,4},{2,7},{3,6},{4,1},{5,0},{6,3},{7,2},{8,13},{9,12},{10,... | collective-permute-start | bytes 196616 | tf_op jit(solution)/shard_map/ppermute | solution.py:136
  11.4 4.0 %collective-permute-start.4 = (bf16[128,256]{1,0:T(8,128)(2,1)S(1)}, bf16[128,256]{1,0:T(8,128)(2,1)S(1)}, u32[]{:S(2)}, u32[]{:S(2)}) collective-permute-start(bf16[128,256]{1,0:T(8,128)(2,1)S(1)} %collective-permute-done.3), channel_id=1, source_target_pairs={{0,1},{1,0},{2,3},{3,2},{4,5},{5,4},{6,7},{7,6},{8,9},{9,8},{10,11... | collective-permute-start | bytes 196616 | tf_op jit(solution)/shard_map/ppermute | solution.py:136
  15.6 1.3 %collective-permute-start.9 = (bf16[128,256]{1,0:T(8,128)(2,1)S(1)}, bf16[128,256]{1,0:T(8,128)(2,1)S(1)}, u32[]{:S(2)}, u32[]{:S(2)}) collective-permute-start(bf16[128,256]{1,0:T(8,128)(2,1)S(1)} %late_first.3), channel_id=1, source_target_pairs={{0,1},{1,0},{2,3},{3,2},{4,5},{5,4},{6,7},{7,6},{8,9},{9,8},{10,11... | collective-permute-start | bytes 196616 | tf_op jit(solution)/shard_map/ppermute | solution.py:136
  16.2 2.5 %collective-permute-start.8 = (bf16[128,256]{1,0:T(8,128)(2,1)S(1)}, bf16[128,256]{1,0:T(8,128)(2,1)S(1)}, u32[]{:S(2)}, u32[]{:S(2)}) collective-permute-start(bf16[128,256]{1,0:T(8,128)(2,1)S(1)} %get-tuple-element.15), channel_id=1, source_target_pairs={{0,1},{1,0},{2,3},{3,2},{4,5},{5,4},{6,7},{7,6},{8,9},{9,8},{10,11... | collective-permute-start | bytes 196616 | tf_op jit(solution)/shard_map/ppermute | solution.py:136
  17.0 4.3 %collective-permute-start.10 = (bf16[128,256]{1,0:T(8,128)(2,1)S(1)}, bf16[128,256]{1,0:T(8,128)(2,1)S(1)}, u32[]{:S(2)}, u32[]{:S(2)}) collective-permute-start(bf16[128,256]{1,0:T(8,128)(2,1)S(1)} %add_convert_fusion.2), channel_id=1, source_target_pairs={{0,2},{1,3},{2,0},{3,1},{4,6},{5,7},{6,4},{7,5},{8,10},{9,11},{10,... | collective-permute-start | bytes 196616 | tf_op jit(solution)/shard_map/ppermute | solution.py:136
  21.5 4.7 %collective-permute-start.14 = (bf16[128,256]{1,0:T(8,128)(2,1)S(1)}, bf16[128,256]{1,0:T(8,128)(2,1)S(1)}, u32[]{:S(2)}, u32[]{:S(2)}) collective-permute-start(bf16[128,256]{1,0:T(8,128)(2,1)S(1)} %update.2.refs_0_), channel_id=1, source_target_pairs={{0,17},{1,16},{2,19},{3,18},{4,21},{5,20},{6,23},{7,22},{8,25},{9,... | collective-permute-start | bytes 196616 | tf_op jit(solution)/shard_map/ppermute | solution.py:136
  22.4 6.4 %collective-permute-start.13 = (bf16[128,256]{1,0:T(8,128)(2,1)S(1)}, bf16[128,256]{1,0:T(8,128)(2,1)S(1)}, u32[]{:S(2)}, u32[]{:S(2)}) collective-permute-start(bf16[128,256]{1,0:T(8,128)(2,1)S(1)} %update.2.refs_0_), channel_id=1, source_target_pairs={{0,12},{1,13},{2,14},{3,15},{4,8},{5,9},{6,10},{7,11},{8,4},{9,5},... | collective-permute-start | bytes 196616 | tf_op jit(solution)/shard_map/ppermute | solution.py:136
  24.9 4.8 %collective-permute-start.12 = (bf16[128,256]{1,0:T(8,128)(2,1)S(1)}, bf16[128,256]{1,0:T(8,128)(2,1)S(1)}, u32[]{:S(2)}, u32[]{:S(2)}) collective-permute-start(bf16[128,256]{1,0:T(8,128)(2,1)S(1)} %update.2.refs_0_), channel_id=1, source_target_pairs={{0,8},{1,9},{2,10},{3,11},{4,12},{5,13},{6,14},{7,15},{8,0},{9,1},... | collective-permute-start | bytes 196616 | tf_op jit(solution)/shard_map/ppermute | solution.py:136
  24.9 4.8 %collective-permute-start.11 = (bf16[128,256]{1,0:T(8,128)(2,1)S(1)}, bf16[128,256]{1,0:T(8,128)(2,1)S(1)}, u32[]{:S(2)}, u32[]{:S(2)}) collective-permute-start(bf16[128,256]{1,0:T(8,128)(2,1)S(1)} %update.2.refs_0_), channel_id=1, source_target_pairs={{0,4},{1,5},{2,6},{3,7},{4,0},{5,1},{6,2},{7,3},{8,12},{9,13},{10,... | collective-permute-start | bytes 196616 | tf_op jit(solution)/shard_map/ppermute | solution.py:136
  26.2 5.1 %collective-permute-start.18 = (bf16[128,256]{1,0:T(8,128)(2,1)S(1)}, bf16[128,256]{1,0:T(8,128)(2,1)S(1)}, u32[]{:S(2)}, u32[]{:S(2)}) collective-permute-start(bf16[128,256]{1,0:T(8,128)(2,1)S(1)} %collective-permute-done.14), channel_id=1, source_target_pairs={{0,13},{1,12},{2,15},{3,14},{4,9},{5,8},{6,11},{7,10},{8,5},{9,4},... | collective-permute-start | bytes 196616 | tf_op jit(solution)/shard_map/ppermute | solution.py:136
  28.8 3.8 %collective-permute-start.17 = (bf16[128,256]{1,0:T(8,128)(2,1)S(1)}, bf16[128,256]{1,0:T(8,128)(2,1)S(1)}, u32[]{:S(2)}, u32[]{:S(2)}) collective-permute-start(bf16[128,256]{1,0:T(8,128)(2,1)S(1)} %collective-permute-done.14), channel_id=1, source_target_pairs={{0,9},{1,8},{2,11},{3,10},{4,13},{5,12},{6,15},{7,14},{8,1},{9,0},... | collective-permute-start | bytes 196616 | tf_op jit(solution)/shard_map/ppermute | solution.py:136
  28.8 3.8 %collective-permute-start.16 = (bf16[128,256]{1,0:T(8,128)(2,1)S(1)}, bf16[128,256]{1,0:T(8,128)(2,1)S(1)}, u32[]{:S(2)}, u32[]{:S(2)}) collective-permute-start(bf16[128,256]{1,0:T(8,128)(2,1)S(1)} %collective-permute-done.14), channel_id=1, source_target_pairs={{0,5},{1,4},{2,7},{3,6},{4,1},{5,0},{6,3},{7,2},{8,13},{9,12},{10,... | collective-permute-start | bytes 196616 | tf_op jit(solution)/shard_map/ppermute | solution.py:136
  29.7 2.9 %collective-permute-start.15 = (bf16[128,256]{1,0:T(8,128)(2,1)S(1)}, bf16[128,256]{1,0:T(8,128)(2,1)S(1)}, u32[]{:S(2)}, u32[]{:S(2)}) collective-permute-start(bf16[128,256]{1,0:T(8,128)(2,1)S(1)} %collective-permute-done.14), channel_id=1, source_target_pairs={{0,1},{1,0},{2,3},{3,2},{4,5},{5,4},{6,7},{7,6},{8,9},{9,8},{10,11... | collective-permute-start | bytes 196616 | tf_op jit(solution)/shard_map/ppermute | solution.py:136
  32.8 1.3 %collective-permute-start.20 = (bf16[128,256]{1,0:T(8,128)(2,1)S(1)}, bf16[128,256]{1,0:T(8,128)(2,1)S(1)}, u32[]{:S(2)}, u32[]{:S(2)}) collective-permute-start(bf16[128,256]{1,0:T(8,128)(2,1)S(1)} %late_first.4), channel_id=1, source_target_pairs={{0,1},{1,0},{2,3},{3,2},{4,5},{5,4},{6,7},{7,6},{8,9},{9,8},{10,11... | collective-permute-start | bytes 196616 | tf_op jit(solution)/shard_map/ppermute | solution.py:136
  33.5 2.2 %collective-permute-start.19 = (bf16[128,256]{1,0:T(8,128)(2,1)S(1)}, bf16[128,256]{1,0:T(8,128)(2,1)S(1)}, u32[]{:S(2)}, u32[]{:S(2)}) collective-permute-start(bf16[128,256]{1,0:T(8,128)(2,1)S(1)} %get-tuple-element.18), channel_id=1, source_target_pairs={{0,1},{1,0},{2,3},{3,2},{4,5},{5,4},{6,7},{7,6},{8,9},{9,8},{10,11... | collective-permute-start | bytes 196616 | tf_op jit(solution)/shard_map/ppermute | solution.py:136
  34.2 4.4 %collective-permute-start.21 = (bf16[128,256]{1,0:T(8,128)(2,1)S(1)}, bf16[128,256]{1,0:T(8,128)(2,1)S(1)}, u32[]{:S(2)}, u32[]{:S(2)}) collective-permute-start(bf16[128,256]{1,0:T(8,128)(2,1)S(1)} %add_convert_fusion.1), channel_id=1, source_target_pairs={{0,2},{1,3},{2,0},{3,1},{4,6},{5,7},{6,4},{7,5},{8,10},{9,11},{10,... | collective-permute-start | bytes 196616 | tf_op jit(solution)/shard_map/ppermute | solution.py:136
  38.8 5.3 %collective-permute-start.25 = (bf16[128,256]{1,0:T(8,128)(2,1)S(1)}, bf16[128,256]{1,0:T(8,128)(2,1)S(1)}, u32[]{:S(2)}, u32[]{:S(2)}) collective-permute-start(bf16[128,256]{1,0:T(8,128)(2,1)S(1)} %update.3.refs_0_), channel_id=1, source_target_pairs={{0,17},{1,16},{2,19},{3,18},{4,21},{5,20},{6,23},{7,22},{8,25},{9,... | collective-permute-start | bytes 196616 | tf_op jit(solution)/shard_map/ppermute | solution.py:136
  40.0 6.8 %collective-permute-start.24 = (bf16[128,256]{1,0:T(8,128)(2,1)S(1)}, bf16[128,256]{1,0:T(8,128)(2,1)S(1)}, u32[]{:S(2)}, u32[]{:S(2)}) collective-permute-start(bf16[128,256]{1,0:T(8,128)(2,1)S(1)} %update.3.refs_0_), channel_id=1, source_target_pairs={{0,12},{1,13},{2,14},{3,15},{4,8},{5,9},{6,10},{7,11},{8,4},{9,5},... | collective-permute-start | bytes 196616 | tf_op jit(solution)/shard_map/ppermute | solution.py:136
  42.8 5.1 %collective-permute-start.23 = (bf16[128,256]{1,0:T(8,128)(2,1)S(1)}, bf16[128,256]{1,0:T(8,128)(2,1)S(1)}, u32[]{:S(2)}, u32[]{:S(2)}) collective-permute-start(bf16[128,256]{1,0:T(8,128)(2,1)S(1)} %update.3.refs_0_), channel_id=1, source_target_pairs={{0,8},{1,9},{2,10},{3,11},{4,12},{5,13},{6,14},{7,15},{8,0},{9,1},... | collective-permute-start | bytes 196616 | tf_op jit(solution)/shard_map/ppermute | solution.py:136
  42.9 5.1 %collective-permute-start.22 = (bf16[128,256]{1,0:T(8,128)(2,1)S(1)}, bf16[128,256]{1,0:T(8,128)(2,1)S(1)}, u32[]{:S(2)}, u32[]{:S(2)}) collective-permute-start(bf16[128,256]{1,0:T(8,128)(2,1)S(1)} %update.3.refs_0_), channel_id=1, source_target_pairs={{0,4},{1,5},{2,6},{3,7},{4,0},{5,1},{6,2},{7,3},{8,12},{9,13},{10,... | collective-permute-start | bytes 196616 | tf_op jit(solution)/shard_map/ppermute | solution.py:136
  44.1 5.2 %collective-permute-start.29 = (bf16[128,256]{1,0:T(8,128)(2,1)S(1)}, bf16[128,256]{1,0:T(8,128)(2,1)S(1)}, u32[]{:S(2)}, u32[]{:S(2)}) collective-permute-start(bf16[128,256]{1,0:T(8,128)(2,1)S(1)} %collective-permute-done.25), channel_id=1, source_target_pairs={{0,13},{1,12},{2,15},{3,14},{4,9},{5,8},{6,11},{7,10},{8,5},{9,4},... | collective-permute-start | bytes 196616 | tf_op jit(solution)/shard_map/ppermute | solution.py:136
  46.8 3.8 %collective-permute-start.28 = (bf16[128,256]{1,0:T(8,128)(2,1)S(1)}, bf16[128,256]{1,0:T(8,128)(2,1)S(1)}, u32[]{:S(2)}, u32[]{:S(2)}) collective-permute-start(bf16[128,256]{1,0:T(8,128)(2,1)S(1)} %collective-permute-done.25), channel_id=1, source_target_pairs={{0,9},{1,8},{2,11},{3,10},{4,13},{5,12},{6,15},{7,14},{8,1},{9,0},... | collective-permute-start | bytes 196616 | tf_op jit(solution)/shard_map/ppermute | solution.py:136
  46.9 3.9 %collective-permute-start.27 = (bf16[128,256]{1,0:T(8,128)(2,1)S(1)}, bf16[128,256]{1,0:T(8,128)(2,1)S(1)}, u32[]{:S(2)}, u32[]{:S(2)}) collective-permute-start(bf16[128,256]{1,0:T(8,128)(2,1)S(1)} %collective-permute-done.25), channel_id=1, source_target_pairs={{0,5},{1,4},{2,7},{3,6},{4,1},{5,0},{6,3},{7,2},{8,13},{9,12},{10,... | collective-permute-start | bytes 196616 | tf_op jit(solution)/shard_map/ppermute | solution.py:136
  47.9 2.9 %collective-permute-start.26 = (bf16[128,256]{1,0:T(8,128)(2,1)S(1)}, bf16[128,256]{1,0:T(8,128)(2,1)S(1)}, u32[]{:S(2)}, u32[]{:S(2)}) collective-permute-start(bf16[128,256]{1,0:T(8,128)(2,1)S(1)} %collective-permute-done.25), channel_id=1, source_target_pairs={{0,1},{1,0},{2,3},{3,2},{4,5},{5,4},{6,7},{7,6},{8,9},{9,8},{10,11... | collective-permute-start | bytes 196616 | tf_op jit(solution)/shard_map/ppermute | solution.py:136
  51.0 1.3 %collective-permute-start.31 = (bf16[128,256]{1,0:T(8,128)(2,1)S(1)}, bf16[128,256]{1,0:T(8,128)(2,1)S(1)}, u32[]{:S(2)}, u32[]{:S(2)}) collective-permute-start(bf16[128,256]{1,0:T(8,128)(2,1)S(1)} %late_first.5), channel_id=1, source_target_pairs={{0,1},{1,0},{2,3},{3,2},{4,5},{5,4},{6,7},{7,6},{8,9},{9,8},{10,11... | collective-permute-start | bytes 196616 | tf_op jit(solution)/shard_map/ppermute | solution.py:136
  51.7 2.3 %collective-permute-start.30 = (bf16[128,256]{1,0:T(8,128)(2,1)S(1)}, bf16[128,256]{1,0:T(8,128)(2,1)S(1)}, u32[]{:S(2)}, u32[]{:S(2)}) collective-permute-start(bf16[128,256]{1,0:T(8,128)(2,1)S(1)} %get-tuple-element.21), channel_id=1, source_target_pairs={{0,1},{1,0},{2,3},{3,2},{4,5},{5,4},{6,7},{7,6},{8,9},{9,8},{10,11... | collective-permute-start | bytes 196616 | tf_op jit(solution)/shard_map/ppermute | solution.py:136
  52.3 4.4 %collective-permute-start.32 = (bf16[128,256]{1,0:T(8,128)(2,1)S(1)}, bf16[128,256]{1,0:T(8,128)(2,1)S(1)}, u32[]{:S(2)}, u32[]{:S(2)}) collective-permute-start(bf16[128,256]{1,0:T(8,128)(2,1)S(1)} %add_convert_fusion), channel_id=1, source_target_pairs={{0,2},{1,3},{2,0},{3,1},{4,6},{5,7},{6,4},{7,5},{8,10},{9,11},{10,... | collective-permute-start | bytes 196616 | tf_op jit(solution)/shard_map/ppermute | solution.py:136
